TPU v7x, 512 devices: a whole 4x4x16 slice. The times are simulated.
512 devices in a mesh: dp: 16 (over z), seq: 32 (over x, y, core).
Axes of the slice: x: 4, y: 4, z: 16, core: 2. Of those that a mesh axis runs over, the one named last changes fastest.
Arguments:
- queries: bfloat16 [16, 32, 256, 1152], P('dp', 'seq'), may hold values from -9 to 9
- key_vectors: bfloat16 [16, 32, 256, 1152], P('dp', 'seq'), may hold values from -9 to 9
- value_vectors: bfloat16 [16, 32, 256, 1152], P('dp', 'seq'), may hold values from -6 to 6
- out_grad: bfloat16 [16, 32, 256, 1152], P('dp', 'seq'), may hold values from -6 to 6
- out_weight: bfloat16 [1152, 1152], P(None, 'seq'), may hold values from -0.1875 to 0.1875
- clip_frames: int32 [16, 4], P('dp'), may hold values from 1 to 16, 32 in all within a row
Outputs:
- attn_out: bfloat16 [16, 32, 256, 1152], P('dp', 'seq')
- query_grad: bfloat16 [16, 32, 256, 1152], P('dp', 'seq')
- key_grad: bfloat16 [16, 32, 256, 1152], P('dp', 'seq')
- value_grad: bfloat16 [16, 32, 256, 1152], P('dp', 'seq')
- weight_grad: float32 [1152, 1152], P(None, 'seq')
Inputs may be any that keep to these rules, and one draw needn't show every extreme that they name: `clip_frames`: row g lists the frame counts of the 4 clips of group g in frame order; they sum to 32, and the largest of each row is 16.
All inputs are finite; a program needn't handle non-finite values.
Results may differ from a plain program's by a relative error of at most 0.023.
Values may be sent and summed in bfloat16 or wider, within the bound.
No kernel may reach another device: no remote copies, remote signals or barrier semaphores. Data moves between devices by JAX's collectives and lax.ppermute only.
A program may use at most 64 MiB of HBM per device.

v0:
```python
import functools
import math

import jax
import jax.numpy as jnp
from jax import lax
from jax.experimental import pallas as pl
from jax.experimental.pallas import tpu as pltpu
from jax.sharding import PartitionSpec as P

HEADS = 16
HEAD_DIM = 72
LANES = 128
F32 = jnp.float32
BF16 = jnp.bfloat16
VMEM_LIMIT = 48 * 1024 * 1024
NT = (((1,), (1,)), ((), ()))
TN = (((0,), (0,)), ((), ()))


def dot(a, b):
    return jnp.dot(a, b, preferred_element_type=F32)


def dot_nt(a, b):
    return lax.dot_general(a, b, NT, preferred_element_type=F32)


def dot_tn(a, b):
    return lax.dot_general(a, b, TN, preferred_element_type=F32)


def window(head):
    first = head * HEAD_DIM // LANES
    last = (head * HEAD_DIM + HEAD_DIM - 1) // LANES
    return first * LANES, (last + 1 - first) * LANES


def head_lanes(head, rows):
    start, size = window(head)
    lane = lax.broadcasted_iota(jnp.int32, (rows, size), 1) + (start - head * HEAD_DIM)
    return (lane >= 0) & (lane < HEAD_DIM)


def clip_bias(lens_ref, rows, positions):
    def ids(axis):
        index = lax.broadcasted_iota(jnp.int32, (rows, rows), axis)
        frame = lax.div(index, jnp.int32(positions))
        clip = jnp.zeros_like(frame)
        end = jnp.int32(0)
        for j in range(lens_ref.shape[1]):
            end = end + lens_ref[0, j]
            clip = clip + jnp.where(frame >= end, 1, 0)
        return clip * positions + (index - frame * positions)

    return jnp.where(ids(0) == ids(1), 0.0, -jnp.inf).astype(F32)


def softmax(query_win, key_win, bias):
    scores = dot_nt(query_win, key_win) * (1.0 / math.sqrt(HEAD_DIM)) + bias
    raised = jnp.exp(scores - jnp.max(scores, axis=-1, keepdims=True))
    return raised * (1.0 / jnp.sum(raised, axis=-1, keepdims=True))


class Tiles:
    def __init__(self, ref, base=0):
        self.ref, self.base, self.held = ref, base, {}

    def add(self, head, value):
        start, size = window(head)
        for off in range(0, size, LANES):
            piece = value[:, off : off + LANES]
            tile = start + off
            self.held[tile] = piece if tile not in self.held else self.held[tile] + piece
        done = (head + 1) * HEAD_DIM
        for tile in [t for t in self.held if t + LANES <= done]:
            lanes = pl.ds(self.base + tile, LANES)
            self.ref[:, lanes] = self.held.pop(tile).astype(self.ref.dtype)


def forward_kernel(shard, pitch, positions, core_ref, lens_ref, x_ref, mixed_ref, keep_ref, send_ref):
    rows = x_ref.shape[0]
    width = x_ref.shape[1] // 4
    bias = clip_bias(lens_ref, rows, positions)
    mixed_tiles = Tiles(mixed_ref)
    for head in range(HEADS):
        start, size = window(head)
        lanes = head_lanes(head, rows)
        query_win = jnp.where(lanes, x_ref[:, pl.ds(start, size)], 0)
        key_win = x_ref[:, pl.ds(width + start, size)]
        value_win = jnp.where(lanes, x_ref[:, pl.ds(2 * width + start, size)], 0)
        attention = softmax(query_win, key_win, bias).astype(BF16)
        mixed_tiles.add(head, dot(attention, value_win))
    half = keep_ref.shape[0]
    feature = lax.broadcasted_iota(jnp.int32, (1, width), 1)
    owner = lax.div(feature, jnp.int32(shard))
    other = jnp.bitwise_and(owner + core_ref[0], 1)
    place = other * half + lax.div(owner, jnp.int32(2)) * pitch + (feature - owner * shard)
    mixed = mixed_ref[...]
    grad = x_ref[:, pl.ds(3 * width, width)]
    block = half // 4
    for step in range(8):
        at = lax.broadcasted_iota(jnp.int32, (block, width), 0) + step * block
        pick = jnp.where(at == place, 1.0, 0.0).astype(BF16)
        grad_rows = dot_nt(pick, grad).astype(BF16)
        part = dot(grad_rows, mixed).astype(BF16)
        out_ref = keep_ref if step < 4 else send_ref
        out_ref[pl.ds((step % 4) * block, block), :] = part


def backward_kernel(shard, pitch, positions, lens_ref, x_ref, mixed_ref, weight_ref, y_ref, back_ref):
    rows = x_ref.shape[0]
    width = x_ref.shape[1] // 4
    padded = weight_ref.shape[0]
    feature = lax.broadcasted_iota(jnp.int32, (1, width), 1)
    owner = lax.div(feature, jnp.int32(shard))
    place = owner * pitch + (feature - owner * shard)
    pick = jnp.where(lax.broadcasted_iota(jnp.int32, (padded, width), 0) == place, 1.0, 0.0).astype(BF16)
    grad_padded = dot_nt(x_ref[:, pl.ds(3 * width, width)], pick).astype(BF16)
    back_ref[...] = dot(grad_padded, weight_ref[...]).astype(BF16)
    out_padded = dot_nt(mixed_ref[...], weight_ref[...]).astype(BF16)
    y_ref[:, pl.ds(0, width)] = dot(out_padded, pick).astype(BF16)
    bias = clip_bias(lens_ref, rows, positions)
    query_tiles = Tiles(y_ref, width)
    key_tiles = Tiles(y_ref, 2 * width)
    value_tiles = Tiles(y_ref, 3 * width)
    for head in range(HEADS):
        start, size = window(head)
        lanes = head_lanes(head, rows)
        query_win = jnp.where(lanes, x_ref[:, pl.ds(start, size)], 0)
        key_win = jnp.where(lanes, x_ref[:, pl.ds(width + start, size)], 0)
        value_win = x_ref[:, pl.ds(2 * width + start, size)]
        back_win = jnp.where(lanes, back_ref[:, pl.ds(start, size)], 0)
        attention = softmax(query_win, key_win, bias)
        value_tiles.add(head, dot_tn(attention.astype(BF16), back_win))
        prob_grad = dot_nt(back_win, value_win)
        inner = jnp.sum(attention * prob_grad, axis=-1, keepdims=True)
        score_grad = (attention * (prob_grad - inner) * (1.0 / math.sqrt(HEAD_DIM))).astype(BF16)
        query_tiles.add(head, dot(score_grad, key_win))
        key_tiles.add(head, dot_tn(score_grad, query_win))


def spec(space=pltpu.VMEM):
    return pl.BlockSpec(memory_space=space)


def forward(core, lengths, x, shard, pitch, n_seq, positions):
    rows, wide = x.shape
    width = wide // 4
    half = n_seq * pitch // 2
    return pl.pallas_call(
        functools.partial(forward_kernel, shard, pitch, positions),
        out_shape=(
            jax.ShapeDtypeStruct((rows, width), BF16),
            jax.ShapeDtypeStruct((half, width), BF16),
            jax.ShapeDtypeStruct((half, width), BF16),
        ),
        in_specs=[spec(pltpu.SMEM), spec(pltpu.SMEM), spec()],
        out_specs=(spec(), spec(), spec()),
        compiler_params=pltpu.CompilerParams(vmem_limit_bytes=VMEM_LIMIT),
        cost_estimate=pl.CostEstimate(
            flops=4 * half * rows * width + 4 * HEADS * rows * rows * 256,
            bytes_accessed=16 * rows * width + 8 * half * width,
            transcendentals=HEADS * rows * rows,
        ),
        name="forward",
    )(core, lengths, x)


def backward(lengths, x, mixed, weight, shard, pitch, positions):
    rows, wide = x.shape
    width = wide // 4
    return pl.pallas_call(
        functools.partial(backward_kernel, shard, pitch, positions),
        out_shape=jax.ShapeDtypeStruct((rows, wide), BF16),
        in_specs=[spec(pltpu.SMEM), spec(), spec(), spec()],
        out_specs=spec(),
        scratch_shapes=[pltpu.VMEM((rows, width), BF16)],
        compiler_params=pltpu.CompilerParams(vmem_limit_bytes=VMEM_LIMIT),
        cost_estimate=pl.CostEstimate(
            flops=8 * rows * width * weight.shape[0] + 10 * HEADS * rows * rows * 256,
            bytes_accessed=20 * rows * width + 2 * weight.shape[0] * width,
            transcendentals=HEADS * rows * rows,
        ),
        name="backward",
    )(lengths, x, mixed, weight)


def on_device(n_seq, n_dp, queries, key_vectors, value_vectors, out_grad, out_weight, clip_frames):
    patches, width = queries.shape[2:]
    positions = patches // n_seq
    shard = out_weight.shape[1]
    pitch = -(-shard // 8) * 8
    core = jnp.bitwise_and(lax.axis_index("seq"), 1).astype(jnp.int32)

    def swap(block):
        return lax.all_to_all(block.reshape(n_seq, positions, -1), "seq", 0, 0, tiled=True)

    weight_rows = jnp.pad(out_weight.T, ((0, pitch - shard), (0, 0)))
    weight = lax.all_gather(weight_rows, "seq", axis=0, tiled=True)

    flat = [a.reshape(patches, width) for a in (queries, key_vectors, value_vectors, out_grad)]
    x = swap(jnp.concatenate(flat, axis=1)).reshape(patches, 4 * width)
    mixed, keep, send = forward(core.reshape(1), clip_frames, x, shard, pitch, n_seq, positions)

    partner = lax.ppermute(send, "seq", [(i, i ^ 1) for i in range(n_seq)])
    chip = (keep.astype(F32) + partner.astype(F32)).astype(BF16)
    planes = [[i for i in range(n_seq) if i % 2 == c] for c in (0, 1)]
    parts = lax.all_to_all(
        chip.reshape(n_seq // 2, pitch, width), "seq", 0, 0, tiled=True, axis_index_groups=planes
    )

    y = backward(clip_frames, x, mixed, weight, shard, pitch, positions)
    parts, y = lax.optimization_barrier((parts, y))
    back = swap(y).reshape(patches, 4 * width)

    total = jnp.sum(parts.astype(F32), axis=0)
    hop = 1
    while hop < n_dp:
        mine = total.astype(BF16)
        theirs = lax.ppermute(mine, "dp", [(i, i ^ hop) for i in range(n_dp)])
        total = mine.astype(F32) + theirs.astype(F32)
        hop *= 2
    weight_grad = total[:shard].T
    outs = [back[:, i * width : (i + 1) * width].reshape(queries.shape) for i in range(4)]
    return (*outs, weight_grad)


def solution(mesh):
    whole = P("dp", "seq", None, None)
    return jax.shard_map(
        functools.partial(on_device, mesh.shape["seq"], mesh.shape["dp"]),
        mesh=mesh,
        in_specs=(whole, whole, whole, whole, P(None, "seq"), P("dp", None)),
        out_specs=(whole, whole, whole, whole, P(None, "seq")),
        check_vma=False,
    )
```

profile of v0, /device:TPU:6, one launch (start us, length us, event | category | flops | bytes accessed | tf_op | source)
XLA Modules:
  0.0 180.4 jit_solution(12167987557535496156)
XLA Ops:
  7.2 0.0 all-gather.2.cloned.1.call-start
  7.2 1.5 pad.4
  8.8 0.0 all-gather.2.cloned.1.call-update
  8.8 3.2 %pad_maximum_fusion = bf16[32,8,4608]{2,1,0:T(8,128)(2,1)} fusion(bf16[32,8,1152]{2,1,0:T(8,128)(2,1)} %bitcast.24, bf16[32,8,1152]{2,1,0:T(8,128)(2,1)} %bitcast.25, bf16[32,8,1152]{2,1,0:T(8,128)(2,1)} %bitcast.26, bf16[32,8,1152]{2,1,0:T(8,128)(2,1)} %bitcast.27), kind=kLoop, calls=%fused_computation.1 | loop fusion | flops 9437184 | bytes 4718592 | tf_op jit(solution)/shard_map/concatenate | solution.py:203
  12.0 0.0 copy-start
  12.0 9.8 %all-to-all-start = ((bf16[32,8,4608]{2,1,0:T(8,128)(2,1)}), bf16[32,8,4608]{2,1,0:T(8,128)(2,1)S(1)}, u32[]{:S(2)}, u32[]{:S(2)}) async-start(bf16[32,8,4608]{2,1,0:T(8,128)(2,1)} %pad_maximum_fusion), calls=%async_computation | async-start | bytes 4718592 | tf_op jit(solution)/shard_map/all_to_all | solution.py:197
  21.9 29.3 %all-to-all-done = bf16[32,8,4608]{2,1,0:T(8,128)(2,1)S(1)} async-done(((bf16[32,8,4608]{2,1,0:T(8,128)(2,1)}), bf16[32,8,4608]{2,1,0:T(8,128)(2,1)S(1)}, u32[]{:S(2)}, u32[]{:S(2)}) %all-to-all-start) | async-done | bytes 2359328 | tf_op jit(solution)/shard_map/all_to_all | solution.py:197
  51.1 0.0 copy-done
  51.1 7.8 %forward.1 = (bf16[256,1152]{1,0:T(8,128)(2,1)S(1)}, bf16[640,1152]{1,0:T(8,128)(2,1)S(1)}, bf16[640,1152]{1,0:T(8,128)(2,1)S(1)}) custom-call(s32[1]{0:T(128)} %bitcast.core_ref, s32[1,4]{1,0:T(1,128)S(1)} %copy-done, bf16[256,4608]{1,0:T(8,128)(2,1)S(1)} %bitcast.20), custom_call_target="tpu_custom_call" | custom-call | flops 1828716544 | bytes 10616832 | tf_op jit(solution)/shard_map/forward/pallas_call | solution.py:151
  59.0 2.6 %collective-permute-start = (bf16[640,1152]{1,0:T(8,128)(2,1)S(1)}, bf16[640,1152]{1,0:T(8,128)(2,1)S(1)}, u32[]{:S(2)}, u32[]{:S(2)}) collective-permute-start(bf16[640,1152]{1,0:T(8,128)(2,1)S(1)} %get-tuple-element.11), channel_id=1, source_target_pairs={{0,1},{1,0},{2,3},{3,2},{4,5},{5,4},{6,7},{7,6},{8,9},{9,8},{10,11... | collective-permute-start | bytes 4423688 | tf_op jit(solution)/shard_map/ppermute | solution.py:206
  61.6 2.9 %collective-permute-done = bf16[640,1152]{1,0:T(8,128)(2,1)S(1)} collective-permute-done((bf16[640,1152]{1,0:T(8,128)(2,1)S(1)}, bf16[640,1152]{1,0:T(8,128)(2,1)S(1)}, u32[]{:S(2)}, u32[]{:S(2)}) %collective-permute-start) | collective-permute-done | bytes 1474592 | tf_op jit(solution)/shard_map/ppermute | solution.py:206
  64.5 1.5 add_convert_fusion
  66.0 7.7 %all-to-all-start.1 = ((bf16[16,40,1152]{2,1,0:T(8,128)(2,1)}), bf16[16,40,1152]{2,1,0:T(8,128)(2,1)}, u32[]{:S(2)}, u32[]{:S(2)}) async-start(bf16[16,40,1152]{2,1,0:T(8,128)(2,1)} %bitcast.23), calls=%async_computation.1 | async-start | bytes 2949120 | tf_op jit(solution)/shard_map/all_to_all | solution.py:209
  73.7 23.8 %all-gather.2.cloned.1.call-done.weight_ref = bf16[1280,1152]{1,0:T(8,128)(2,1)} async-done(((bf16[40,1152]{1,0:T(8,128)(2,1)}), bf16[1280,1152]{1,0:T(8,128)(2,1)}) %all-gather.2.cloned.1.call-update) | async-done | bytes 2949136 | tf_op jit(solution)/shard_map/all_gather | solution.py:200
  97.5 15.5 %backward.1 = bf16[256,4608]{1,0:T(8,128)(2,1)} custom-call(s32[1,4]{1,0:T(1,128)S(1)} %copy-done, bf16[256,4608]{1,0:T(8,128)(2,1)S(1)} %bitcast.21, bf16[256,1152]{1,0:T(8,128)(2,1)S(1)} %get-tuple-element.12.mixed_ref, bf16[1280,1152]{1,0:T(8,128)(2,1)} %all-gather.2.cloned.1.call-done.weight_ref), custom_call_target="tpu_custom_call" | custom-call | flops 5704253440 | bytes 8847360 | tf_op jit(solution)/shard_map/backward/pallas_call | solution.py:173
  113.0 0.0 all-to-all-done.1
  113.0 7.5 %all-to-all-start.2 = ((bf16[32,8,4608]{2,1,0:T(8,128)(2,1)}), bf16[32,8,4608]{2,1,0:T(8,128)(2,1)S(1)}, u32[]{:S(2)}, u32[]{:S(2)}) async-start(bf16[32,8,4608]{2,1,0:T(8,128)(2,1)} %bitcast.8), calls=%async_computation.2 | async-start | bytes 4718592 | tf_op jit(solution)/shard_map/all_to_all | solution.py:197
  120.5 1.6 reduce_sum.12
  122.1 4.2 %collective-permute-start.1 = (bf16[40,1152]{1,0:T(8,128)(2,1)S(1)}, bf16[40,1152]{1,0:T(8,128)(2,1)S(1)}, u32[]{:S(2)}, u32[]{:S(2)}) collective-permute-start(bf16[40,1152]{1,0:T(8,128)(2,1)S(1)} %reduce_sum.12), channel_id=1, source_target_pairs={{0,32},{32,0},{64,96},{96,64},{128,160},{160,128},{192,224},{224,1... | collective-permute-start | bytes 276488 | tf_op jit(solution)/shard_map/ppermute | solution.py:221
  126.2 3.0 %collective-permute-done.1 = bf16[40,1152]{1,0:T(8,128)(2,1)S(1)} collective-permute-done((bf16[40,1152]{1,0:T(8,128)(2,1)S(1)}, bf16[40,1152]{1,0:T(8,128)(2,1)S(1)}, u32[]{:S(2)}, u32[]{:S(2)}) %collective-permute-start.1) | collective-permute-done | bytes 92192 | tf_op jit(solution)/shard_map/ppermute | solution.py:221
  129.2 5.0 %collective-permute-start.2 = (bf16[40,1152]{1,0:T(8,128)(2,1)S(1)}, bf16[40,1152]{1,0:T(8,128)(2,1)S(1)}, u32[]{:S(2)}, u32[]{:S(2)}) collective-permute-start(bf16[40,1152]{1,0:T(8,128)(2,1)S(1)} %add_convert_fusion.3), channel_id=1, source_target_pairs={{0,64},{32,96},{64,0},{96,32},{128,192},{160,224},{192,128},{224,1... | collective-permute-start | bytes 276488 | tf_op jit(solution)/shard_map/ppermute | solution.py:221
  134.2 4.1 %collective-permute-done.2 = bf16[40,1152]{1,0:T(8,128)(2,1)S(1)} collective-permute-done((bf16[40,1152]{1,0:T(8,128)(2,1)S(1)}, bf16[40,1152]{1,0:T(8,128)(2,1)S(1)}, u32[]{:S(2)}, u32[]{:S(2)}) %collective-permute-start.2) | collective-permute-done | bytes 92192 | tf_op jit(solution)/shard_map/ppermute | solution.py:221
  138.4 7.1 %collective-permute-start.3 = (bf16[40,1152]{1,0:T(8,128)(2,1)S(1)}, bf16[40,1152]{1,0:T(8,128)(2,1)S(1)}, u32[]{:S(2)}, u32[]{:S(2)}) collective-permute-start(bf16[40,1152]{1,0:T(8,128)(2,1)S(1)} %add_convert_fusion.2), channel_id=1, source_target_pairs={{0,128},{32,160},{64,192},{96,224},{128,0},{160,32},{192,64},{224,... | collective-permute-start | bytes 276488 | tf_op jit(solution)/shard_map/ppermute | solution.py:221
  145.5 7.5 %collective-permute-done.3 = bf16[40,1152]{1,0:T(8,128)(2,1)S(1)} collective-permute-done((bf16[40,1152]{1,0:T(8,128)(2,1)S(1)}, bf16[40,1152]{1,0:T(8,128)(2,1)S(1)}, u32[]{:S(2)}, u32[]{:S(2)}) %collective-permute-start.3) | collective-permute-done | bytes 92192 | tf_op jit(solution)/shard_map/ppermute | solution.py:221
  153.0 11.6 %collective-permute-start.4 = (bf16[40,1152]{1,0:T(8,128)(2,1)S(1)}, bf16[40,1152]{1,0:T(8,128)(2,1)S(1)}, u32[]{:S(2)}, u32[]{:S(2)}) collective-permute-start(bf16[40,1152]{1,0:T(8,128)(2,1)S(1)} %add_convert_fusion.1), channel_id=1, source_target_pairs={{0,256},{32,288},{64,320},{96,352},{128,384},{160,416},{192,448},{... | collective-permute-start | bytes 276488 | tf_op jit(solution)/shard_map/ppermute | solution.py:221
  164.6 6.9 %collective-permute-done.4 = bf16[40,1152]{1,0:T(8,128)(2,1)S(1)} collective-permute-done((bf16[40,1152]{1,0:T(8,128)(2,1)S(1)}, bf16[40,1152]{1,0:T(8,128)(2,1)S(1)}, u32[]{:S(2)}, u32[]{:S(2)}) %collective-permute-start.4) | collective-permute-done | bytes 92192 | tf_op jit(solution)/shard_map/ppermute | solution.py:221
  171.5 0.7 add_bitcast_fusion
  172.2 0.0 all-to-all-done.2
  172.2 1.4 slice_bitcast_fusion
  (3 shorter events, 0.1 us)
Async XLA Ops:
  7.2 90.3 %all-gather.2.cloned.1.call-start = ((), (), s32[]{:S(2)}) async-start(), calls=%async_computation.3 | async-start | bytes 3041280 | tf_op jit(solution)/shard_map/all_gather | solution.py:200
  12.0 39.1 %copy-start = (s32[1,4]{1,0:T(1,128)S(1)}, s32[1,4]{1,0:T(1,128)}, u32[]{:S(2)}) copy-start(s32[1,4]{1,0:T(1,128)} %lens_ref.3) | copy-start | bytes 52
  12.0 39.1 %all-to-all-start = ((bf16[32,8,4608]{2,1,0:T(8,128)(2,1)}), bf16[32,8,4608]{2,1,0:T(8,128)(2,1)S(1)}, u32[]{:S(2)}, u32[]{:S(2)}) async-start(bf16[32,8,4608]{2,1,0:T(8,128)(2,1)} %pad_maximum_fusion), calls=%async_computation | async-start | bytes 4718592 | tf_op jit(solution)/shard_map/all_to_all | solution.py:197
  59.0 5.5 %collective-permute-start = (bf16[640,1152]{1,0:T(8,128)(2,1)S(1)}, bf16[640,1152]{1,0:T(8,128)(2,1)S(1)}, u32[]{:S(2)}, u32[]{:S(2)}) collective-permute-start(bf16[640,1152]{1,0:T(8,128)(2,1)S(1)} %get-tuple-element.11), channel_id=1, source_target_pairs={{0,1},{1,0},{2,3},{3,2},{4,5},{5,4},{6,7},{7,6},{8,9},{9,8},{10,11... | collective-permute-start | bytes 4423688 | tf_op jit(solution)/shard_map/ppermute | solution.py:206
  66.0 47.0 %all-to-all-start.1 = ((bf16[16,40,1152]{2,1,0:T(8,128)(2,1)}), bf16[16,40,1152]{2,1,0:T(8,128)(2,1)}, u32[]{:S(2)}, u32[]{:S(2)}) async-start(bf16[16,40,1152]{2,1,0:T(8,128)(2,1)} %bitcast.23), calls=%async_computation.1 | async-start | bytes 2949120 | tf_op jit(solution)/shard_map/all_to_all | solution.py:209
  113.0 59.2 %all-to-all-start.2 = ((bf16[32,8,4608]{2,1,0:T(8,128)(2,1)}), bf16[32,8,4608]{2,1,0:T(8,128)(2,1)S(1)}, u32[]{:S(2)}, u32[]{:S(2)}) async-start(bf16[32,8,4608]{2,1,0:T(8,128)(2,1)} %bitcast.8), calls=%async_computation.2 | async-start | bytes 4718592 | tf_op jit(solution)/shard_map/all_to_all | solution.py:197
  122.1 7.1 %collective-permute-start.1 = (bf16[40,1152]{1,0:T(8,128)(2,1)S(1)}, bf16[40,1152]{1,0:T(8,128)(2,1)S(1)}, u32[]{:S(2)}, u32[]{:S(2)}) collective-permute-start(bf16[40,1152]{1,0:T(8,128)(2,1)S(1)} %reduce_sum.12), channel_id=1, source_target_pairs={{0,32},{32,0},{64,96},{96,64},{128,160},{160,128},{192,224},{224,1... | collective-permute-start | bytes 276488 | tf_op jit(solution)/shard_map/ppermute | solution.py:221
  129.2 9.1 %collective-permute-start.2 = (bf16[40,1152]{1,0:T(8,128)(2,1)S(1)}, bf16[40,1152]{1,0:T(8,128)(2,1)S(1)}, u32[]{:S(2)}, u32[]{:S(2)}) collective-permute-start(bf16[40,1152]{1,0:T(8,128)(2,1)S(1)} %add_convert_fusion.3), channel_id=1, source_target_pairs={{0,64},{32,96},{64,0},{96,32},{128,192},{160,224},{192,128},{224,1... | collective-permute-start | bytes 276488 | tf_op jit(solution)/shard_map/ppermute | solution.py:221
  138.4 14.6 %collective-permute-start.3 = (bf16[40,1152]{1,0:T(8,128)(2,1)S(1)}, bf16[40,1152]{1,0:T(8,128)(2,1)S(1)}, u32[]{:S(2)}, u32[]{:S(2)}) collective-permute-start(bf16[40,1152]{1,0:T(8,128)(2,1)S(1)} %add_convert_fusion.2), channel_id=1, source_target_pairs={{0,128},{32,160},{64,192},{96,224},{128,0},{160,32},{192,64},{224,... | collective-permute-start | bytes 276488 | tf_op jit(solution)/shard_map/ppermute | solution.py:221
  153.0 18.5 %collective-permute-start.4 = (bf16[40,1152]{1,0:T(8,128)(2,1)S(1)}, bf16[40,1152]{1,0:T(8,128)(2,1)S(1)}, u32[]{:S(2)}, u32[]{:S(2)}) collective-permute-start(bf16[40,1152]{1,0:T(8,128)(2,1)S(1)} %add_convert_fusion.1), channel_id=1, source_target_pairs={{0,256},{32,288},{64,320},{96,352},{128,384},{160,416},{192,448},{... | collective-permute-start | bytes 276488 | tf_op jit(solution)/shard_map/ppermute | solution.py:221
Sparse Core Ops, SparseCore 0:
  11.8 85.6 all-gather.1
where the time goes:
time: 181 us; the launch traced here: 180 us
  waiting for transfers between devices  77.4 us (43%)
  starting transfers between devices  55.6 us (31%)
  Pallas kernels  23.3 us (13%)
  between operations  14.1 us (8%)
  other arithmetic  7.07 us (4%)
  local copies, waits for them, and re-layouts  2.99 us (2%)
    all_to_all x2, waiting for transfers between devices, swap(): lax.all_to_all(block.reshape(n_seq, positions, -1), 'seq', 0, 0, tiled=True)  29.3 us
    ppermute x4, starting transfers between devices, on_device(): theirs = lax.ppermute(mine, 'dp', [(i, i ^ hop) for i in range(n_dp)])  27.9 us
    all_gather x1, waiting for transfers between devices, on_device(): weight = lax.all_gather(weight_rows, 'seq', axis=0, tiled=True)  23.8 us
    ppermute x4, waiting for transfers between devices, on_device(): theirs = lax.ppermute(mine, 'dp', [(i, i ^ hop) for i in range(n_dp)])  21.4 us
    all_to_all x2, starting transfers between devices, swap(): lax.all_to_all(block.reshape(n_seq, positions, -1), 'seq', 0, 0, tiled=True)  17.4 us
    pallas_call x1, Pallas kernels, backward(): pl.pallas_call(functools.partial(backward_kernel, shard, pitch, positions...  15.5 us
    pallas_call x1, Pallas kernels, forward(): pl.pallas_call(functools.partial(forward_kernel, shard, pitch, positions)...  7.84 us
    all_to_all x1, starting transfers between devices, on_device(): lax.all_to_all(chip.reshape(n_seq // 2, pitch, width), 'seq', 0, 0, tiled...  7.68 us
  transfers between devices with their start and end apart: 9, of which 7 were waited for; matrix products, arithmetic and copies ran while one was open for 4% of the time, Pallas kernels for 13%

commit v1 on v0

v1 whole, which is shorter than its diff:
```python
import functools
import math

import jax
import jax.numpy as jnp
from jax import lax
from jax.experimental import pallas as pl
from jax.experimental.pallas import tpu as pltpu
from jax.sharding import PartitionSpec as P

HEADS = 16
HEAD_DIM = 72
LANES = 128
SCALE = 1.0 / math.sqrt(HEAD_DIM)
F32 = jnp.float32
BF16 = jnp.bfloat16
VMEM_LIMIT = 28 * 1024 * 1024
NT = (((1,), (1,)), ((), ()))
TN = (((0,), (0,)), ((), ()))


def dot(a, b):
    return jnp.dot(a, b, preferred_element_type=F32)


def dot_nt(a, b):
    return lax.dot_general(a, b, NT, preferred_element_type=F32)


def dot_tn(a, b):
    return lax.dot_general(a, b, TN, preferred_element_type=F32)


def window(head):
    first = head * HEAD_DIM // LANES
    last = (head * HEAD_DIM + HEAD_DIM - 1) // LANES
    return first * LANES, (last + 1 - first) * LANES


def head_lanes(head, rows):
    start, size = window(head)
    lane = lax.broadcasted_iota(jnp.int32, (rows, size), 1) + (start - head * HEAD_DIM)
    return (lane >= 0) & (lane < HEAD_DIM)


def clip_bias(lens_ref, rows, positions):
    def ids(axis):
        index = lax.broadcasted_iota(jnp.int32, (rows, rows), axis)
        frame = lax.div(index, jnp.int32(positions))
        clip = jnp.zeros_like(frame)
        end = jnp.int32(0)
        for j in range(lens_ref.shape[1]):
            end = end + lens_ref[0, j]
            clip = clip + jnp.where(frame >= end, 1, 0)
        return clip * positions + (index - frame * positions)

    return jnp.where(ids(0) == ids(1), 0.0, -jnp.inf).astype(F32)


def softmax(query_win, key_win, bias):
    scores = dot_nt(query_win, key_win) * SCALE + bias
    raised = jnp.exp(scores - jnp.max(scores, axis=-1, keepdims=True))
    return raised, 1.0 / jnp.sum(raised, axis=-1, keepdims=True)


class Tiles:
    def __init__(self, ref, base=0):
        self.ref, self.base, self.held = ref, base, {}

    def add(self, head, value):
        start, size = window(head)
        for off in range(0, size, LANES):
            piece = value[:, off : off + LANES]
            tile = start + off
            self.held[tile] = piece if tile not in self.held else self.held[tile] + piece
        done = (head + 1) * HEAD_DIM
        for tile in [t for t in self.held if t + LANES <= done]:
            lanes = pl.ds(self.base + tile, LANES)
            self.ref[:, lanes] = self.held.pop(tile).astype(self.ref.dtype)


GROUP = 8
FULL = 16
ODD = 2
CHUNK = 3
ODD_LANES = 384


def selection(rows, columns, wanted):
    row = lax.broadcasted_iota(jnp.int32, (rows, columns), 0)
    column = lax.broadcasted_iota(jnp.int32, (rows, columns), 1)
    return jnp.where(column == wanted(row), 1.0, 0.0).astype(BF16)


def chunk_tiles(ref, q):
    pieces = [ref[:, pl.ds((CHUNK * u + q) * LANES, LANES)] for u in range(CHUNK)]
    return jnp.concatenate(pieces, axis=1)


def pack_kernel(*refs):
    *parts, weight_ref, x_ref, held_ref, sems = refs
    shard, width = weight_ref.shape
    rows = held_ref.shape[0]
    copies = [
        pltpu.make_async_copy(part, x_ref.at[:, pl.ds(i * width, width)], sems.at[i])
        for i, part in enumerate(parts)
    ]
    for copy in copies:
        copy.start()
    weight = weight_ref[...]

    def core(row):
        return jnp.bitwise_and(lax.div(row, jnp.int32(GROUP)), 1)

    def place(row):
        return jnp.bitwise_and(row, GROUP - 1)

    for block in range(FULL // GROUP):
        pick = selection(rows, shard, lambda row: FULL * core(row) + GROUP * block + place(row))
        held_ref[:, pl.ds(block * width, width)] = dot(pick, weight).astype(BF16)
    odd = jnp.zeros((rows, ODD_LANES), F32)
    for q in range(CHUNK):

        def wanted(row):
            k = lax.div(place(row) - q, jnp.int32(CHUNK))
            exact = (place(row) == CHUNK * k + q) & (k < ODD)
            return jnp.where(exact, 2 * FULL + ODD * core(row) + k, -1)

        odd = odd + dot(selection(rows, shard, wanted), chunk_tiles(weight_ref, q))
    held_ref[:, pl.ds(FULL // GROUP * width, ODD_LANES)] = odd.astype(BF16)
    lanes = pl.ds(len(parts) * width, held_ref.shape[1])
    copies.append(pltpu.make_async_copy(held_ref, x_ref.at[:, lanes], sems.at[len(parts)]))
    copies[-1].start()
    for copy in copies:
        copy.wait()


def pick_rows(ref, place):
    padded, width = ref.shape
    block = padded // 8
    for step in range(8):
        at = lax.broadcasted_iota(jnp.int32, (block, width), 0) + step * block
        ref[pl.ds(step * block, block), :] = jnp.where(at == place, 1.0, 0.0).astype(BF16)


def tables_kernel(shard, pitch, positions, core_ref, lens_ref, pick_ref, turned_ref, bias_ref, held_ref, sems):
    padded, width = turned_ref.shape
    feature = lax.broadcasted_iota(jnp.int32, (1, width), 1)
    owner = lax.div(feature, jnp.int32(shard))
    rest = feature - owner * shard
    other = jnp.bitwise_and(owner + core_ref[0], 1)
    turned = other * (padded // 2) + lax.div(owner, jnp.int32(2)) * pitch + rest
    holder = jnp.where(rest < 2 * FULL, lax.div(rest, jnp.int32(FULL)), lax.div(rest - 2 * FULL, jnp.int32(ODD)))
    other = jnp.bitwise_and(holder + core_ref[0], 1)
    within = rest - FULL * holder
    block = lax.div(within, jnp.int32(GROUP))
    size = width // shard * GROUP
    full = (other * (FULL // GROUP) + block) * size + owner * GROUP + within - block * GROUP
    odd = 2 * (FULL // GROUP) * size + (other * (width // shard) + owner) * ODD + rest - 2 * FULL - ODD * holder
    picked = jnp.where(rest < 2 * FULL, full, odd)
    copies = []
    for i, (ref, place) in enumerate(((turned_ref, turned), (pick_ref, picked))):
        rows = pl.ds(0, ref.shape[0])
        pick_rows(held_ref.at[i, rows], place)
        copies.append(pltpu.make_async_copy(held_ref.at[i, rows], ref, sems.at[i]))
        copies[-1].start()
    bias_ref[...] = clip_bias(lens_ref, bias_ref.shape[0], positions)
    for copy in copies:
        copy.wait()


def forward_kernel(turned_ref, x_ref, bias_ref, mixed_ref, keep_ref, send_ref, pick_ref, held_ref, sems):
    fetch = pltpu.make_async_copy(turned_ref, pick_ref, sems.at[4])
    fetch.start()
    rows, width = mixed_ref.shape
    bias = bias_ref[...]
    mixed_tiles = Tiles(mixed_ref)
    for head in range(HEADS):
        start, size = window(head)
        lanes = head_lanes(head, rows)
        query_win = jnp.where(lanes, x_ref[:, pl.ds(start, size)], 0)
        key_win = x_ref[:, pl.ds(width + start, size)]
        value_win = jnp.where(lanes, x_ref[:, pl.ds(2 * width + start, size)], 0)
        raised, recip = softmax(query_win, key_win, bias)
        mixed_tiles.add(head, dot((raised * recip).astype(BF16), value_win))
    mixed = mixed_ref[...]
    grad = x_ref[:, pl.ds(3 * width, width)]
    half = keep_ref.shape[0]
    block = half // 4
    copies = []
    fetch.wait()
    for step in (4, 5, 6, 7, 0, 1, 2, 3):
        grad_rows = dot_nt(pick_ref[pl.ds(step * block, block), :], grad).astype(BF16)
        part = dot(grad_rows, mixed).astype(BF16)
        at = pl.ds((step % 4) * block, block)
        if step < 4:
            keep_ref[at, :] = part
        else:
            held_ref[at, :] = part
            copies.append(pltpu.make_async_copy(held_ref.at[at, :], send_ref.at[at, :], sems.at[step % 4]))
            copies[-1].start()
    for copy in copies:
        copy.wait()


def join_kernel(keep_ref, theirs_ref, out_ref):
    size = out_ref.shape[2]
    total = (keep_ref[...].astype(F32) + theirs_ref[...].astype(F32)).astype(BF16)
    out_ref[0] = total[:, :size]
    out_ref[1] = total[:, total.shape[1] - size :]


def backward_kernel(
    pick_hbm, x_ref, other_ref, bias_ref, mixed_ref, y_ref, pick_ref, odd_ref, back_ref, out_ref, held_ref, sems
):
    rows, width = mixed_ref.shape
    fetch = pltpu.make_async_copy(pick_hbm, pick_ref, sems.at[7])
    fetch.start()
    copies = []

    def send(start, size):
        lanes = pl.ds(start, size)
        copies.append(pltpu.make_async_copy(held_ref.at[:, lanes], y_ref.at[:, lanes], sems.at[len(copies)]))
        copies[-1].start()

    blocks = FULL // GROUP
    weight = []
    for ref, base in ((x_ref, 4 * width), (other_ref, 0)):
        weight += [ref[:, pl.ds(base + b * width, width)] for b in range(blocks)]
    odd_rows = odd_ref.shape[0] // 2
    for i, (ref, base) in enumerate(((x_ref, 4 * width), (other_ref, 0))):
        left = ref[:, pl.ds(base + blocks * width, ODD_LANES)]
        for q in range(CHUNK):

            def wanted(row):
                source = lax.div(row, jnp.int32(ODD))
                return source * GROUP + CHUNK * (row - ODD * source) + q

            got = dot(selection(odd_rows, rows, wanted), left).astype(BF16)
            for u in range(CHUNK):
                lanes = pl.ds((CHUNK * u + q) * LANES, LANES)
                odd_ref[pl.ds(i * odd_rows, odd_rows), lanes] = got[:, u * LANES : (u + 1) * LANES]
    weight.append(odd_ref[...])
    fetch.wait()
    grad = dot_nt(x_ref[:, pl.ds(3 * width, width)], pick_ref[...]).astype(BF16)
    mixed = mixed_ref[...]
    back = jnp.zeros((rows, width), F32)
    at = 0
    for block in weight:
        size = block.shape[0]
        back = back + dot(grad[:, at : at + size], block)
        out_ref[:, pl.ds(at, size)] = dot_nt(mixed, block).astype(BF16)
        at += size
    back_ref[...] = back.astype(BF16)
    held_ref[:, pl.ds(0, width)] = dot(out_ref[...], pick_ref[...]).astype(BF16)
    send(0, width)
    query_tiles, key_tiles, value_tiles = [Tiles(held_ref, i * width) for i in (1, 2, 3)]
    bias = bias_ref[...]
    sent = 0
    for head in range(HEADS):
        start, size = window(head)
        lanes = head_lanes(head, rows)
        query_win = jnp.where(lanes, x_ref[:, pl.ds(start, size)], 0)
        key_win = jnp.where(lanes, x_ref[:, pl.ds(width + start, size)], 0)
        value_win = x_ref[:, pl.ds(2 * width + start, size)]
        back_win = jnp.where(lanes, back_ref[:, pl.ds(start, size)], 0)
        raised, recip = softmax(query_win, key_win, bias)
        attention = raised * recip
        value_tiles.add(head, dot_tn(attention.astype(BF16), back_win))
        drawn = attention * dot_nt(back_win, value_win)
        inner = jnp.sum(drawn, axis=-1, keepdims=True)
        score_grad = ((drawn - attention * inner) * SCALE).astype(BF16)
        query_tiles.add(head, dot(score_grad, key_win))
        key_tiles.add(head, dot_tn(score_grad, query_win))
        if head in (HEADS // 2 - 1, HEADS - 1):
            done = (head + 1) * HEAD_DIM // LANES * LANES
            for i in (1, 2, 3):
                send(i * width + sent, done - sent)
            sent = done
    for copy in copies:
        copy.wait()


def call(kernel, name, outs, args, smem=0, hbm_in=0, hbm_out=(), scratch=(), flops=0):
    space = [pltpu.SMEM] * smem + [pltpu.HBM] * hbm_in + [pltpu.VMEM] * (len(args) - smem - hbm_in)
    args = [pltpu.with_memory_space_constraint(a, s) if s == pltpu.HBM else a for a, s in zip(args, space)]
    shapes = [jax.ShapeDtypeStruct(shape, dtype) for shape, dtype in outs]
    moved = sum(a.size * a.dtype.itemsize for a in args) + sum(math.prod(s.shape) * s.dtype.itemsize for s in shapes)
    return pl.pallas_call(
        kernel,
        out_shape=[pltpu.HBM(s.shape, s.dtype) if i in hbm_out else s for i, s in enumerate(shapes)],
        in_specs=[pl.BlockSpec(memory_space=s) for s in space],
        out_specs=[pl.BlockSpec(memory_space=pltpu.HBM if i in hbm_out else pltpu.VMEM) for i in range(len(outs))],
        scratch_shapes=scratch,
        compiler_params=pltpu.CompilerParams(vmem_limit_bytes=VMEM_LIMIT),
        cost_estimate=pl.CostEstimate(flops=flops, bytes_accessed=moved, transcendentals=0),
        name=name,
    )(*args)


def dma(count):
    return pltpu.SemaphoreType.DMA((count,))


def pack(arrays, weight_t):
    rows, width = arrays[0].shape
    extra = FULL // GROUP * width + ODD_LANES
    outs = [((rows, len(arrays) * width + extra), BF16)]
    scratch = [pltpu.VMEM((rows, extra), BF16), dma(len(arrays) + 1)]
    return call(pack_kernel, "pack", outs, (*arrays, weight_t), hbm_in=len(arrays), hbm_out=(0,), scratch=scratch)[0]


def tables(core, lengths, rows, width, shard, pitch, positions):
    kernel = functools.partial(tables_kernel, shard, pitch, positions)
    padded = width // shard * pitch
    outs = [((width, width), BF16), ((padded, width), BF16), ((rows, rows), F32)]
    scratch = [pltpu.VMEM((2, padded, width), BF16), dma(2)]
    return call(kernel, "tables", outs, (core, lengths), smem=2, hbm_out=(0, 1), scratch=scratch)


def forward(x, turned, bias):
    rows = x.shape[0]
    padded, width = turned.shape
    half = (padded // 2, width)
    outs = [((rows, width), BF16), (half, BF16), (half, BF16)]
    flops = 4 * padded * rows * width + 4 * HEADS * rows * rows * 256
    scratch = [pltpu.VMEM(turned.shape, BF16), pltpu.VMEM(half, BF16), dma(5)]
    return call(forward_kernel, "forward", outs, (turned, x, bias), hbm_in=1, hbm_out=(2,), scratch=scratch, flops=flops)


def join(keep, theirs):
    rows, width = keep.shape
    return call(join_kernel, "join", [((2, rows, lane_half(width)), BF16)], (keep, theirs))[0]


def backward(pick, x, other, bias, mixed):
    rows, width = mixed.shape
    flops = 8 * width * rows * width + 12 * HEADS * rows * rows * 256
    one = pltpu.VMEM((rows, width), BF16)
    odd = pltpu.VMEM((width - 4 * rows, width), BF16)
    scratch = [pltpu.VMEM((width, width), BF16), odd, one, one, pltpu.VMEM((rows, 4 * width), BF16), dma(8)]
    args = (pick, x, other, bias, mixed)
    outs = [((rows, 4 * width), BF16)]
    return call(backward_kernel, "backward", outs, args, hbm_in=1, hbm_out=(0,), scratch=scratch, flops=flops)[0]


def lane_half(width):
    return (width // LANES + 1) // 2 * LANES


def sum_over_pairs(block, n_dp, width):
    def exchange(block, hop):
        return lax.ppermute(block, "dp", [(i, i ^ hop) for i in range(n_dp)])

    hop = 2
    while hop < n_dp:
        block = (block.astype(F32) + exchange(block, hop).astype(F32)).astype(BF16)
        hop *= 2
    theirs = exchange(block, 1)
    low = jnp.bitwise_and(lax.axis_index("dp"), 1) == 0
    lower, upper = jnp.where(low, block, theirs), jnp.where(low, theirs, block)
    return jnp.concatenate([lower, upper[:, 2 * lower.shape[1] - width :]], axis=1).astype(F32)


def on_device(n_seq, n_dp, queries, key_vectors, value_vectors, out_grad, out_weight, clip_frames):
    patches, width = queries.shape[2:]
    positions = patches // n_seq
    shard = out_weight.shape[1]
    pitch = -(-shard // 8) * 8
    core = jnp.bitwise_and(lax.axis_index("seq"), 1).astype(jnp.int32)

    def swap(block):
        return lax.all_to_all(block.reshape(n_seq, positions, -1), "seq", 0, 0, tiled=True)

    def partner(block):
        return lax.ppermute(block, "seq", [(i, i ^ 1) for i in range(n_seq)])

    arrays = [a.reshape(patches, width) for a in (queries, key_vectors, value_vectors, out_grad)]
    x = swap(pack(arrays, out_weight.T)).reshape(patches, -1)
    pick, turned, bias = tables(core.reshape(1), clip_frames, patches, width, shard, pitch, positions)
    mixed, keep, send = forward(x, turned, bias)

    chip = join(keep, partner(send)).reshape(n_seq, pitch, -1)
    pairs = [
        [(p + d) * n_seq + i for d in (0, 1) for i in range(c, n_seq, 2)] for p in range(0, n_dp, 2) for c in (0, 1)
    ]
    parts = lax.all_to_all(chip, ("dp", "seq"), 0, 0, tiled=True, axis_index_groups=pairs)

    y = backward(pick, x, partner(x[:, 4 * width :]), bias, mixed)
    parts, y = lax.optimization_barrier((parts, y))
    back = swap(y).reshape(patches, 4 * width)
    total = jnp.sum(parts.astype(F32), axis=0).astype(BF16)
    weight_grad = sum_over_pairs(total, n_dp, width)[:shard].T
    outs = [back[:, i * width : (i + 1) * width].reshape(queries.shape) for i in range(4)]
    return (*outs, weight_grad)


def solution(mesh):
    whole = P("dp", "seq", None, None)
    return jax.shard_map(
        functools.partial(on_device, mesh.shape["seq"], mesh.shape["dp"]),
        mesh=mesh,
        in_specs=(whole, whole, whole, whole, P(None, "seq"), P("dp", None)),
        out_specs=(whole, whole, whole, whole, P(None, "seq")),
        check_vma=False,
    )
```

time: 181 us -> 234 us (1.29)
  Pallas kernels: 23.3 us -> 105 us
  waiting for transfers between devices: 77.4 us -> 62.4 us
  between operations: 14.1 us -> 0.82 us
  other arithmetic: 7.07 us -> 2.42 us
    pallas_call x2 -> x5, Pallas kernels: 23.3 us -> 105 us  [call(): pl.pallas_call(kernel, out_shape=[pltpu.HBM(s.shape, s.dtype) if i in hbm...]
    all_gather x1 -> x0, waiting for transfers between devices: 23.8 us -> none  [on_device(): weight = lax.all_gather(weight_rows, 'seq', axis=0, tiled=True)]
    all_to_all x2, waiting for transfers between devices: 29.3 us -> 41.7 us  [swap(): lax.all_to_all(block.reshape(n_seq, positions, -1), 'seq', 0, 0, tiled=True)]
    ppermute x5 -> x6, waiting for transfers between devices: 24.3 us -> 20.7 us  [the longest x4 14.3 us: exchange(): return lax.ppermute(block, 'dp', [(i, i ^ hop) for i in range(n_dp)])]
    concatenate x1 -> x0, other arithmetic: 3.21 us -> none  [on_device(): x = swap(jnp.concatenate(flat, axis=1)).reshape(patches, 4 * width)]
    ppermute x5 -> x6, starting transfers between devices: 30.5 us -> 31.6 us  [the longest x4 27.6 us: exchange(): return lax.ppermute(block, 'dp', [(i, i ^ hop) for i in range(n_dp)])]
  transfers between devices with their start and end apart: 9 -> 9, of which waited for: 7 -> 7; matrix products, arithmetic and copies ran while one was open for 4% -> 2% of each run, Pallas kernels for 13% -> 9%
where the time goes in v1:
time: 234 us; the launch traced here: 233 us
  Pallas kernels  105 us (45%)
  waiting for transfers between devices  62.4 us (27%)
  starting transfers between devices  57.7 us (25%)
  local copies, waits for them, and re-layouts  4.96 us (2%)
  other arithmetic  2.42 us (1%)
    pallas_call x5, Pallas kernels, call(): pl.pallas_call(kernel, out_shape=[pltpu.HBM(s.shape, s.dtype) if i in hbm...  105 us
    all_to_all x2, waiting for transfers between devices, swap(): lax.all_to_all(block.reshape(n_seq, positions, -1), 'seq', 0, 0, tiled=True)  41.7 us
    ppermute x4, starting transfers between devices, exchange(): return lax.ppermute(block, 'dp', [(i, i ^ hop) for i in range(n_dp)])  27.6 us
    all_to_all x2, starting transfers between devices, swap(): lax.all_to_all(block.reshape(n_seq, positions, -1), 'seq', 0, 0, tiled=True)  17.9 us
    ppermute x4, waiting for transfers between devices, exchange(): return lax.ppermute(block, 'dp', [(i, i ^ hop) for i in range(n_dp)])  14.3 us
    all_to_all x1, starting transfers between devices, on_device(): lax.all_to_all(chip, ('dp', 'seq'), 0, 0, tiled=True, axis_index_groups=p...  8.19 us
    ppermute x2, waiting for transfers between devices, partner(): return lax.ppermute(block, 'seq', [(i, i ^ 1) for i in range(n_seq)])  6.36 us
  transfers between devices with their start and end apart: 9, of which 7 were waited for; matrix products, arithmetic and copies ran while one was open for 2% of the time, Pallas kernels for 9%

profile of v1, /device:TPU:6, one launch (start us, length us, event | category | flops | bytes accessed | tf_op | source)
XLA Modules:
  0.0 233.1 jit_solution(10945603019549446523)
XLA Ops:
  0.6 0.0 copy-start
  0.6 0.9 copy-done
  1.5 72.6 %pack.1 = bf16[256,7296]{1,0:T(8,128)(2,1)} custom-call(bf16[256,1152]{1,0:T(8,128)(2,1)} %bitcast.25, bf16[256,1152]{1,0:T(8,128)(2,1)} %bitcast.26, bf16[256,1152]{1,0:T(8,128)(2,1)} %bitcast.27, bf16[256,1152]{1,0:T(8,128)(2,1)} %bitcast.28, bf16[36,1152]{1,0:T(8,128)(2,1)S(1)} %bitcast.21), custom_call_target="tpu_custom_call" | custom-call | bytes 6177792 | tf_op jit(solution)/shard_map/pack/pallas_call | solution.py:289
  74.1 0.0 copy-start.1
  74.2 10.4 %all-to-all-start = ((bf16[32,8,7296]{2,1,0:T(8,128)(2,1)}), bf16[32,8,7296]{2,1,0:T(8,128)(2,1)}, u32[]{:S(2)}, u32[]{:S(2)}) async-start(bf16[32,8,7296]{2,1,0:T(8,128)(2,1)} %bitcast.22), calls=%async_computation | async-start | bytes 7471104 | tf_op jit(solution)/shard_map/all_to_all | solution.py:373
  84.6 0.0 copy-done.1
  84.6 3.6 %tables.1 = (bf16[1152,1152]{1,0:T(8,128)(2,1)}, bf16[1280,1152]{1,0:T(8,128)(2,1)}, f32[256,256]{1,0:T(8,128)S(1)}) custom-call(s32[1]{0:T(128)} %bitcast.core_ref, s32[1,4]{1,0:T(1,128)S(1)} %copy-done.1), custom_call_target="tpu_custom_call" | custom-call | bytes 5865492 | tf_op jit(solution)/shard_map/tables/pallas_call | solution.py:289
  88.2 41.7 %all-to-all-done = bf16[32,8,7296]{2,1,0:T(8,128)(2,1)} async-done(((bf16[32,8,7296]{2,1,0:T(8,128)(2,1)}), bf16[32,8,7296]{2,1,0:T(8,128)(2,1)}, u32[]{:S(2)}, u32[]{:S(2)}) %all-to-all-start) | async-done | bytes 3735584 | tf_op jit(solution)/shard_map/all_to_all | solution.py:373
  129.9 10.0 %forward.1 = (bf16[256,1152]{1,0:T(8,128)(2,1)S(1)}, bf16[640,1152]{1,0:T(8,128)(2,1)S(1)}, bf16[640,1152]{1,0:T(8,128)(2,1)}) custom-call(bf16[1280,1152]{1,0:T(8,128)(2,1)} %get-tuple-element.13.turned_ref, bf16[256,7296]{1,0:T(8,128)(2,1)} %bitcast.7.x_ref, f32[256,256]{1,0:T(8,128)S(1)} %get-tuple-element.14.bias_ref), custom_call_target="tpu_custom_call" | custom-call | flops 2583691264 | bytes 10485760 | tf_op jit(solution)/shard_map/forward/pallas_call | solution.py:289
  139.9 1.9 collective-permute-start
  141.9 3.4 %collective-permute-done.theirs_ref = bf16[640,1152]{1,0:T(8,128)(2,1)S(1)} collective-permute-done((bf16[640,1152]{1,0:T(8,128)(2,1)}, bf16[640,1152]{1,0:T(8,128)(2,1)S(1)}, u32[]{:S(2)}, u32[]{:S(2)}) %collective-permute-start) | collective-permute-done | bytes 1474592 | tf_op jit(solution)/shard_map/ppermute | solution.py:376
  145.3 1.5 join.1
  146.8 8.2 %all-to-all-start.1 = ((bf16[32,40,640]{2,1,0:T(8,128)(2,1)}), bf16[32,40,640]{2,1,0:T(8,128)(2,1)S(1)}, u32[]{:S(2)}, u32[]{:S(2)}) async-start(bf16[32,40,640]{2,1,0:T(8,128)(2,1)} %bitcast.8), calls=%async_computation.1 | async-start | bytes 3276800 | tf_op jit(solution)/shard_map/all_to_all | solution.py:387
  155.0 1.4 slice.29
  156.5 2.1 collective-permute-start.1
  158.6 2.9 %collective-permute-done.1.other_ref = bf16[256,2688]{1,0:T(8,128)(2,1)S(1)} collective-permute-done((bf16[256,2688]{1,0:T(8,128)(2,1)S(1)}, bf16[256,2688]{1,0:T(8,128)(2,1)S(1)}, u32[]{:S(2)}, u32[]{:S(2)}) %collective-permute-start.1) | collective-permute-done | bytes 1376288 | tf_op jit(solution)/shard_map/ppermute | solution.py:376
  161.5 17.1 %backward.1 = bf16[256,4608]{1,0:T(8,128)(2,1)} custom-call(bf16[1152,1152]{1,0:T(8,128)(2,1)} %get-tuple-element.17.pick_hbm, bf16[256,7296]{1,0:T(8,128)(2,1)} %bitcast.7.x_ref, bf16[256,2688]{1,0:T(8,128)(2,1)S(1)} %collective-permute-done.1.other_ref, f32[256,256]{1,0:T(8,128)S(1)} %get-tuple-element.14.bias_ref, ...), custom_call_target="tpu_custom_call" | custom-call | flops 5939134464 | bytes 10977280 | tf_op jit(solution)/shard_map/backward/pallas_call | solution.py:289
  178.6 0.0 all-to-all-done.1
  178.6 1.2 copy-done.2
  179.8 7.4 %all-to-all-start.2 = ((bf16[32,8,4608]{2,1,0:T(8,128)(2,1)}), bf16[32,8,4608]{2,1,0:T(8,128)(2,1)S(1)}, u32[]{:S(2)}, u32[]{:S(2)}) async-start(bf16[32,8,4608]{2,1,0:T(8,128)(2,1)} %bitcast.24), calls=%async_computation.2 | async-start | bytes 4718592 | tf_op jit(solution)/shard_map/all_to_all | solution.py:373
  187.2 1.7 reduce_sum.12
  188.9 3.8 %collective-permute-start.2 = (bf16[40,640]{1,0:T(8,128)(2,1)S(1)}, bf16[40,640]{1,0:T(8,128)(2,1)S(1)}, u32[]{:S(2)}, u32[]{:S(2)}) collective-permute-start(bf16[40,640]{1,0:T(8,128)(2,1)S(1)} %reduce_sum.12), channel_id=1, source_target_pairs={{0,64},{32,96},{64,0},{96,32},{128,192},{160,224},{192,128},{224,1... | collective-permute-start | bytes 153608 | tf_op jit(solution)/shard_map/ppermute | solution.py:353
  192.7 4.2 %collective-permute-done.2 = bf16[40,640]{1,0:T(8,128)(2,1)S(1)} collective-permute-done((bf16[40,640]{1,0:T(8,128)(2,1)S(1)}, bf16[40,640]{1,0:T(8,128)(2,1)S(1)}, u32[]{:S(2)}, u32[]{:S(2)}) %collective-permute-start.2) | collective-permute-done | bytes 51232 | tf_op jit(solution)/shard_map/ppermute | solution.py:353
  196.9 8.1 %collective-permute-start.3 = (bf16[40,640]{1,0:T(8,128)(2,1)S(1)}, bf16[40,640]{1,0:T(8,128)(2,1)S(1)}, u32[]{:S(2)}, u32[]{:S(2)}) collective-permute-start(bf16[40,640]{1,0:T(8,128)(2,1)S(1)} %add_convert_fusion.2), channel_id=1, source_target_pairs={{0,128},{32,160},{64,192},{96,224},{128,0},{160,32},{192,64},{224,... | collective-permute-start | bytes 153608 | tf_op jit(solution)/shard_map/ppermute | solution.py:353
  205.0 3.6 %collective-permute-done.3 = bf16[40,640]{1,0:T(8,128)(2,1)S(1)} collective-permute-done((bf16[40,640]{1,0:T(8,128)(2,1)S(1)}, bf16[40,640]{1,0:T(8,128)(2,1)S(1)}, u32[]{:S(2)}, u32[]{:S(2)}) %collective-permute-start.3) | collective-permute-done | bytes 51232 | tf_op jit(solution)/shard_map/ppermute | solution.py:353
  208.6 13.7 %collective-permute-start.4 = (bf16[40,640]{1,0:T(8,128)(2,1)S(1)}, bf16[40,640]{1,0:T(8,128)(2,1)S(1)}, u32[]{:S(2)}, u32[]{:S(2)}) collective-permute-start(bf16[40,640]{1,0:T(8,128)(2,1)S(1)} %add_convert_fusion.1), channel_id=1, source_target_pairs={{0,256},{32,288},{64,320},{96,352},{128,384},{160,416},{192,448},{... | collective-permute-start | bytes 153608 | tf_op jit(solution)/shard_map/ppermute | solution.py:353
  222.3 2.6 %collective-permute-done.4 = bf16[40,640]{1,0:T(8,128)(2,1)S(1)} collective-permute-done((bf16[40,640]{1,0:T(8,128)(2,1)S(1)}, bf16[40,640]{1,0:T(8,128)(2,1)S(1)}, u32[]{:S(2)}, u32[]{:S(2)}) %collective-permute-start.4) | collective-permute-done | bytes 51232 | tf_op jit(solution)/shard_map/ppermute | solution.py:353
  224.9 2.0 collective-permute-start.5
  227.0 3.9 %collective-permute-done.5 = bf16[40,640]{1,0:T(8,128)(2,1)S(1)} collective-permute-done((bf16[40,640]{1,0:T(8,128)(2,1)S(1)}, bf16[40,640]{1,0:T(8,128)(2,1)S(1)}, u32[]{:S(2)}, u32[]{:S(2)}) %collective-permute-start.5) | collective-permute-done | bytes 51232 | tf_op jit(solution)/shard_map/ppermute | solution.py:353
  230.9 0.7 convert_bitcast_fusion
  231.6 0.0 all-to-all-done.2
  231.6 1.4 slice_bitcast_fusion
  (6 shorter events, 0.1 us)
Async XLA Ops:
  0.6 0.9 copy-start
  74.1 10.5 %copy-start.1 = (s32[1,4]{1,0:T(1,128)S(1)}, s32[1,4]{1,0:T(1,128)}, u32[]{:S(2)}) copy-start(s32[1,4]{1,0:T(1,128)} %lens_ref.1) | copy-start | bytes 52
  74.2 55.8 %all-to-all-start = ((bf16[32,8,7296]{2,1,0:T(8,128)(2,1)}), bf16[32,8,7296]{2,1,0:T(8,128)(2,1)}, u32[]{:S(2)}, u32[]{:S(2)}) async-start(bf16[32,8,7296]{2,1,0:T(8,128)(2,1)} %bitcast.22), calls=%async_computation | async-start | bytes 7471104 | tf_op jit(solution)/shard_map/all_to_all | solution.py:373
  139.9 5.4 %collective-permute-start = (bf16[640,1152]{1,0:T(8,128)(2,1)}, bf16[640,1152]{1,0:T(8,128)(2,1)S(1)}, u32[]{:S(2)}, u32[]{:S(2)}) collective-permute-start(bf16[640,1152]{1,0:T(8,128)(2,1)} %get-tuple-element.16), channel_id=1, source_target_pairs={{0,1},{1,0},{2,3},{3,2},{4,5},{5,4},{6,7},{7,6},{8,9},{9,8},{10,11... | collective-permute-start | bytes 4423688 | tf_op jit(solution)/shard_map/ppermute | solution.py:376
  146.8 31.8 %all-to-all-start.1 = ((bf16[32,40,640]{2,1,0:T(8,128)(2,1)}), bf16[32,40,640]{2,1,0:T(8,128)(2,1)S(1)}, u32[]{:S(2)}, u32[]{:S(2)}) async-start(bf16[32,40,640]{2,1,0:T(8,128)(2,1)} %bitcast.8), calls=%async_computation.1 | async-start | bytes 3276800 | tf_op jit(solution)/shard_map/all_to_all | solution.py:387
  156.5 5.0 %collective-permute-start.1 = (bf16[256,2688]{1,0:T(8,128)(2,1)S(1)}, bf16[256,2688]{1,0:T(8,128)(2,1)S(1)}, u32[]{:S(2)}, u32[]{:S(2)}) collective-permute-start(bf16[256,2688]{1,0:T(8,128)(2,1)S(1)} %slice.29), channel_id=1, source_target_pairs={{0,1},{1,0},{2,3},{3,2},{4,5},{5,4},{6,7},{7,6},{8,9},{9,8},{10,11... | collective-permute-start | bytes 4128776 | tf_op jit(solution)/shard_map/ppermute | solution.py:376
  178.6 1.2 copy-start.2
  179.8 51.9 %all-to-all-start.2 = ((bf16[32,8,4608]{2,1,0:T(8,128)(2,1)}), bf16[32,8,4608]{2,1,0:T(8,128)(2,1)S(1)}, u32[]{:S(2)}, u32[]{:S(2)}) async-start(bf16[32,8,4608]{2,1,0:T(8,128)(2,1)} %bitcast.24), calls=%async_computation.2 | async-start | bytes 4718592 | tf_op jit(solution)/shard_map/all_to_all | solution.py:373
  188.9 8.0 %collective-permute-start.2 = (bf16[40,640]{1,0:T(8,128)(2,1)S(1)}, bf16[40,640]{1,0:T(8,128)(2,1)S(1)}, u32[]{:S(2)}, u32[]{:S(2)}) collective-permute-start(bf16[40,640]{1,0:T(8,128)(2,1)S(1)} %reduce_sum.12), channel_id=1, source_target_pairs={{0,64},{32,96},{64,0},{96,32},{128,192},{160,224},{192,128},{224,1... | collective-permute-start | bytes 153608 | tf_op jit(solution)/shard_map/ppermute | solution.py:353
  196.9 11.6 %collective-permute-start.3 = (bf16[40,640]{1,0:T(8,128)(2,1)S(1)}, bf16[40,640]{1,0:T(8,128)(2,1)S(1)}, u32[]{:S(2)}, u32[]{:S(2)}) collective-permute-start(bf16[40,640]{1,0:T(8,128)(2,1)S(1)} %add_convert_fusion.2), channel_id=1, source_target_pairs={{0,128},{32,160},{64,192},{96,224},{128,0},{160,32},{192,64},{224,... | collective-permute-start | bytes 153608 | tf_op jit(solution)/shard_map/ppermute | solution.py:353
  208.6 16.3 %collective-permute-start.4 = (bf16[40,640]{1,0:T(8,128)(2,1)S(1)}, bf16[40,640]{1,0:T(8,128)(2,1)S(1)}, u32[]{:S(2)}, u32[]{:S(2)}) collective-permute-start(bf16[40,640]{1,0:T(8,128)(2,1)S(1)} %add_convert_fusion.1), channel_id=1, source_target_pairs={{0,256},{32,288},{64,320},{96,352},{128,384},{160,416},{192,448},{... | collective-permute-start | bytes 153608 | tf_op jit(solution)/shard_map/ppermute | solution.py:353
  224.9 6.0 %collective-permute-start.5 = (bf16[40,640]{1,0:T(8,128)(2,1)S(1)}, bf16[40,640]{1,0:T(8,128)(2,1)S(1)}, u32[]{:S(2)}, u32[]{:S(2)}) collective-permute-start(bf16[40,640]{1,0:T(8,128)(2,1)S(1)} %add_convert_fusion), channel_id=1, source_target_pairs={{0,32},{32,0},{64,96},{96,64},{128,160},{160,128},{192,224},{224,1... | collective-permute-start | bytes 153608 | tf_op jit(solution)/shard_map/ppermute | solution.py:353

commit v2 on v1

--- a/solution.py
+++ b/solution.py
@@ -98,15 +98,12 @@
 
 
 def pack_kernel(*refs):
-    *parts, weight_ref, x_ref, held_ref, sems = refs
+    *parts, weight_ref, x_ref, staged_ref, held_ref, sems = refs
     shard, width = weight_ref.shape
     rows = held_ref.shape[0]
-    copies = [
-        pltpu.make_async_copy(part, x_ref.at[:, pl.ds(i * width, width)], sems.at[i])
-        for i, part in enumerate(parts)
-    ]
-    for copy in copies:
-        copy.start()
+    fetches = [pltpu.make_async_copy(part, staged_ref.at[i], sems.at[i]) for i, part in enumerate(parts)]
+    for fetch in fetches:
+        fetch.start()
     weight = weight_ref[...]
 
     def core(row):
@@ -129,8 +126,13 @@
         odd = odd + dot(selection(rows, shard, wanted), chunk_tiles(weight_ref, q))
     held_ref[:, pl.ds(FULL // GROUP * width, ODD_LANES)] = odd.astype(BF16)
     lanes = pl.ds(len(parts) * width, held_ref.shape[1])
-    copies.append(pltpu.make_async_copy(held_ref, x_ref.at[:, lanes], sems.at[len(parts)]))
+    copies = [pltpu.make_async_copy(held_ref, x_ref.at[:, lanes], sems.at[2 * len(parts)])]
     copies[-1].start()
+    for i, fetch in enumerate(fetches):
+        fetch.wait()
+        lanes = pl.ds(i * width, width)
+        copies.append(pltpu.make_async_copy(staged_ref.at[i], x_ref.at[:, lanes], sems.at[len(parts) + i]))
+        copies[-1].start()
     for copy in copies:
         copy.wait()
 
@@ -264,14 +266,15 @@
         key_win = jnp.where(lanes, x_ref[:, pl.ds(width + start, size)], 0)
         value_win = x_ref[:, pl.ds(2 * width + start, size)]
         back_win = jnp.where(lanes, back_ref[:, pl.ds(start, size)], 0)
-        raised, recip = softmax(query_win, key_win, bias)
-        attention = raised * recip
-        value_tiles.add(head, dot_tn(attention.astype(BF16), back_win))
-        drawn = attention * dot_nt(back_win, value_win)
-        inner = jnp.sum(drawn, axis=-1, keepdims=True)
+        scores = dot_nt(key_win, query_win) * SCALE + bias
+        raised = jnp.exp(scores - jnp.max(scores, axis=0, keepdims=True))
+        attention = raised * (1.0 / jnp.sum(raised, axis=0, keepdims=True))
+        value_tiles.add(head, dot(attention.astype(BF16), back_win))
+        drawn = attention * dot_nt(value_win, back_win)
+        inner = jnp.sum(drawn, axis=0, keepdims=True)
         score_grad = ((drawn - attention * inner) * SCALE).astype(BF16)
-        query_tiles.add(head, dot(score_grad, key_win))
-        key_tiles.add(head, dot_tn(score_grad, query_win))
+        key_tiles.add(head, dot(score_grad, query_win))
+        query_tiles.add(head, dot_tn(score_grad, key_win))
         if head in (HEADS // 2 - 1, HEADS - 1):
             done = (head + 1) * HEAD_DIM // LANES * LANES
             for i in (1, 2, 3):
@@ -306,7 +309,7 @@
     rows, width = arrays[0].shape
     extra = FULL // GROUP * width + ODD_LANES
     outs = [((rows, len(arrays) * width + extra), BF16)]
-    scratch = [pltpu.VMEM((rows, extra), BF16), dma(len(arrays) + 1)]
+    scratch = [pltpu.VMEM((len(arrays), rows, width), BF16), pltpu.VMEM((rows, extra), BF16), dma(2 * len(arrays) + 1)]
     return call(pack_kernel, "pack", outs, (*arrays, weight_t), hbm_in=len(arrays), hbm_out=(0,), scratch=scratch)[0]
 
 
@@ -387,7 +390,6 @@
     parts = lax.all_to_all(chip, ("dp", "seq"), 0, 0, tiled=True, axis_index_groups=pairs)
 
     y = backward(pick, x, partner(x[:, 4 * width :]), bias, mixed)
-    parts, y = lax.optimization_barrier((parts, y))
     back = swap(y).reshape(patches, 4 * width)
     total = jnp.sum(parts.astype(F32), axis=0).astype(BF16)
     weight_grad = sum_over_pairs(total, n_dp, width)[:shard].T

time: 234 us -> 162 us (0.69)
  Pallas kernels: 105 us -> 34.2 us
    pallas_call x5, Pallas kernels: 105 us -> 34.2 us  [call(): pl.pallas_call(kernel, out_shape=[pltpu.HBM(s.shape, s.dtype) if i in hbm...]
  transfers between devices with their start and end apart: 9 -> 9, of which waited for: 7 -> 8; matrix products, arithmetic and copies ran while one was open for 2% -> 3% of each run, Pallas kernels for 9% -> 12%
where the time goes in v2:
time: 162 us; the launch traced here: 161 us
  waiting for transfers between devices  61.2 us (38%)
  starting transfers between devices  57.4 us (35%)
  Pallas kernels  34.2 us (21%)
  local copies, waits for them, and re-layouts  4.97 us (3%)
  other arithmetic  2.42 us (1%)
    all_to_all x2, waiting for transfers between devices, swap(): lax.all_to_all(block.reshape(n_seq, positions, -1), 'seq', 0, 0, tiled=True)  41.7 us
    pallas_call x5, Pallas kernels, call(): pl.pallas_call(kernel, out_shape=[pltpu.HBM(s.shape, s.dtype) if i in hbm...  34.2 us
    ppermute x4, starting transfers between devices, exchange(): return lax.ppermute(block, 'dp', [(i, i ^ hop) for i in range(n_dp)])  27.6 us
    all_to_all x2, starting transfers between devices, swap(): lax.all_to_all(block.reshape(n_seq, positions, -1), 'seq', 0, 0, tiled=True)  17.6 us
    ppermute x4, waiting for transfers between devices, exchange(): return lax.ppermute(block, 'dp', [(i, i ^ hop) for i in range(n_dp)])  12.9 us
    all_to_all x1, starting transfers between devices, on_device(): lax.all_to_all(chip, ('dp', 'seq'), 0, 0, tiled=True, axis_index_groups=p...  8.18 us
    ppermute x2, waiting for transfers between devices, partner(): return lax.ppermute(block, 'seq', [(i, i ^ 1) for i in range(n_seq)])  6.36 us
    ppermute x2, starting transfers between devices, partner(): return lax.ppermute(block, 'seq', [(i, i ^ 1) for i in range(n_seq)])  4.02 us
  transfers between devices with their start and end apart: 9, of which 8 were waited for; matrix products, arithmetic and copies ran while one was open for 3% of the time, Pallas kernels for 12%

profile of v2, /device:TPU:6, one launch (start us, length us, event | category | flops | bytes accessed | tf_op | source)
XLA Modules:
  0.0 161.1 jit_solution(11535425301564811984)
XLA Ops:
  0.6 0.0 copy-start
  0.6 0.9 copy-done
  1.5 3.8 %pack.1 = bf16[256,7296]{1,0:T(8,128)(2,1)} custom-call(bf16[256,1152]{1,0:T(8,128)(2,1)} %bitcast.25, bf16[256,1152]{1,0:T(8,128)(2,1)} %bitcast.26, bf16[256,1152]{1,0:T(8,128)(2,1)} %bitcast.27, bf16[256,1152]{1,0:T(8,128)(2,1)} %bitcast.28, bf16[36,1152]{1,0:T(8,128)(2,1)S(1)} %bitcast.21), custom_call_target="tpu_custom_call" | custom-call | bytes 6177792 | tf_op jit(solution)/shard_map/pack/pallas_call | solution.py:292
  5.3 0.0 copy-start.1
  5.3 10.4 %all-to-all-start = ((bf16[32,8,7296]{2,1,0:T(8,128)(2,1)}), bf16[32,8,7296]{2,1,0:T(8,128)(2,1)}, u32[]{:S(2)}, u32[]{:S(2)}) async-start(bf16[32,8,7296]{2,1,0:T(8,128)(2,1)} %bitcast.22), calls=%async_computation | async-start | bytes 7471104 | tf_op jit(solution)/shard_map/all_to_all | solution.py:376
  15.8 0.0 copy-done.1
  15.8 3.6 %tables.1 = (bf16[1152,1152]{1,0:T(8,128)(2,1)}, bf16[1280,1152]{1,0:T(8,128)(2,1)}, f32[256,256]{1,0:T(8,128)S(1)}) custom-call(s32[1]{0:T(128)} %bitcast.core_ref, s32[1,4]{1,0:T(1,128)S(1)} %copy-done.1), custom_call_target="tpu_custom_call" | custom-call | bytes 5865492 | tf_op jit(solution)/shard_map/tables/pallas_call | solution.py:292
  19.4 41.7 %all-to-all-done = bf16[32,8,7296]{2,1,0:T(8,128)(2,1)} async-done(((bf16[32,8,7296]{2,1,0:T(8,128)(2,1)}), bf16[32,8,7296]{2,1,0:T(8,128)(2,1)}, u32[]{:S(2)}, u32[]{:S(2)}) %all-to-all-start) | async-done | bytes 3735584 | tf_op jit(solution)/shard_map/all_to_all | solution.py:376
  61.1 10.0 %forward.1 = (bf16[256,1152]{1,0:T(8,128)(2,1)S(1)}, bf16[640,1152]{1,0:T(8,128)(2,1)S(1)}, bf16[640,1152]{1,0:T(8,128)(2,1)}) custom-call(bf16[1280,1152]{1,0:T(8,128)(2,1)} %get-tuple-element.13.turned_ref, bf16[256,7296]{1,0:T(8,128)(2,1)} %bitcast.7.x_ref, f32[256,256]{1,0:T(8,128)S(1)} %get-tuple-element.12.bias_ref), custom_call_target="tpu_custom_call" | custom-call | flops 2583691264 | bytes 10485760 | tf_op jit(solution)/shard_map/forward/pallas_call | solution.py:292
  71.1 1.9 %collective-permute-start.1 = (bf16[640,1152]{1,0:T(8,128)(2,1)}, bf16[640,1152]{1,0:T(8,128)(2,1)S(1)}, u32[]{:S(2)}, u32[]{:S(2)}) collective-permute-start(bf16[640,1152]{1,0:T(8,128)(2,1)} %get-tuple-element.16), channel_id=1, source_target_pairs={{0,1},{1,0},{2,3},{3,2},{4,5},{5,4},{6,7},{7,6},{8,9},{9,8},{10,11... | collective-permute-start | bytes 4423688 | tf_op jit(solution)/shard_map/ppermute | solution.py:379
  73.0 3.4 %collective-permute-done.1.theirs_ref = bf16[640,1152]{1,0:T(8,128)(2,1)S(1)} collective-permute-done((bf16[640,1152]{1,0:T(8,128)(2,1)}, bf16[640,1152]{1,0:T(8,128)(2,1)S(1)}, u32[]{:S(2)}, u32[]{:S(2)}) %collective-permute-start.1) | collective-permute-done | bytes 1474592 | tf_op jit(solution)/shard_map/ppermute | solution.py:379
  76.5 1.5 join.1
  78.0 8.2 %all-to-all-start.2 = ((bf16[32,40,640]{2,1,0:T(8,128)(2,1)}), bf16[32,40,640]{2,1,0:T(8,128)(2,1)S(1)}, u32[]{:S(2)}, u32[]{:S(2)}) async-start(bf16[32,40,640]{2,1,0:T(8,128)(2,1)} %bitcast.14), calls=%async_computation.2 | async-start | bytes 3276800 | tf_op jit(solution)/shard_map/all_to_all | solution.py:390
  86.2 1.4 slice.29
  87.6 2.1 %collective-permute-start = (bf16[256,2688]{1,0:T(8,128)(2,1)S(1)}, bf16[256,2688]{1,0:T(8,128)(2,1)S(1)}, u32[]{:S(2)}, u32[]{:S(2)}) collective-permute-start(bf16[256,2688]{1,0:T(8,128)(2,1)S(1)} %slice.29), channel_id=1, source_target_pairs={{0,1},{1,0},{2,3},{3,2},{4,5},{5,4},{6,7},{7,6},{8,9},{9,8},{10,11... | collective-permute-start | bytes 4128776 | tf_op jit(solution)/shard_map/ppermute | solution.py:379
  89.7 2.9 %collective-permute-done.other_ref = bf16[256,2688]{1,0:T(8,128)(2,1)S(1)} collective-permute-done((bf16[256,2688]{1,0:T(8,128)(2,1)S(1)}, bf16[256,2688]{1,0:T(8,128)(2,1)S(1)}, u32[]{:S(2)}, u32[]{:S(2)}) %collective-permute-start) | collective-permute-done | bytes 1376288 | tf_op jit(solution)/shard_map/ppermute | solution.py:379
  92.6 15.4 %backward.1 = bf16[256,4608]{1,0:T(8,128)(2,1)} custom-call(bf16[1152,1152]{1,0:T(8,128)(2,1)} %get-tuple-element.11.pick_hbm, bf16[256,7296]{1,0:T(8,128)(2,1)} %bitcast.7.x_ref, bf16[256,2688]{1,0:T(8,128)(2,1)S(1)} %collective-permute-done.other_ref, f32[256,256]{1,0:T(8,128)S(1)} %get-tuple-element.12.bias_ref, ...), custom_call_target="tpu_custom_call" | custom-call | flops 5939134464 | bytes 10977280 | tf_op jit(solution)/shard_map/backward/pallas_call | solution.py:292
  108.0 0.3 all-to-all-done.2
  108.3 1.2 copy-done.2
  109.5 7.2 %all-to-all-start.1 = ((bf16[32,8,4608]{2,1,0:T(8,128)(2,1)}), bf16[32,8,4608]{2,1,0:T(8,128)(2,1)S(1)}, u32[]{:S(2)}, u32[]{:S(2)}) async-start(bf16[32,8,4608]{2,1,0:T(8,128)(2,1)} %bitcast.24), calls=%async_computation.1 | async-start | bytes 4718592 | tf_op jit(solution)/shard_map/all_to_all | solution.py:376
  116.6 1.7 %reduce_sum.12 = bf16[40,640]{1,0:T(8,128)(2,1)S(1)} reduce(bf16[32,40,640]{2,1,0:T(8,128)(2,1)} %copy-done.2, bf16[]{:T(256)} %constant.15.clone.1), dimensions={0}, to_apply=%region_0.0 | reduce | flops 793600 | bytes 1689602 | tf_op jit(solution)/shard_map/reduce_sum | solution.py:394
  118.3 3.8 %collective-permute-start.2 = (bf16[40,640]{1,0:T(8,128)(2,1)S(1)}, bf16[40,640]{1,0:T(8,128)(2,1)S(1)}, u32[]{:S(2)}, u32[]{:S(2)}) collective-permute-start(bf16[40,640]{1,0:T(8,128)(2,1)S(1)} %reduce_sum.12), channel_id=1, source_target_pairs={{0,64},{32,96},{64,0},{96,32},{128,192},{160,224},{192,128},{224,1... | collective-permute-start | bytes 153608 | tf_op jit(solution)/shard_map/ppermute | solution.py:356
  122.1 4.2 %collective-permute-done.2 = bf16[40,640]{1,0:T(8,128)(2,1)S(1)} collective-permute-done((bf16[40,640]{1,0:T(8,128)(2,1)S(1)}, bf16[40,640]{1,0:T(8,128)(2,1)S(1)}, u32[]{:S(2)}, u32[]{:S(2)}) %collective-permute-start.2) | collective-permute-done | bytes 51232 | tf_op jit(solution)/shard_map/ppermute | solution.py:356
  126.3 8.1 %collective-permute-start.3 = (bf16[40,640]{1,0:T(8,128)(2,1)S(1)}, bf16[40,640]{1,0:T(8,128)(2,1)S(1)}, u32[]{:S(2)}, u32[]{:S(2)}) collective-permute-start(bf16[40,640]{1,0:T(8,128)(2,1)S(1)} %add_convert_fusion.2), channel_id=1, source_target_pairs={{0,128},{32,160},{64,192},{96,224},{128,0},{160,32},{192,64},{224,... | collective-permute-start | bytes 153608 | tf_op jit(solution)/shard_map/ppermute | solution.py:356
  134.4 3.6 %collective-permute-done.3 = bf16[40,640]{1,0:T(8,128)(2,1)S(1)} collective-permute-done((bf16[40,640]{1,0:T(8,128)(2,1)S(1)}, bf16[40,640]{1,0:T(8,128)(2,1)S(1)}, u32[]{:S(2)}, u32[]{:S(2)}) %collective-permute-start.3) | collective-permute-done | bytes 51232 | tf_op jit(solution)/shard_map/ppermute | solution.py:356
  138.0 13.7 %collective-permute-start.4 = (bf16[40,640]{1,0:T(8,128)(2,1)S(1)}, bf16[40,640]{1,0:T(8,128)(2,1)S(1)}, u32[]{:S(2)}, u32[]{:S(2)}) collective-permute-start(bf16[40,640]{1,0:T(8,128)(2,1)S(1)} %add_convert_fusion.1), channel_id=1, source_target_pairs={{0,256},{32,288},{64,320},{96,352},{128,384},{160,416},{192,448},{... | collective-permute-start | bytes 153608 | tf_op jit(solution)/shard_map/ppermute | solution.py:356
  151.7 2.6 %collective-permute-done.4 = bf16[40,640]{1,0:T(8,128)(2,1)S(1)} collective-permute-done((bf16[40,640]{1,0:T(8,128)(2,1)S(1)}, bf16[40,640]{1,0:T(8,128)(2,1)S(1)}, u32[]{:S(2)}, u32[]{:S(2)}) %collective-permute-start.4) | collective-permute-done | bytes 51232 | tf_op jit(solution)/shard_map/ppermute | solution.py:356
  154.4 2.0 %collective-permute-start.5 = (bf16[40,640]{1,0:T(8,128)(2,1)S(1)}, bf16[40,640]{1,0:T(8,128)(2,1)S(1)}, u32[]{:S(2)}, u32[]{:S(2)}) collective-permute-start(bf16[40,640]{1,0:T(8,128)(2,1)S(1)} %add_convert_fusion), channel_id=1, source_target_pairs={{0,32},{32,0},{64,96},{96,64},{128,160},{160,128},{192,224},{224,1... | collective-permute-start | bytes 153608 | tf_op jit(solution)/shard_map/ppermute | solution.py:356
  156.4 0.0 all-to-all-done.1
  156.4 1.4 slice_bitcast_fusion
  157.9 2.5 %collective-permute-done.5 = bf16[40,640]{1,0:T(8,128)(2,1)S(1)} collective-permute-done((bf16[40,640]{1,0:T(8,128)(2,1)S(1)}, bf16[40,640]{1,0:T(8,128)(2,1)S(1)}, u32[]{:S(2)}, u32[]{:S(2)}) %collective-permute-start.5) | collective-permute-done | bytes 51232 | tf_op jit(solution)/shard_map/ppermute | solution.py:356
  160.4 0.7 convert_bitcast_fusion
  (6 shorter events, 0.1 us)
Async XLA Ops:
  0.6 0.9 copy-start
  5.3 10.5 %copy-start.1 = (s32[1,4]{1,0:T(1,128)S(1)}, s32[1,4]{1,0:T(1,128)}, u32[]{:S(2)}) copy-start(s32[1,4]{1,0:T(1,128)} %lens_ref.1) | copy-start | bytes 52
  5.3 55.8 %all-to-all-start = ((bf16[32,8,7296]{2,1,0:T(8,128)(2,1)}), bf16[32,8,7296]{2,1,0:T(8,128)(2,1)}, u32[]{:S(2)}, u32[]{:S(2)}) async-start(bf16[32,8,7296]{2,1,0:T(8,128)(2,1)} %bitcast.22), calls=%async_computation | async-start | bytes 7471104 | tf_op jit(solution)/shard_map/all_to_all | solution.py:376
  71.1 5.4 %collective-permute-start.1 = (bf16[640,1152]{1,0:T(8,128)(2,1)}, bf16[640,1152]{1,0:T(8,128)(2,1)S(1)}, u32[]{:S(2)}, u32[]{:S(2)}) collective-permute-start(bf16[640,1152]{1,0:T(8,128)(2,1)} %get-tuple-element.16), channel_id=1, source_target_pairs={{0,1},{1,0},{2,3},{3,2},{4,5},{5,4},{6,7},{7,6},{8,9},{9,8},{10,11... | collective-permute-start | bytes 4423688 | tf_op jit(solution)/shard_map/ppermute | solution.py:379
  78.0 30.3 %all-to-all-start.2 = ((bf16[32,40,640]{2,1,0:T(8,128)(2,1)}), bf16[32,40,640]{2,1,0:T(8,128)(2,1)S(1)}, u32[]{:S(2)}, u32[]{:S(2)}) async-start(bf16[32,40,640]{2,1,0:T(8,128)(2,1)} %bitcast.14), calls=%async_computation.2 | async-start | bytes 3276800 | tf_op jit(solution)/shard_map/all_to_all | solution.py:390
  87.6 5.0 %collective-permute-start = (bf16[256,2688]{1,0:T(8,128)(2,1)S(1)}, bf16[256,2688]{1,0:T(8,128)(2,1)S(1)}, u32[]{:S(2)}, u32[]{:S(2)}) collective-permute-start(bf16[256,2688]{1,0:T(8,128)(2,1)S(1)} %slice.29), channel_id=1, source_target_pairs={{0,1},{1,0},{2,3},{3,2},{4,5},{5,4},{6,7},{7,6},{8,9},{9,8},{10,11... | collective-permute-start | bytes 4128776 | tf_op jit(solution)/shard_map/ppermute | solution.py:379
  108.3 1.2 copy-start.2
  109.5 46.9 %all-to-all-start.1 = ((bf16[32,8,4608]{2,1,0:T(8,128)(2,1)}), bf16[32,8,4608]{2,1,0:T(8,128)(2,1)S(1)}, u32[]{:S(2)}, u32[]{:S(2)}) async-start(bf16[32,8,4608]{2,1,0:T(8,128)(2,1)} %bitcast.24), calls=%async_computation.1 | async-start | bytes 4718592 | tf_op jit(solution)/shard_map/all_to_all | solution.py:376
  118.3 8.0 %collective-permute-start.2 = (bf16[40,640]{1,0:T(8,128)(2,1)S(1)}, bf16[40,640]{1,0:T(8,128)(2,1)S(1)}, u32[]{:S(2)}, u32[]{:S(2)}) collective-permute-start(bf16[40,640]{1,0:T(8,128)(2,1)S(1)} %reduce_sum.12), channel_id=1, source_target_pairs={{0,64},{32,96},{64,0},{96,32},{128,192},{160,224},{192,128},{224,1... | collective-permute-start | bytes 153608 | tf_op jit(solution)/shard_map/ppermute | solution.py:356
  126.3 11.7 %collective-permute-start.3 = (bf16[40,640]{1,0:T(8,128)(2,1)S(1)}, bf16[40,640]{1,0:T(8,128)(2,1)S(1)}, u32[]{:S(2)}, u32[]{:S(2)}) collective-permute-start(bf16[40,640]{1,0:T(8,128)(2,1)S(1)} %add_convert_fusion.2), channel_id=1, source_target_pairs={{0,128},{32,160},{64,192},{96,224},{128,0},{160,32},{192,64},{224,... | collective-permute-start | bytes 153608 | tf_op jit(solution)/shard_map/ppermute | solution.py:356
  138.0 16.3 %collective-permute-start.4 = (bf16[40,640]{1,0:T(8,128)(2,1)S(1)}, bf16[40,640]{1,0:T(8,128)(2,1)S(1)}, u32[]{:S(2)}, u32[]{:S(2)}) collective-permute-start(bf16[40,640]{1,0:T(8,128)(2,1)S(1)} %add_convert_fusion.1), channel_id=1, source_target_pairs={{0,256},{32,288},{64,320},{96,352},{128,384},{160,416},{192,448},{... | collective-permute-start | bytes 153608 | tf_op jit(solution)/shard_map/ppermute | solution.py:356
  154.4 6.0 %collective-permute-start.5 = (bf16[40,640]{1,0:T(8,128)(2,1)S(1)}, bf16[40,640]{1,0:T(8,128)(2,1)S(1)}, u32[]{:S(2)}, u32[]{:S(2)}) collective-permute-start(bf16[40,640]{1,0:T(8,128)(2,1)S(1)} %add_convert_fusion), channel_id=1, source_target_pairs={{0,32},{32,0},{64,96},{96,64},{128,160},{160,128},{192,224},{224,1... | collective-permute-start | bytes 153608 | tf_op jit(solution)/shard_map/ppermute | solution.py:356

commit v3 on v2

--- a/solution.py
+++ b/solution.py
@@ -98,13 +98,20 @@
 
 
 def pack_kernel(*refs):
-    *parts, weight_ref, x_ref, staged_ref, held_ref, sems = refs
-    shard, width = weight_ref.shape
-    rows = held_ref.shape[0]
-    fetches = [pltpu.make_async_copy(part, staged_ref.at[i], sems.at[i]) for i, part in enumerate(parts)]
+    *parts, weight_hbm, x_ref, staged_ref, weight_ref, held_ref, sems, weight_sems = refs
+    rows, width = parts[0].shape
+    shard = weight_ref.shape[0]
+    half = rows // 2
+    fetch_weight = pltpu.make_async_copy(weight_hbm, weight_ref, weight_sems.at[0])
+    fetch_weight.start()
+    fetches, copies = [], []
+    for i, part in enumerate(parts):
+        for j in range(2):
+            at, lanes, n = pl.ds(j * half, half), pl.ds(i * width, width), 2 * i + j
+            fetches.append(pltpu.make_async_copy(part.at[at], staged_ref.at[i, at], sems.at[0, n]))
+            copies.append(pltpu.make_async_copy(staged_ref.at[i, at], x_ref.at[at, lanes], sems.at[1, n]))
     for fetch in fetches:
         fetch.start()
-    weight = weight_ref[...]
 
     def core(row):
         return jnp.bitwise_and(lax.div(row, jnp.int32(GROUP)), 1)
@@ -112,9 +119,14 @@
     def place(row):
         return jnp.bitwise_and(row, GROUP - 1)
 
+    fetch_weight.wait()
+    weight = weight_ref[...]
     for block in range(FULL // GROUP):
         pick = selection(rows, shard, lambda row: FULL * core(row) + GROUP * block + place(row))
         held_ref[:, pl.ds(block * width, width)] = dot(pick, weight).astype(BF16)
+    for fetch, copy in list(zip(fetches, copies))[:4]:
+        fetch.wait()
+        copy.start()
     odd = jnp.zeros((rows, ODD_LANES), F32)
     for q in range(CHUNK):
 
@@ -126,14 +138,12 @@
         odd = odd + dot(selection(rows, shard, wanted), chunk_tiles(weight_ref, q))
     held_ref[:, pl.ds(FULL // GROUP * width, ODD_LANES)] = odd.astype(BF16)
     lanes = pl.ds(len(parts) * width, held_ref.shape[1])
-    copies = [pltpu.make_async_copy(held_ref, x_ref.at[:, lanes], sems.at[2 * len(parts)])]
-    copies[-1].start()
-    for i, fetch in enumerate(fetches):
+    last = pltpu.make_async_copy(held_ref, x_ref.at[:, lanes], weight_sems.at[1])
+    last.start()
+    for fetch, copy in list(zip(fetches, copies))[4:]:
         fetch.wait()
-        lanes = pl.ds(i * width, width)
-        copies.append(pltpu.make_async_copy(staged_ref.at[i], x_ref.at[:, lanes], sems.at[len(parts) + i]))
-        copies[-1].start()
-    for copy in copies:
+        copy.start()
+    for copy in (*copies, last):
         copy.wait()
 
 
@@ -145,13 +155,11 @@
         ref[pl.ds(step * block, block), :] = jnp.where(at == place, 1.0, 0.0).astype(BF16)
 
 
-def tables_kernel(shard, pitch, positions, core_ref, lens_ref, pick_ref, turned_ref, bias_ref, held_ref, sems):
-    padded, width = turned_ref.shape
+def tables_kernel(shard, positions, core_ref, lens_ref, pick_ref, bias_ref, held_ref, sem):
+    width = pick_ref.shape[1]
     feature = lax.broadcasted_iota(jnp.int32, (1, width), 1)
     owner = lax.div(feature, jnp.int32(shard))
     rest = feature - owner * shard
-    other = jnp.bitwise_and(owner + core_ref[0], 1)
-    turned = other * (padded // 2) + lax.div(owner, jnp.int32(2)) * pitch + rest
     holder = jnp.where(rest < 2 * FULL, lax.div(rest, jnp.int32(FULL)), lax.div(rest - 2 * FULL, jnp.int32(ODD)))
     other = jnp.bitwise_and(holder + core_ref[0], 1)
     within = rest - FULL * holder
@@ -159,25 +167,34 @@
     size = width // shard * GROUP
     full = (other * (FULL // GROUP) + block) * size + owner * GROUP + within - block * GROUP
     odd = 2 * (FULL // GROUP) * size + (other * (width // shard) + owner) * ODD + rest - 2 * FULL - ODD * holder
-    picked = jnp.where(rest < 2 * FULL, full, odd)
-    copies = []
-    for i, (ref, place) in enumerate(((turned_ref, turned), (pick_ref, picked))):
-        rows = pl.ds(0, ref.shape[0])
-        pick_rows(held_ref.at[i, rows], place)
-        copies.append(pltpu.make_async_copy(held_ref.at[i, rows], ref, sems.at[i]))
-        copies[-1].start()
+    pick_rows(held_ref, jnp.where(rest < 2 * FULL, full, odd))
+    copy = pltpu.make_async_copy(held_ref, pick_ref, sem.at[0])
+    copy.start()
     bias_ref[...] = clip_bias(lens_ref, bias_ref.shape[0], positions)
-    for copy in copies:
-        copy.wait()
-
-
-def forward_kernel(turned_ref, x_ref, bias_ref, mixed_ref, keep_ref, send_ref, pick_ref, held_ref, sems):
-    fetch = pltpu.make_async_copy(turned_ref, pick_ref, sems.at[4])
-    fetch.start()
+    copy.wait()
+
+
+def forward_kernel(
+    core_ref, x_hbm, bias_ref, mixed_ref, keep_ref, send_ref, rest_ref, x_ref, left_ref, part_ref, held_ref, sems
+):
     rows, width = mixed_ref.shape
+    middle = lane_half(width)
+    pieces = [(a * width + b, c) for b, c in ((0, middle), (middle, width - middle)) for a in range(3)]
+    pieces.append((3 * width, width))
+    fetches = [
+        pltpu.make_async_copy(x_hbm.at[:, pl.ds(at, size)], x_ref.at[:, pl.ds(at, size)], sems.at[5 + i])
+        for i, (at, size) in enumerate(pieces)
+    ]
+    left = pl.ds(4 * width, left_ref.shape[1])
+    fetches.append(pltpu.make_async_copy(x_hbm.at[:, left], left_ref, sems.at[5 + len(pieces)]))
+    for fetch in fetches:
+        fetch.start()
     bias = bias_ref[...]
     mixed_tiles = Tiles(mixed_ref)
     for head in range(HEADS):
+        if head in (0, HEADS // 2):
+            for fetch in fetches[3 * (head > 0) : 3 * (head > 0) + 3]:
+                fetch.wait()
         start, size = window(head)
         lanes = head_lanes(head, rows)
         query_win = jnp.where(lanes, x_ref[:, pl.ds(start, size)], 0)
@@ -185,39 +202,53 @@
         value_win = jnp.where(lanes, x_ref[:, pl.ds(2 * width + start, size)], 0)
         raised, recip = softmax(query_win, key_win, bias)
         mixed_tiles.add(head, dot((raised * recip).astype(BF16), value_win))
+    fetches[7].wait()
+    copies = [pltpu.make_async_copy(left_ref, rest_ref, sems.at[4])]
+    copies[0].start()
+    fetches[6].wait()
     mixed = mixed_ref[...]
-    grad = x_ref[:, pl.ds(3 * width, width)]
-    half = keep_ref.shape[0]
-    block = half // 4
-    copies = []
-    fetch.wait()
-    for step in (4, 5, 6, 7, 0, 1, 2, 3):
-        grad_rows = dot_nt(pick_ref[pl.ds(step * block, block), :], grad).astype(BF16)
-        part = dot(grad_rows, mixed).astype(BF16)
-        at = pl.ds((step % 4) * block, block)
-        if step < 4:
-            keep_ref[at, :] = part
-        else:
-            held_ref[at, :] = part
-            copies.append(pltpu.make_async_copy(held_ref.at[at, :], send_ref.at[at, :], sems.at[step % 4]))
-            copies[-1].start()
+    block = 3 * LANES
+    for at in range(0, width, block):
+        part_ref[pl.ds(at, block), :] = dot_tn(x_ref[:, pl.ds(3 * width + at, block)], mixed)
+    chips, pitch, _ = held_ref.shape
+    own = core_ref[0] * (width // chips - pitch)
+    other = (width // chips - pitch) - own
+    for step in range(4):
+        some = chips // 4
+        for j in range(step * some, (step + 1) * some):
+            at = pl.multiple_of(j * (width // chips) + other, 8)
+            held_ref[j] = part_ref[pl.ds(at, pitch), :].astype(BF16)
+        ids = pl.ds(step * some, some)
+        copies.append(pltpu.make_async_copy(held_ref.at[ids], send_ref.at[ids], sems.at[step]))
+        copies[-1].start()
+    for j in range(chips):
+        at = pl.multiple_of(j * (width // chips) + own, 8)
+        keep_ref[j] = part_ref[pl.ds(at, pitch), :].astype(BF16)
     for copy in copies:
         copy.wait()
 
 
 def join_kernel(keep_ref, theirs_ref, out_ref):
-    size = out_ref.shape[2]
+    size = out_ref.shape[3]
     total = (keep_ref[...].astype(F32) + theirs_ref[...].astype(F32)).astype(BF16)
-    out_ref[0] = total[:, :size]
-    out_ref[1] = total[:, total.shape[1] - size :]
+    out_ref[0] = total[:, :, :size]
+    out_ref[1] = total[:, :, total.shape[2] - size :]
 
 
 def backward_kernel(
-    pick_hbm, x_ref, other_ref, bias_ref, mixed_ref, y_ref, pick_ref, odd_ref, back_ref, out_ref, held_ref, sems
+    pick_hbm, x_hbm, own_hbm, other_ref, bias_ref, mixed_ref, y_ref,
+    pick_ref, x_ref, own_ref, odd_ref, back_ref, out_ref, held_ref, sems
 ):
     rows, width = mixed_ref.shape
-    fetch = pltpu.make_async_copy(pick_hbm, pick_ref, sems.at[7])
-    fetch.start()
+    three, fourth = pl.ds(0, 3 * width), pl.ds(3 * width, width)
+    fetches = [
+        pltpu.make_async_copy(own_hbm, own_ref, sems.at[7]),
+        pltpu.make_async_copy(pick_hbm, pick_ref, sems.at[8]),
+        pltpu.make_async_copy(x_hbm.at[:, fourth], x_ref.at[:, fourth], sems.at[9]),
+        pltpu.make_async_copy(x_hbm.at[:, three], x_ref.at[:, three], sems.at[10]),
+    ]
+    for fetch in fetches:
+        fetch.start()
     copies = []
 
     def send(start, size):
@@ -226,12 +257,13 @@
         copies[-1].start()
 
     blocks = FULL // GROUP
+    fetches[0].wait()
     weight = []
-    for ref, base in ((x_ref, 4 * width), (other_ref, 0)):
-        weight += [ref[:, pl.ds(base + b * width, width)] for b in range(blocks)]
+    for ref in (own_ref, other_ref):
+        weight += [ref[:, pl.ds(b * width, width)] for b in range(blocks)]
     odd_rows = odd_ref.shape[0] // 2
-    for i, (ref, base) in enumerate(((x_ref, 4 * width), (other_ref, 0))):
-        left = ref[:, pl.ds(base + blocks * width, ODD_LANES)]
+    for i, ref in enumerate((own_ref, other_ref)):
+        left = ref[:, pl.ds(blocks * width, ODD_LANES)]
         for q in range(CHUNK):
 
             def wanted(row):
@@ -243,8 +275,9 @@
                 lanes = pl.ds((CHUNK * u + q) * LANES, LANES)
                 odd_ref[pl.ds(i * odd_rows, odd_rows), lanes] = got[:, u * LANES : (u + 1) * LANES]
     weight.append(odd_ref[...])
-    fetch.wait()
-    grad = dot_nt(x_ref[:, pl.ds(3 * width, width)], pick_ref[...]).astype(BF16)
+    fetches[1].wait()
+    fetches[2].wait()
+    grad = dot_nt(x_ref[:, fourth], pick_ref[...]).astype(BF16)
     mixed = mixed_ref[...]
     back = jnp.zeros((rows, width), F32)
     at = 0
@@ -258,6 +291,7 @@
     send(0, width)
     query_tiles, key_tiles, value_tiles = [Tiles(held_ref, i * width) for i in (1, 2, 3)]
     bias = bias_ref[...]
+    fetches[3].wait()
     sent = 0
     for head in range(HEADS):
         start, size = window(head)
@@ -284,6 +318,23 @@
         copy.wait()
 
 
+def total_kernel(parts_hbm, out_ref, parts_ref, sems):
+    count = parts_hbm.shape[0]
+    step = count // 4
+    fetches = [
+        pltpu.make_async_copy(parts_hbm.at[pl.ds(i * step, step)], parts_ref.at[pl.ds(i * step, step)], sems.at[i])
+        for i in range(4)
+    ]
+    for fetch in fetches:
+        fetch.start()
+    total = jnp.zeros(out_ref.shape, F32)
+    for i, fetch in enumerate(fetches):
+        fetch.wait()
+        for j in range(i * step, (i + 1) * step):
+            total = total + parts_ref[j].astype(F32)
+    out_ref[...] = total.astype(BF16)
+
+
 def call(kernel, name, outs, args, smem=0, hbm_in=0, hbm_out=(), scratch=(), flops=0):
     space = [pltpu.SMEM] * smem + [pltpu.HBM] * hbm_in + [pltpu.VMEM] * (len(args) - smem - hbm_in)
     args = [pltpu.with_memory_space_constraint(a, s) if s == pltpu.HBM else a for a, s in zip(args, space)]
@@ -307,44 +358,59 @@
 
 def pack(arrays, weight_t):
     rows, width = arrays[0].shape
+    count = len(arrays)
     extra = FULL // GROUP * width + ODD_LANES
-    outs = [((rows, len(arrays) * width + extra), BF16)]
-    scratch = [pltpu.VMEM((len(arrays), rows, width), BF16), pltpu.VMEM((rows, extra), BF16), dma(2 * len(arrays) + 1)]
-    return call(pack_kernel, "pack", outs, (*arrays, weight_t), hbm_in=len(arrays), hbm_out=(0,), scratch=scratch)[0]
-
-
-def tables(core, lengths, rows, width, shard, pitch, positions):
-    kernel = functools.partial(tables_kernel, shard, pitch, positions)
-    padded = width // shard * pitch
-    outs = [((width, width), BF16), ((padded, width), BF16), ((rows, rows), F32)]
-    scratch = [pltpu.VMEM((2, padded, width), BF16), dma(2)]
-    return call(kernel, "tables", outs, (core, lengths), smem=2, hbm_out=(0, 1), scratch=scratch)
-
-
-def forward(x, turned, bias):
-    rows = x.shape[0]
-    padded, width = turned.shape
-    half = (padded // 2, width)
-    outs = [((rows, width), BF16), (half, BF16), (half, BF16)]
-    flops = 4 * padded * rows * width + 4 * HEADS * rows * rows * 256
-    scratch = [pltpu.VMEM(turned.shape, BF16), pltpu.VMEM(half, BF16), dma(5)]
-    return call(forward_kernel, "forward", outs, (turned, x, bias), hbm_in=1, hbm_out=(2,), scratch=scratch, flops=flops)
+    outs = [((rows, count * width + extra), BF16)]
+    scratch = [
+        pltpu.VMEM((count, rows, width), BF16),
+        pltpu.VMEM(weight_t.shape, BF16),
+        pltpu.VMEM((rows, extra), BF16),
+        pltpu.SemaphoreType.DMA((2, 2 * count)),
+        dma(2),
+    ]
+    args = (*arrays, weight_t)
+    return call(pack_kernel, "pack", outs, args, hbm_in=count + 1, hbm_out=(0,), scratch=scratch)[0]
+
+
+def tables(core, lengths, rows, width, shard, positions):
+    kernel = functools.partial(tables_kernel, shard, positions)
+    outs = [((width, width), BF16), ((rows, rows), F32)]
+    scratch = [pltpu.VMEM((width, width), BF16), dma(1)]
+    return call(kernel, "tables", outs, (core, lengths), smem=2, hbm_out=(0,), scratch=scratch)
+
+
+def forward(core, x, bias, width, chips):
+    rows, wide = x.shape
+    pitch = -(-width // chips // 2 // 8) * 8
+    part, rest = (chips, pitch, width), (rows, wide - 4 * width)
+    outs = [((rows, width), BF16), (part, BF16), (part, BF16), (rest, BF16)]
+    flops = 2 * width * rows * width + 4 * HEADS * rows * rows * 256
+    scratch = [pltpu.VMEM((rows, 4 * width), BF16), pltpu.VMEM(rest, BF16), pltpu.VMEM((width, width), F32)]
+    scratch += [pltpu.VMEM(part, BF16), dma(13)]
+    args = (core, x, bias)
+    return call(
+        forward_kernel, "forward", outs, args, smem=1, hbm_in=1, hbm_out=(2, 3), scratch=scratch, flops=flops
+    )
 
 
 def join(keep, theirs):
-    rows, width = keep.shape
-    return call(join_kernel, "join", [((2, rows, lane_half(width)), BF16)], (keep, theirs))[0]
-
-
-def backward(pick, x, other, bias, mixed):
+    chips, pitch, width = keep.shape
+    return call(join_kernel, "join", [((2, chips, pitch, lane_half(width)), BF16)], (keep, theirs))[0]
+
+
+def backward(pick, x, own, other, bias, mixed):
     rows, width = mixed.shape
     flops = 8 * width * rows * width + 12 * HEADS * rows * rows * 256
-    one = pltpu.VMEM((rows, width), BF16)
-    odd = pltpu.VMEM((width - 4 * rows, width), BF16)
-    scratch = [pltpu.VMEM((width, width), BF16), odd, one, one, pltpu.VMEM((rows, 4 * width), BF16), dma(8)]
-    args = (pick, x, other, bias, mixed)
-    outs = [((rows, 4 * width), BF16)]
-    return call(backward_kernel, "backward", outs, args, hbm_in=1, hbm_out=(0,), scratch=scratch, flops=flops)[0]
+    one, wide = (rows, width), (rows, 4 * width)
+    shapes = ((width, width), wide, own.shape, (width - 4 * rows, width), one, one, wide)
+    scratch = [pltpu.VMEM(shape, BF16) for shape in shapes] + [dma(11)]
+    args = (pick, x, own, other, bias, mixed)
+    return call(backward_kernel, "backward", [(wide, BF16)], args, hbm_in=3, hbm_out=(0,), scratch=scratch, flops=flops)[0]
+
+
+def total_of(parts):
+    scratch = [pltpu.VMEM(parts.shape, BF16), dma(4)]
+    return call(total_kernel, "total", [(parts.shape[1:], BF16)], (parts,), hbm_in=1, scratch=scratch)[0]
 
 
 def lane_half(width):
@@ -352,14 +418,18 @@
 
 
 def sum_over_pairs(block, n_dp, width):
-    def exchange(block, hop):
-        return lax.ppermute(block, "dp", [(i, i ^ hop) for i in range(n_dp)])
+    def exchange(block, other):
+        return lax.ppermute(block, "dp", [(i, other(i)) for i in range(n_dp)])
+
+    def mirrored(i):
+        return i ^ (n_dp // 2) if (i + 1) % (n_dp // 2) == 0 else n_dp - 2 - i
 
     hop = 2
     while hop < n_dp:
-        block = (block.astype(F32) + exchange(block, hop).astype(F32)).astype(BF16)
+        theirs = exchange(block, mirrored if hop == n_dp // 2 else lambda i: i ^ hop)
+        block = (block.astype(F32) + theirs.astype(F32)).astype(BF16)
         hop *= 2
-    theirs = exchange(block, 1)
+    theirs = exchange(block, lambda i: i ^ 1)
     low = jnp.bitwise_and(lax.axis_index("dp"), 1) == 0
     lower, upper = jnp.where(low, block, theirs), jnp.where(low, theirs, block)
     return jnp.concatenate([lower, upper[:, 2 * lower.shape[1] - width :]], axis=1).astype(F32)
@@ -369,7 +439,6 @@
     patches, width = queries.shape[2:]
     positions = patches // n_seq
     shard = out_weight.shape[1]
-    pitch = -(-shard // 8) * 8
     core = jnp.bitwise_and(lax.axis_index("seq"), 1).astype(jnp.int32)
 
     def swap(block):
@@ -380,19 +449,20 @@
 
     arrays = [a.reshape(patches, width) for a in (queries, key_vectors, value_vectors, out_grad)]
     x = swap(pack(arrays, out_weight.T)).reshape(patches, -1)
-    pick, turned, bias = tables(core.reshape(1), clip_frames, patches, width, shard, pitch, positions)
-    mixed, keep, send = forward(x, turned, bias)
-
-    chip = join(keep, partner(send)).reshape(n_seq, pitch, -1)
+    pick, bias = tables(core.reshape(1), clip_frames, patches, width, shard, positions)
+    mixed, keep, send, own = forward(core.reshape(1), x, bias, width, n_seq // 2)
+
+    chip = join(keep, partner(send))
+    chip = chip.reshape(n_seq, *chip.shape[2:])
     pairs = [
         [(p + d) * n_seq + i for d in (0, 1) for i in range(c, n_seq, 2)] for p in range(0, n_dp, 2) for c in (0, 1)
     ]
     parts = lax.all_to_all(chip, ("dp", "seq"), 0, 0, tiled=True, axis_index_groups=pairs)
 
-    y = backward(pick, x, partner(x[:, 4 * width :]), bias, mixed)
+    y = backward(pick, x, own, partner(own), bias, mixed)
     back = swap(y).reshape(patches, 4 * width)
-    total = jnp.sum(parts.astype(F32), axis=0).astype(BF16)
-    weight_grad = sum_over_pairs(total, n_dp, width)[:shard].T
+    total = sum_over_pairs(total_of(parts), n_dp, width)
+    weight_grad = jnp.where(core == 0, total[:shard], total[total.shape[0] - shard :]).T
     outs = [back[:, i * width : (i + 1) * width].reshape(queries.shape) for i in range(4)]
     return (*outs, weight_grad)
 

time: 162 us -> 152 us (0.938)
  the two profiles are of different devices: /device:TPU:6 before, /device:TPU:224 now
where the time goes in v3:
time: 152 us
  waiting for transfers between devices  79.7 us (52%)
  starting transfers between devices  37.6 us (25%)
  Pallas kernels  30.2 us (20%)
  local copies, waits for them, and re-layouts  2.64 us (2%)
    all_to_all x2, waiting for transfers between devices, swap(): lax.all_to_all(block.reshape(n_seq, positions, -1), 'seq', 0, 0, tiled=True)  44.7 us
    pallas_call x6, Pallas kernels, call(): pl.pallas_call(kernel, out_shape=[pltpu.HBM(s.shape, s.dtype) if i in hbm...  30.2 us
    ppermute x4, waiting for transfers between devices, exchange(): return lax.ppermute(block, 'dp', [(i, other(i)) for i in range(n_dp)])  25.2 us
    ppermute x4, starting transfers between devices, exchange(): return lax.ppermute(block, 'dp', [(i, other(i)) for i in range(n_dp)])  14.3 us
    all_to_all x2, starting transfers between devices, swap(): lax.all_to_all(block.reshape(n_seq, positions, -1), 'seq', 0, 0, tiled=True)  12 us
    all_to_all x1, starting transfers between devices, on_device(): lax.all_to_all(chip, ('dp', 'seq'), 0, 0, tiled=True, axis_index_groups=p...  7.38 us
    ppermute x2, waiting for transfers between devices, partner(): return lax.ppermute(block, 'seq', [(i, i ^ 1) for i in range(n_seq)])  6.57 us
    ppermute x2, starting transfers between devices, partner(): return lax.ppermute(block, 'seq', [(i, i ^ 1) for i in range(n_seq)])  4.02 us
  transfers between devices with their start and end apart: 9, of which 8 were waited for; matrix products, arithmetic and copies ran while one was open for 1% of the time, Pallas kernels for 12%

profile of v3, /device:TPU:224, one launch (start us, length us, event | category | flops | bytes accessed | tf_op | source)
XLA Modules:
  0.0 151.7 jit_solution(17190809765814303366)
XLA Ops:
  0.6 4.0 %pack.1 = bf16[256,7296]{1,0:T(8,128)(2,1)} custom-call(bf16[256,1152]{1,0:T(8,128)(2,1)} %bitcast.24, bf16[256,1152]{1,0:T(8,128)(2,1)} %bitcast.25, bf16[256,1152]{1,0:T(8,128)(2,1)} %bitcast.26, bf16[256,1152]{1,0:T(8,128)(2,1)} %bitcast.27, bf16[36,1152]{1,0:T(8,128)(2,1)} %bitcast.28), custom_call_target="tpu_custom_call" | custom-call | bytes 6177792 | tf_op jit(solution)/shard_map/pack/pallas_call | solution.py:343
  4.6 0.0 copy-start
  4.7 7.4 %all-to-all-start = ((bf16[32,8,7296]{2,1,0:T(8,128)(2,1)}), bf16[32,8,7296]{2,1,0:T(8,128)(2,1)}, u32[]{:S(2)}, u32[]{:S(2)}) async-start(bf16[32,8,7296]{2,1,0:T(8,128)(2,1)} %bitcast.21), calls=%async_computation | async-start | bytes 7471104 | tf_op jit(solution)/shard_map/all_to_all | solution.py:445
  12.1 0.0 copy-done
  12.1 2.7 %tables.1 = (bf16[1152,1152]{1,0:T(8,128)(2,1)}, f32[256,256]{1,0:T(8,128)S(1)}) custom-call(s32[1]{0:T(128)} %bitcast.core_ref, s32[1,4]{1,0:T(1,128)S(1)} %copy-done), custom_call_target="tpu_custom_call" | custom-call | bytes 2916372 | tf_op jit(solution)/shard_map/tables/pallas_call | solution.py:343
  14.8 44.7 %all-to-all-done = bf16[32,8,7296]{2,1,0:T(8,128)(2,1)} async-done(((bf16[32,8,7296]{2,1,0:T(8,128)(2,1)}), bf16[32,8,7296]{2,1,0:T(8,128)(2,1)}, u32[]{:S(2)}, u32[]{:S(2)}) %all-to-all-start) | async-done | bytes 3735584 | tf_op jit(solution)/shard_map/all_to_all | solution.py:445
  59.5 6.6 %forward.1 = (bf16[256,1152]{1,0:T(8,128)(2,1)S(1)}, bf16[16,40,1152]{2,1,0:T(8,128)(2,1)S(1)}, bf16[16,40,1152]{2,1,0:T(8,128)(2,1)}, bf16[256,2688]{1,0:T(8,128)(2,1)}) custom-call(s32[1]{0:T(128)} %bitcast.core_ref, bf16[256,7296]{1,0:T(8,128)(2,1)} %bitcast.7.x_hbm, f32[256,256]{1,0:T(8,128)S(1)} %get-tuple-element.12.bias_ref), custom_call_target="tpu_custom_call" | custom-call | flops 1753219072 | bytes 8912900 | tf_op jit(solution)/shard_map/forward/pallas_call | solution.py:343
  66.1 1.9 %collective-permute-start.1 = (bf16[16,40,1152]{2,1,0:T(8,128)(2,1)}, bf16[16,40,1152]{2,1,0:T(8,128)(2,1)S(1)}, u32[]{:S(2)}, u32[]{:S(2)}) collective-permute-start(bf16[16,40,1152]{2,1,0:T(8,128)(2,1)} %get-tuple-element.16), channel_id=1, source_target_pairs={{0,1},{1,0},{2,3},{3,2},{4,5},{5,4},{6,7},{7,6},{8,9},{9,8},{10,11... | collective-permute-start | bytes 4423688 | tf_op jit(solution)/shard_map/ppermute | solution.py:448
  68.1 3.4 %collective-permute-done.1.theirs_ref = bf16[16,40,1152]{2,1,0:T(8,128)(2,1)S(1)} collective-permute-done((bf16[16,40,1152]{2,1,0:T(8,128)(2,1)}, bf16[16,40,1152]{2,1,0:T(8,128)(2,1)S(1)}, u32[]{:S(2)}, u32[]{:S(2)}) %collective-permute-start.1) | collective-permute-done | bytes 1474592 | tf_op jit(solution)/shard_map/ppermute | solution.py:448
  71.5 1.5 %join.1 = bf16[2,16,40,640]{3,2,1,0:T(8,128)(2,1)} custom-call(bf16[16,40,1152]{2,1,0:T(8,128)(2,1)S(1)} %get-tuple-element.15.keep_ref, bf16[16,40,1152]{2,1,0:T(8,128)(2,1)S(1)} %collective-permute-done.1.theirs_ref), custom_call_target="tpu_custom_call" | custom-call | bytes 4587520 | tf_op jit(solution)/shard_map/join/pallas_call | solution.py:343
  73.0 7.4 %all-to-all-start.2 = ((bf16[32,40,640]{2,1,0:T(8,128)(2,1)}), bf16[32,40,640]{2,1,0:T(8,128)(2,1)S(1)}, u32[]{:S(2)}, u32[]{:S(2)}) async-start(bf16[32,40,640]{2,1,0:T(8,128)(2,1)} %bitcast.14), calls=%async_computation.2 | async-start | bytes 3276800 | tf_op jit(solution)/shard_map/all_to_all | solution.py:460
  80.4 2.1 %collective-permute-start = (bf16[256,2688]{1,0:T(8,128)(2,1)}, bf16[256,2688]{1,0:T(8,128)(2,1)S(1)}, u32[]{:S(2)}, u32[]{:S(2)}) collective-permute-start(bf16[256,2688]{1,0:T(8,128)(2,1)} %get-tuple-element.13.own_hbm), channel_id=1, source_target_pairs={{0,1},{1,0},{2,3},{3,2},{4,5},{5,4},{6,7},{7,6},{8,9},{9,8},{10,11... | collective-permute-start | bytes 4128776 | tf_op jit(solution)/shard_map/ppermute | solution.py:448
  82.5 3.1 %collective-permute-done.other_ref = bf16[256,2688]{1,0:T(8,128)(2,1)S(1)} collective-permute-done((bf16[256,2688]{1,0:T(8,128)(2,1)}, bf16[256,2688]{1,0:T(8,128)(2,1)S(1)}, u32[]{:S(2)}, u32[]{:S(2)}) %collective-permute-start) | collective-permute-done | bytes 1376288 | tf_op jit(solution)/shard_map/ppermute | solution.py:448
  85.7 13.9 %backward.1 = bf16[256,4608]{1,0:T(8,128)(2,1)} custom-call(bf16[1152,1152]{1,0:T(8,128)(2,1)} %get-tuple-element.11.pick_hbm, bf16[256,7296]{1,0:T(8,128)(2,1)} %bitcast.7.x_hbm, bf16[256,2688]{1,0:T(8,128)(2,1)} %get-tuple-element.13.own_hbm, bf16[256,2688]{1,0:T(8,128)(2,1)S(1)} %collective-permute-done.other_ref, ...), custom_call_target="tpu_custom_call" | custom-call | flops 5939134464 | bytes 12353536 | tf_op jit(solution)/shard_map/backward/pallas_call | solution.py:343
  99.5 3.2 %all-to-all-done.2.parts_hbm = bf16[32,40,640]{2,1,0:T(8,128)(2,1)S(1)} async-done(((bf16[32,40,640]{2,1,0:T(8,128)(2,1)}), bf16[32,40,640]{2,1,0:T(8,128)(2,1)S(1)}, u32[]{:S(2)}, u32[]{:S(2)}) %all-to-all-start.2) | async-done | bytes 1638432 | tf_op jit(solution)/shard_map/all_to_all | solution.py:460
  102.7 0.0 copy-start.1
  102.7 1.2 copy-done.1
  103.9 4.5 %all-to-all-start.1 = ((bf16[32,8,4608]{2,1,0:T(8,128)(2,1)}), bf16[32,8,4608]{2,1,0:T(8,128)(2,1)S(1)}, u32[]{:S(2)}, u32[]{:S(2)}) async-start(bf16[32,8,4608]{2,1,0:T(8,128)(2,1)} %bitcast.23), calls=%async_computation.1 | async-start | bytes 4718592 | tf_op jit(solution)/shard_map/all_to_all | solution.py:445
  108.5 1.5 total.1
  109.9 1.9 %collective-permute-start.2 = (bf16[40,640]{1,0:T(8,128)(2,1)S(1)}, bf16[40,640]{1,0:T(8,128)(2,1)S(1)}, u32[]{:S(2)}, u32[]{:S(2)}) collective-permute-start(bf16[40,640]{1,0:T(8,128)(2,1)S(1)} %total.1), channel_id=1, source_target_pairs={{0,64},{32,96},{64,0},{96,32},{128,192},{160,224},{192,128},{224,1... | collective-permute-start | bytes 153608 | tf_op jit(solution)/shard_map/ppermute | solution.py:422
  111.9 5.9 %collective-permute-done.2 = bf16[40,640]{1,0:T(8,128)(2,1)S(1)} collective-permute-done((bf16[40,640]{1,0:T(8,128)(2,1)S(1)}, bf16[40,640]{1,0:T(8,128)(2,1)S(1)}, u32[]{:S(2)}, u32[]{:S(2)}) %collective-permute-start.2) | collective-permute-done | bytes 51232 | tf_op jit(solution)/shard_map/ppermute | solution.py:422
  117.8 1.9 %collective-permute-start.3 = (bf16[40,640]{1,0:T(8,128)(2,1)S(1)}, bf16[40,640]{1,0:T(8,128)(2,1)S(1)}, u32[]{:S(2)}, u32[]{:S(2)}) collective-permute-start(bf16[40,640]{1,0:T(8,128)(2,1)S(1)} %add_convert_fusion.2), channel_id=1, source_target_pairs={{0,128},{32,160},{64,192},{96,224},{128,0},{160,32},{192,64},{224,... | collective-permute-start | bytes 153608 | tf_op jit(solution)/shard_map/ppermute | solution.py:422
  119.7 9.5 %collective-permute-done.3 = bf16[40,640]{1,0:T(8,128)(2,1)S(1)} collective-permute-done((bf16[40,640]{1,0:T(8,128)(2,1)S(1)}, bf16[40,640]{1,0:T(8,128)(2,1)S(1)}, u32[]{:S(2)}, u32[]{:S(2)}) %collective-permute-start.3) | collective-permute-done | bytes 51232 | tf_op jit(solution)/shard_map/ppermute | solution.py:422
  129.2 8.5 %collective-permute-start.4 = (bf16[40,640]{1,0:T(8,128)(2,1)S(1)}, bf16[40,640]{1,0:T(8,128)(2,1)S(1)}, u32[]{:S(2)}, u32[]{:S(2)}) collective-permute-start(bf16[40,640]{1,0:T(8,128)(2,1)S(1)} %add_convert_fusion.1), channel_id=1, source_target_pairs={{0,448},{32,416},{64,384},{96,352},{128,320},{160,288},{192,256},{... | collective-permute-start | bytes 153608 | tf_op jit(solution)/shard_map/ppermute | solution.py:422
  137.8 7.2 %collective-permute-done.4 = bf16[40,640]{1,0:T(8,128)(2,1)S(1)} collective-permute-done((bf16[40,640]{1,0:T(8,128)(2,1)S(1)}, bf16[40,640]{1,0:T(8,128)(2,1)S(1)}, u32[]{:S(2)}, u32[]{:S(2)}) %collective-permute-start.4) | collective-permute-done | bytes 51232 | tf_op jit(solution)/shard_map/ppermute | solution.py:422
  145.0 1.9 %collective-permute-start.5 = (bf16[40,640]{1,0:T(8,128)(2,1)S(1)}, bf16[40,640]{1,0:T(8,128)(2,1)S(1)}, u32[]{:S(2)}, u32[]{:S(2)}) collective-permute-start(bf16[40,640]{1,0:T(8,128)(2,1)S(1)} %add_convert_fusion), channel_id=1, source_target_pairs={{0,32},{32,0},{64,96},{96,64},{128,160},{160,128},{192,224},{224,1... | collective-permute-start | bytes 153608 | tf_op jit(solution)/shard_map/ppermute | solution.py:422
  146.9 0.0 all-to-all-done.1
  146.9 1.4 slice_bitcast_fusion
  148.4 2.6 %collective-permute-done.5 = bf16[40,640]{1,0:T(8,128)(2,1)S(1)} collective-permute-done((bf16[40,640]{1,0:T(8,128)(2,1)S(1)}, bf16[40,640]{1,0:T(8,128)(2,1)S(1)}, u32[]{:S(2)}, u32[]{:S(2)}) %collective-permute-start.5) | collective-permute-done | bytes 51232 | tf_op jit(solution)/shard_map/ppermute | solution.py:422
  151.0 0.7 fusion
  (6 shorter events, 0.1 us)
Async XLA Ops:
  4.6 7.5 %copy-start = (s32[1,4]{1,0:T(1,128)S(1)}, s32[1,4]{1,0:T(1,128)}, u32[]{:S(2)}) copy-start(s32[1,4]{1,0:T(1,128)} %lens_ref.1) | copy-start | bytes 52
  4.7 54.8 %all-to-all-start = ((bf16[32,8,7296]{2,1,0:T(8,128)(2,1)}), bf16[32,8,7296]{2,1,0:T(8,128)(2,1)}, u32[]{:S(2)}, u32[]{:S(2)}) async-start(bf16[32,8,7296]{2,1,0:T(8,128)(2,1)} %bitcast.21), calls=%async_computation | async-start | bytes 7471104 | tf_op jit(solution)/shard_map/all_to_all | solution.py:445
  66.1 5.4 %collective-permute-start.1 = (bf16[16,40,1152]{2,1,0:T(8,128)(2,1)}, bf16[16,40,1152]{2,1,0:T(8,128)(2,1)S(1)}, u32[]{:S(2)}, u32[]{:S(2)}) collective-permute-start(bf16[16,40,1152]{2,1,0:T(8,128)(2,1)} %get-tuple-element.16), channel_id=1, source_target_pairs={{0,1},{1,0},{2,3},{3,2},{4,5},{5,4},{6,7},{7,6},{8,9},{9,8},{10,11... | collective-permute-start | bytes 4423688 | tf_op jit(solution)/shard_map/ppermute | solution.py:448
  73.0 29.7 %all-to-all-start.2 = ((bf16[32,40,640]{2,1,0:T(8,128)(2,1)}), bf16[32,40,640]{2,1,0:T(8,128)(2,1)S(1)}, u32[]{:S(2)}, u32[]{:S(2)}) async-start(bf16[32,40,640]{2,1,0:T(8,128)(2,1)} %bitcast.14), calls=%async_computation.2 | async-start | bytes 3276800 | tf_op jit(solution)/shard_map/all_to_all | solution.py:460
  80.4 5.2 %collective-permute-start = (bf16[256,2688]{1,0:T(8,128)(2,1)}, bf16[256,2688]{1,0:T(8,128)(2,1)S(1)}, u32[]{:S(2)}, u32[]{:S(2)}) collective-permute-start(bf16[256,2688]{1,0:T(8,128)(2,1)} %get-tuple-element.13.own_hbm), channel_id=1, source_target_pairs={{0,1},{1,0},{2,3},{3,2},{4,5},{5,4},{6,7},{7,6},{8,9},{9,8},{10,11... | collective-permute-start | bytes 4128776 | tf_op jit(solution)/shard_map/ppermute | solution.py:448
  102.7 1.2 copy-start.1
  103.9 43.0 %all-to-all-start.1 = ((bf16[32,8,4608]{2,1,0:T(8,128)(2,1)}), bf16[32,8,4608]{2,1,0:T(8,128)(2,1)S(1)}, u32[]{:S(2)}, u32[]{:S(2)}) async-start(bf16[32,8,4608]{2,1,0:T(8,128)(2,1)} %bitcast.23), calls=%async_computation.1 | async-start | bytes 4718592 | tf_op jit(solution)/shard_map/all_to_all | solution.py:445
  109.9 7.9 %collective-permute-start.2 = (bf16[40,640]{1,0:T(8,128)(2,1)S(1)}, bf16[40,640]{1,0:T(8,128)(2,1)S(1)}, u32[]{:S(2)}, u32[]{:S(2)}) collective-permute-start(bf16[40,640]{1,0:T(8,128)(2,1)S(1)} %total.1), channel_id=1, source_target_pairs={{0,64},{32,96},{64,0},{96,32},{128,192},{160,224},{192,128},{224,1... | collective-permute-start | bytes 153608 | tf_op jit(solution)/shard_map/ppermute | solution.py:422
  117.8 11.4 %collective-permute-start.3 = (bf16[40,640]{1,0:T(8,128)(2,1)S(1)}, bf16[40,640]{1,0:T(8,128)(2,1)S(1)}, u32[]{:S(2)}, u32[]{:S(2)}) collective-permute-start(bf16[40,640]{1,0:T(8,128)(2,1)S(1)} %add_convert_fusion.2), channel_id=1, source_target_pairs={{0,128},{32,160},{64,192},{96,224},{128,0},{160,32},{192,64},{224,... | collective-permute-start | bytes 153608 | tf_op jit(solution)/shard_map/ppermute | solution.py:422
  129.2 15.7 %collective-permute-start.4 = (bf16[40,640]{1,0:T(8,128)(2,1)S(1)}, bf16[40,640]{1,0:T(8,128)(2,1)S(1)}, u32[]{:S(2)}, u32[]{:S(2)}) collective-permute-start(bf16[40,640]{1,0:T(8,128)(2,1)S(1)} %add_convert_fusion.1), channel_id=1, source_target_pairs={{0,448},{32,416},{64,384},{96,352},{128,320},{160,288},{192,256},{... | collective-permute-start | bytes 153608 | tf_op jit(solution)/shard_map/ppermute | solution.py:422
  145.0 6.0 %collective-permute-start.5 = (bf16[40,640]{1,0:T(8,128)(2,1)S(1)}, bf16[40,640]{1,0:T(8,128)(2,1)S(1)}, u32[]{:S(2)}, u32[]{:S(2)}) collective-permute-start(bf16[40,640]{1,0:T(8,128)(2,1)S(1)} %add_convert_fusion), channel_id=1, source_target_pairs={{0,32},{32,0},{64,96},{96,64},{128,160},{160,128},{192,224},{224,1... | collective-permute-start | bytes 153608 | tf_op jit(solution)/shard_map/ppermute | solution.py:422

commit v4 on v3

--- a/solution.py
+++ b/solution.py
@@ -79,6 +79,8 @@
             self.ref[:, lanes] = self.held.pop(tile).astype(self.ref.dtype)
 
 
+FWD_FLOPS = 10**11
+JOIN_FLOPS = 10**9
 GROUP = 8
 FULL = 16
 ODD = 2
@@ -98,12 +100,9 @@
 
 
 def pack_kernel(*refs):
-    *parts, weight_hbm, x_ref, staged_ref, weight_ref, held_ref, sems, weight_sems = refs
+    *parts, x_ref, staged_ref, sems = refs
     rows, width = parts[0].shape
-    shard = weight_ref.shape[0]
     half = rows // 2
-    fetch_weight = pltpu.make_async_copy(weight_hbm, weight_ref, weight_sems.at[0])
-    fetch_weight.start()
     fetches, copies = [], []
     for i, part in enumerate(parts):
         for j in range(2):
@@ -112,6 +111,17 @@
             copies.append(pltpu.make_async_copy(staged_ref.at[i, at], x_ref.at[at, lanes], sems.at[1, n]))
     for fetch in fetches:
         fetch.start()
+    for fetch, copy in zip(fetches, copies):
+        fetch.wait()
+        copy.start()
+    for copy in copies:
+        copy.wait()
+
+
+def spread_kernel(weight_ref, out_ref, held_ref, sem):
+    shard, width = weight_ref.shape
+    rows = held_ref.shape[0]
+    weight = weight_ref[...]
 
     def core(row):
         return jnp.bitwise_and(lax.div(row, jnp.int32(GROUP)), 1)
@@ -119,14 +129,9 @@
     def place(row):
         return jnp.bitwise_and(row, GROUP - 1)
 
-    fetch_weight.wait()
-    weight = weight_ref[...]
     for block in range(FULL // GROUP):
         pick = selection(rows, shard, lambda row: FULL * core(row) + GROUP * block + place(row))
         held_ref[:, pl.ds(block * width, width)] = dot(pick, weight).astype(BF16)
-    for fetch, copy in list(zip(fetches, copies))[:4]:
-        fetch.wait()
-        copy.start()
     odd = jnp.zeros((rows, ODD_LANES), F32)
     for q in range(CHUNK):
 
@@ -137,14 +142,9 @@
 
         odd = odd + dot(selection(rows, shard, wanted), chunk_tiles(weight_ref, q))
     held_ref[:, pl.ds(FULL // GROUP * width, ODD_LANES)] = odd.astype(BF16)
-    lanes = pl.ds(len(parts) * width, held_ref.shape[1])
-    last = pltpu.make_async_copy(held_ref, x_ref.at[:, lanes], weight_sems.at[1])
-    last.start()
-    for fetch, copy in list(zip(fetches, copies))[4:]:
-        fetch.wait()
-        copy.start()
-    for copy in (*copies, last):
-        copy.wait()
+    copy = pltpu.make_async_copy(held_ref, out_ref, sem.at[0])
+    copy.start()
+    copy.wait()
 
 
 def pick_rows(ref, place):
@@ -175,7 +175,7 @@
 
 
 def forward_kernel(
-    core_ref, x_hbm, bias_ref, mixed_ref, keep_ref, send_ref, rest_ref, x_ref, left_ref, part_ref, held_ref, sems
+    core_ref, x_hbm, bias_ref, mixed_ref, keep_ref, first_ref, second_ref, x_ref, part_ref, held_ref, sems
 ):
     rows, width = mixed_ref.shape
     middle = lane_half(width)
@@ -185,8 +185,6 @@
         pltpu.make_async_copy(x_hbm.at[:, pl.ds(at, size)], x_ref.at[:, pl.ds(at, size)], sems.at[5 + i])
         for i, (at, size) in enumerate(pieces)
     ]
-    left = pl.ds(4 * width, left_ref.shape[1])
-    fetches.append(pltpu.make_async_copy(x_hbm.at[:, left], left_ref, sems.at[5 + len(pieces)]))
     for fetch in fetches:
         fetch.start()
     bias = bias_ref[...]
@@ -202,9 +200,7 @@
         value_win = jnp.where(lanes, x_ref[:, pl.ds(2 * width + start, size)], 0)
         raised, recip = softmax(query_win, key_win, bias)
         mixed_tiles.add(head, dot((raised * recip).astype(BF16), value_win))
-    fetches[7].wait()
-    copies = [pltpu.make_async_copy(left_ref, rest_ref, sems.at[4])]
-    copies[0].start()
+    copies = []
     fetches[6].wait()
     mixed = mixed_ref[...]
     block = 3 * LANES
@@ -218,8 +214,9 @@
         for j in range(step * some, (step + 1) * some):
             at = pl.multiple_of(j * (width // chips) + other, 8)
             held_ref[j] = part_ref[pl.ds(at, pitch), :].astype(BF16)
-        ids = pl.ds(step * some, some)
-        copies.append(pltpu.make_async_copy(held_ref.at[ids], send_ref.at[ids], sems.at[step]))
+        source, place = pl.ds(step * some, some), pl.ds(step % 2 * some, some)
+        send_ref = first_ref if step < 2 else second_ref
+        copies.append(pltpu.make_async_copy(held_ref.at[source], send_ref.at[place], sems.at[step]))
         copies[-1].start()
     for j in range(chips):
         at = pl.multiple_of(j * (width // chips) + own, 8)
@@ -228,11 +225,14 @@
         copy.wait()
 
 
-def join_kernel(keep_ref, theirs_ref, out_ref):
+def join_kernel(keep_ref, first_ref, second_ref, out_ref):
     size = out_ref.shape[3]
-    total = (keep_ref[...].astype(F32) + theirs_ref[...].astype(F32)).astype(BF16)
-    out_ref[0] = total[:, :, :size]
-    out_ref[1] = total[:, :, total.shape[2] - size :]
+    half = first_ref.shape[0]
+    for at, ref in ((0, first_ref), (half, second_ref)):
+        rows = pl.ds(at, half)
+        total = (keep_ref[rows].astype(F32) + ref[...].astype(F32)).astype(BF16)
+        out_ref[0, rows] = total[:, :, :size]
+        out_ref[1, rows] = total[:, :, total.shape[2] - size :]
 
 
 def backward_kernel(
@@ -347,7 +347,7 @@
         out_specs=[pl.BlockSpec(memory_space=pltpu.HBM if i in hbm_out else pltpu.VMEM) for i in range(len(outs))],
         scratch_shapes=scratch,
         compiler_params=pltpu.CompilerParams(vmem_limit_bytes=VMEM_LIMIT),
-        cost_estimate=pl.CostEstimate(flops=flops, bytes_accessed=moved, transcendentals=0),
+        cost_estimate=pl.CostEstimate(flops=flops, bytes_accessed=0 if flops else moved, transcendentals=0),
         name=name,
     )(*args)
 
@@ -356,20 +356,18 @@
     return pltpu.SemaphoreType.DMA((count,))
 
 
-def pack(arrays, weight_t):
+def pack(arrays):
     rows, width = arrays[0].shape
     count = len(arrays)
-    extra = FULL // GROUP * width + ODD_LANES
-    outs = [((rows, count * width + extra), BF16)]
-    scratch = [
-        pltpu.VMEM((count, rows, width), BF16),
-        pltpu.VMEM(weight_t.shape, BF16),
-        pltpu.VMEM((rows, extra), BF16),
-        pltpu.SemaphoreType.DMA((2, 2 * count)),
-        dma(2),
-    ]
-    args = (*arrays, weight_t)
-    return call(pack_kernel, "pack", outs, args, hbm_in=count + 1, hbm_out=(0,), scratch=scratch)[0]
+    outs = [((rows, count * width), BF16)]
+    scratch = [pltpu.VMEM((count, rows, width), BF16), pltpu.SemaphoreType.DMA((2, 2 * count))]
+    return call(pack_kernel, "pack", outs, arrays, hbm_in=count, hbm_out=(0,), scratch=scratch)[0]
+
+
+def spread(weight_t, rows):
+    shape = (rows, FULL // GROUP * weight_t.shape[1] + ODD_LANES)
+    scratch = [pltpu.VMEM(shape, BF16), dma(1)]
+    return call(spread_kernel, "spread", [(shape, BF16)], (weight_t,), hbm_out=(0,), scratch=scratch)[0]
 
 
 def tables(core, lengths, rows, width, shard, positions):
@@ -380,22 +378,21 @@
 
 
 def forward(core, x, bias, width, chips):
-    rows, wide = x.shape
+    rows = x.shape[0]
     pitch = -(-width // chips // 2 // 8) * 8
-    part, rest = (chips, pitch, width), (rows, wide - 4 * width)
-    outs = [((rows, width), BF16), (part, BF16), (part, BF16), (rest, BF16)]
-    flops = 2 * width * rows * width + 4 * HEADS * rows * rows * 256
-    scratch = [pltpu.VMEM((rows, 4 * width), BF16), pltpu.VMEM(rest, BF16), pltpu.VMEM((width, width), F32)]
-    scratch += [pltpu.VMEM(part, BF16), dma(13)]
+    part, half = (chips, pitch, width), (chips // 2, pitch, width)
+    outs = [((rows, width), BF16), (part, BF16), (half, BF16), (half, BF16)]
+    scratch = [pltpu.VMEM(x.shape, BF16), pltpu.VMEM((width, width), F32), pltpu.VMEM(part, BF16), dma(12)]
     args = (core, x, bias)
     return call(
-        forward_kernel, "forward", outs, args, smem=1, hbm_in=1, hbm_out=(2, 3), scratch=scratch, flops=flops
+        forward_kernel, "forward", outs, args, smem=1, hbm_in=1, hbm_out=(2, 3), scratch=scratch, flops=FWD_FLOPS
     )
 
 
-def join(keep, theirs):
+def join(keep, first, second):
     chips, pitch, width = keep.shape
-    return call(join_kernel, "join", [((2, chips, pitch, lane_half(width)), BF16)], (keep, theirs))[0]
+    outs = [((2, chips, pitch, lane_half(width)), BF16)]
+    return call(join_kernel, "join", outs, (keep, first, second), flops=JOIN_FLOPS)[0]
 
 
 def backward(pick, x, own, other, bias, mixed):
@@ -422,7 +419,7 @@
         return lax.ppermute(block, "dp", [(i, other(i)) for i in range(n_dp)])
 
     def mirrored(i):
-        return i ^ (n_dp // 2) if (i + 1) % (n_dp // 2) == 0 else n_dp - 2 - i
+        return n_dp - i - (2 if i % 2 == 0 else 0)
 
     hop = 2
     while hop < n_dp:
@@ -448,11 +445,13 @@
         return lax.ppermute(block, "seq", [(i, i ^ 1) for i in range(n_seq)])
 
     arrays = [a.reshape(patches, width) for a in (queries, key_vectors, value_vectors, out_grad)]
-    x = swap(pack(arrays, out_weight.T)).reshape(patches, -1)
+    x = swap(pack(arrays)).reshape(patches, -1)
+    rows, x = lax.optimization_barrier((spread(out_weight.T, patches), x))
+    own = swap(rows).reshape(patches, -1)
     pick, bias = tables(core.reshape(1), clip_frames, patches, width, shard, positions)
-    mixed, keep, send, own = forward(core.reshape(1), x, bias, width, n_seq // 2)
-
-    chip = join(keep, partner(send))
+    mixed, keep, *send = forward(core.reshape(1), x, bias, width, n_seq // 2)
+
+    chip = join(keep, *[partner(block) for block in send])
     chip = chip.reshape(n_seq, *chip.shape[2:])
     pairs = [
         [(p + d) * n_seq + i for d in (0, 1) for i in range(c, n_seq, 2)] for p in range(0, n_dp, 2) for c in (0, 1)
@@ -460,8 +459,9 @@
     parts = lax.all_to_all(chip, ("dp", "seq"), 0, 0, tiled=True, axis_index_groups=pairs)
 
     y = backward(pick, x, own, partner(own), bias, mixed)
+    total, y = lax.optimization_barrier((total_of(parts), y))
     back = swap(y).reshape(patches, 4 * width)
-    total = sum_over_pairs(total_of(parts), n_dp, width)
+    total = sum_over_pairs(total, n_dp, width)
     weight_grad = jnp.where(core == 0, total[:shard], total[total.shape[0] - shard :]).T
     outs = [back[:, i * width : (i + 1) * width].reshape(queries.shape) for i in range(4)]
     return (*outs, weight_grad)

time: 152 us -> 145 us (0.954)
  the two profiles are of different devices: /device:TPU:224 before, /device:TPU:6 now
where the time goes in v4:
time: 145 us; the launch traced here: 144 us
  starting transfers between devices  59.3 us (41%)
  waiting for transfers between devices  50.7 us (35%)
  Pallas kernels  30.6 us (21%)
  local copies, waits for them, and re-layouts  1.46 us (1%)
    pallas_call x7, Pallas kernels, call(): pl.pallas_call(kernel, out_shape=[pltpu.HBM(s.shape, s.dtype) if i in hbm...  30.6 us
    all_to_all x3, waiting for transfers between devices, swap(): lax.all_to_all(block.reshape(n_seq, positions, -1), 'seq', 0, 0, tiled=True)  28.7 us
    ppermute x4, starting transfers between devices, exchange(): return lax.ppermute(block, 'dp', [(i, other(i)) for i in range(n_dp)])  23.3 us
    all_to_all x3, starting transfers between devices, swap(): lax.all_to_all(block.reshape(n_seq, positions, -1), 'seq', 0, 0, tiled=True)  23 us
    ppermute x4, waiting for transfers between devices, exchange(): return lax.ppermute(block, 'dp', [(i, other(i)) for i in range(n_dp)])  13.6 us
    all_to_all x1, starting transfers between devices, on_device(): lax.all_to_all(chip, ('dp', 'seq'), 0, 0, tiled=True, axis_index_groups=p...  6.61 us
    ppermute x3, starting transfers between devices, partner(): return lax.ppermute(block, 'seq', [(i, i ^ 1) for i in range(n_seq)])  6.43 us
    ppermute x3, waiting for transfers between devices, partner(): return lax.ppermute(block, 'seq', [(i, i ^ 1) for i in range(n_seq)])  5.16 us
  transfers between devices with their start and end apart: 11, of which 9 were waited for; matrix products, arithmetic and copies ran while one was open for 1% of the time, Pallas kernels for 18%

profile of v4, /device:TPU:6, one launch (start us, length us, event | category | flops | bytes accessed | tf_op | source)
XLA Modules:
  0.0 143.8 jit_solution(4308974752402332508)
XLA Ops:
  0.6 2.6 %pack.1 = bf16[256,4608]{1,0:T(8,128)(2,1)} custom-call(bf16[256,1152]{1,0:T(8,128)(2,1)} %bitcast.30, bf16[256,1152]{1,0:T(8,128)(2,1)} %bitcast.31, bf16[256,1152]{1,0:T(8,128)(2,1)} %bitcast.32, bf16[256,1152]{1,0:T(8,128)(2,1)} %bitcast.33), custom_call_target="tpu_custom_call" | custom-call | bytes 4718592 | tf_op jit(solution)/shard_map/pack/pallas_call | solution.py:343
  3.3 0.0 copy-start
  3.3 0.0 copy-start.1
  3.3 9.9 %all-to-all-start = ((bf16[32,8,4608]{2,1,0:T(8,128)(2,1)}), bf16[32,8,4608]{2,1,0:T(8,128)(2,1)S(1)}, u32[]{:S(2)}, u32[]{:S(2)}) async-start(bf16[32,8,4608]{2,1,0:T(8,128)(2,1)} %bitcast.25), calls=%async_computation | async-start | bytes 4718592 | tf_op jit(solution)/shard_map/all_to_all | solution.py:442
  13.2 1.8 %spread.1 = bf16[256,2688]{1,0:T(8,128)(2,1)} custom-call(bf16[36,1152]{1,0:T(8,128)(2,1)S(1)} %bitcast.23), custom_call_target="tpu_custom_call" | custom-call | bytes 1459200 | tf_op jit(solution)/shard_map/spread/pallas_call | solution.py:343
  15.0 2.6 %tables.1 = (bf16[1152,1152]{1,0:T(8,128)(2,1)}, f32[256,256]{1,0:T(8,128)S(1)}) custom-call(s32[1]{0:T(128)} %bitcast.core_ref, s32[1,4]{1,0:T(1,128)S(1)} %copy-done.1), custom_call_target="tpu_custom_call" | custom-call | bytes 2916372 | tf_op jit(solution)/shard_map/tables/pallas_call | solution.py:343
  17.6 24.6 %all-to-all-done = bf16[32,8,4608]{2,1,0:T(8,128)(2,1)S(1)} async-done(((bf16[32,8,4608]{2,1,0:T(8,128)(2,1)}), bf16[32,8,4608]{2,1,0:T(8,128)(2,1)S(1)}, u32[]{:S(2)}, u32[]{:S(2)}) %all-to-all-start) | async-done | bytes 2359328 | tf_op jit(solution)/shard_map/all_to_all | solution.py:442
  42.2 7.3 %all-to-all-start.2 = ((bf16[32,8,2688]{2,1,0:T(8,128)(2,1)}), bf16[32,8,2688]{2,1,0:T(8,128)(2,1)}, u32[]{:S(2)}, u32[]{:S(2)}) async-start(bf16[32,8,2688]{2,1,0:T(8,128)(2,1)} %bitcast.26), calls=%async_computation.2 | async-start | bytes 2752512 | tf_op jit(solution)/shard_map/all_to_all | solution.py:442
  49.6 6.7 %forward.1 = (bf16[256,1152]{1,0:T(8,128)(2,1)S(1)}, bf16[16,40,1152]{2,1,0:T(8,128)(2,1)S(1)}, bf16[8,40,1152]{2,1,0:T(8,128)(2,1)}, bf16[8,40,1152]{2,1,0:T(8,128)(2,1)}) custom-call(s32[1]{0:T(128)} %bitcast.core_ref, bf16[256,4608]{1,0:T(8,128)(2,1)} %bitcast.28, f32[256,256]{1,0:T(8,128)S(1)} %get-tuple-element.16.bias_ref), custom_call_target="tpu_custom_call" | custom-call | flops 99999997952 | tf_op jit(solution)/shard_map/forward/pallas_call | solution.py:343
  56.2 2.1 %collective-permute-start = (bf16[8,40,1152]{2,1,0:T(8,128)(2,1)}, bf16[8,40,1152]{2,1,0:T(8,128)(2,1)S(1)}, u32[]{:S(2)}, u32[]{:S(2)}) collective-permute-start(bf16[8,40,1152]{2,1,0:T(8,128)(2,1)} %get-tuple-element.18), channel_id=1, source_target_pairs={{0,1},{1,0},{2,3},{3,2},{4,5},{5,4},{6,7},{7,6},{8,9},{9,8},{10,11... | collective-permute-start | bytes 2211848 | tf_op jit(solution)/shard_map/ppermute | solution.py:445
  58.3 2.3 %collective-permute-start.1 = (bf16[8,40,1152]{2,1,0:T(8,128)(2,1)}, bf16[8,40,1152]{2,1,0:T(8,128)(2,1)S(1)}, u32[]{:S(2)}, u32[]{:S(2)}) collective-permute-start(bf16[8,40,1152]{2,1,0:T(8,128)(2,1)} %get-tuple-element.19), channel_id=1, source_target_pairs={{0,1},{1,0},{2,3},{3,2},{4,5},{5,4},{6,7},{7,6},{8,9},{9,8},{10,11... | collective-permute-start | bytes 2211848 | tf_op jit(solution)/shard_map/ppermute | solution.py:445
  60.6 0.0 collective-permute-done.first_ref
  60.6 2.0 %collective-permute-done.1.second_ref = bf16[8,40,1152]{2,1,0:T(8,128)(2,1)S(1)} collective-permute-done((bf16[8,40,1152]{2,1,0:T(8,128)(2,1)}, bf16[8,40,1152]{2,1,0:T(8,128)(2,1)S(1)}, u32[]{:S(2)}, u32[]{:S(2)}) %collective-permute-start.1) | collective-permute-done | bytes 737312 | tf_op jit(solution)/shard_map/ppermute | solution.py:445
  62.6 1.6 %join.1 = bf16[2,16,40,640]{3,2,1,0:T(8,128)(2,1)} custom-call(bf16[16,40,1152]{2,1,0:T(8,128)(2,1)S(1)} %get-tuple-element.17.keep_ref, bf16[8,40,1152]{2,1,0:T(8,128)(2,1)S(1)} %collective-permute-done.first_ref, bf16[8,40,1152]{2,1,0:T(8,128)(2,1)S(1)} %collective-permute-done.1.second_ref), custom_call_target="tpu_custom_call" | custom-call | flops 1000000000 | tf_op jit(solution)/shard_map/join/pallas_call | solution.py:343
  64.2 4.1 %all-to-all-done.2 = bf16[32,8,2688]{2,1,0:T(8,128)(2,1)} async-done(((bf16[32,8,2688]{2,1,0:T(8,128)(2,1)}), bf16[32,8,2688]{2,1,0:T(8,128)(2,1)}, u32[]{:S(2)}, u32[]{:S(2)}) %all-to-all-start.2) | async-done | bytes 1376288 | tf_op jit(solution)/shard_map/all_to_all | solution.py:442
  68.3 6.6 %all-to-all-start.1 = ((bf16[32,40,640]{2,1,0:T(8,128)(2,1)}), bf16[32,40,640]{2,1,0:T(8,128)(2,1)}, u32[]{:S(2)}, u32[]{:S(2)}) async-start(bf16[32,40,640]{2,1,0:T(8,128)(2,1)} %bitcast.8), calls=%async_computation.1 | async-start | bytes 3276800 | tf_op jit(solution)/shard_map/all_to_all | solution.py:459
  74.9 2.1 %collective-permute-start.2 = (bf16[256,2688]{1,0:T(8,128)(2,1)}, bf16[256,2688]{1,0:T(8,128)(2,1)S(1)}, u32[]{:S(2)}, u32[]{:S(2)}) collective-permute-start(bf16[256,2688]{1,0:T(8,128)(2,1)} %bitcast.10.own_hbm), channel_id=1, source_target_pairs={{0,1},{1,0},{2,3},{3,2},{4,5},{5,4},{6,7},{7,6},{8,9},{9,8},{10,11... | collective-permute-start | bytes 4128776 | tf_op jit(solution)/shard_map/ppermute | solution.py:445
  77.0 3.1 %collective-permute-done.2.other_ref = bf16[256,2688]{1,0:T(8,128)(2,1)S(1)} collective-permute-done((bf16[256,2688]{1,0:T(8,128)(2,1)}, bf16[256,2688]{1,0:T(8,128)(2,1)S(1)}, u32[]{:S(2)}, u32[]{:S(2)}) %collective-permute-start.2) | collective-permute-done | bytes 1376288 | tf_op jit(solution)/shard_map/ppermute | solution.py:445
  80.1 13.9 %backward.1 = bf16[256,4608]{1,0:T(8,128)(2,1)} custom-call(bf16[1152,1152]{1,0:T(8,128)(2,1)} %get-tuple-element.20.pick_hbm, bf16[256,4608]{1,0:T(8,128)(2,1)} %bitcast.29, bf16[256,2688]{1,0:T(8,128)(2,1)} %bitcast.10.own_hbm, bf16[256,2688]{1,0:T(8,128)(2,1)S(1)} %collective-permute-done.2.other_ref, f32[256,256]{1,0:T(8,128)S(1)} %get-tuple-element.16.bias_ref, ...), custom_call_target="tpu_custom_call" | custom-call | flops 5939134464 | tf_op jit(solution)/shard_map/backward/pallas_call | solution.py:343
  94.0 3.2 %all-to-all-done.1.parts_hbm = bf16[32,40,640]{2,1,0:T(8,128)(2,1)} async-done(((bf16[32,40,640]{2,1,0:T(8,128)(2,1)}), bf16[32,40,640]{2,1,0:T(8,128)(2,1)}, u32[]{:S(2)}, u32[]{:S(2)}) %all-to-all-start.1) | async-done | bytes 1638432 | tf_op jit(solution)/shard_map/all_to_all | solution.py:459
  97.3 1.5 %total.1 = bf16[40,640]{1,0:T(8,128)(2,1)S(1)} custom-call(bf16[32,40,640]{2,1,0:T(8,128)(2,1)} %all-to-all-done.1.parts_hbm), custom_call_target="tpu_custom_call" | custom-call | bytes 1689600 | tf_op jit(solution)/shard_map/total/pallas_call | solution.py:343
  98.7 5.8 %all-to-all-start.3 = ((bf16[32,8,4608]{2,1,0:T(8,128)(2,1)}), bf16[32,8,4608]{2,1,0:T(8,128)(2,1)S(1)}, u32[]{:S(2)}, u32[]{:S(2)}) async-start(bf16[32,8,4608]{2,1,0:T(8,128)(2,1)} %bitcast.27), calls=%async_computation.3 | async-start | bytes 4718592 | tf_op jit(solution)/shard_map/all_to_all | solution.py:442
  104.5 2.5 %collective-permute-start.3 = (bf16[40,640]{1,0:T(8,128)(2,1)S(1)}, bf16[40,640]{1,0:T(8,128)(2,1)S(1)}, u32[]{:S(2)}, u32[]{:S(2)}) collective-permute-start(bf16[40,640]{1,0:T(8,128)(2,1)S(1)} %total.1), channel_id=1, source_target_pairs={{0,64},{32,96},{64,0},{96,32},{128,192},{160,224},{192,128},{224,1... | collective-permute-start | bytes 153608 | tf_op jit(solution)/shard_map/ppermute | solution.py:419
  107.0 5.2 %collective-permute-done.3 = bf16[40,640]{1,0:T(8,128)(2,1)S(1)} collective-permute-done((bf16[40,640]{1,0:T(8,128)(2,1)S(1)}, bf16[40,640]{1,0:T(8,128)(2,1)S(1)}, u32[]{:S(2)}, u32[]{:S(2)}) %collective-permute-start.3) | collective-permute-done | bytes 51232 | tf_op jit(solution)/shard_map/ppermute | solution.py:419
  112.3 7.1 %collective-permute-start.4 = (bf16[40,640]{1,0:T(8,128)(2,1)S(1)}, bf16[40,640]{1,0:T(8,128)(2,1)S(1)}, u32[]{:S(2)}, u32[]{:S(2)}) collective-permute-start(bf16[40,640]{1,0:T(8,128)(2,1)S(1)} %add_convert_fusion.2), channel_id=1, source_target_pairs={{0,128},{32,160},{64,192},{96,224},{128,0},{160,32},{192,64},{224,... | collective-permute-start | bytes 153608 | tf_op jit(solution)/shard_map/ppermute | solution.py:419
  119.3 4.2 %collective-permute-done.4 = bf16[40,640]{1,0:T(8,128)(2,1)S(1)} collective-permute-done((bf16[40,640]{1,0:T(8,128)(2,1)S(1)}, bf16[40,640]{1,0:T(8,128)(2,1)S(1)}, u32[]{:S(2)}, u32[]{:S(2)}) %collective-permute-start.4) | collective-permute-done | bytes 51232 | tf_op jit(solution)/shard_map/ppermute | solution.py:419
  123.5 7.7 %collective-permute-start.5 = (bf16[40,640]{1,0:T(8,128)(2,1)S(1)}, bf16[40,640]{1,0:T(8,128)(2,1)S(1)}, u32[]{:S(2)}, u32[]{:S(2)}) collective-permute-start(bf16[40,640]{1,0:T(8,128)(2,1)S(1)} %add_convert_fusion.1), channel_id=1, source_target_pairs={{0,448},{32,480},{64,384},{96,416},{128,320},{160,352},{192,256},{... | collective-permute-start | bytes 153608 | tf_op jit(solution)/shard_map/ppermute | solution.py:419
  131.2 2.2 %collective-permute-done.5 = bf16[40,640]{1,0:T(8,128)(2,1)S(1)} collective-permute-done((bf16[40,640]{1,0:T(8,128)(2,1)S(1)}, bf16[40,640]{1,0:T(8,128)(2,1)S(1)}, u32[]{:S(2)}, u32[]{:S(2)}) %collective-permute-start.5) | collective-permute-done | bytes 51232 | tf_op jit(solution)/shard_map/ppermute | solution.py:419
  133.4 6.0 %collective-permute-start.6 = (bf16[40,640]{1,0:T(8,128)(2,1)S(1)}, bf16[40,640]{1,0:T(8,128)(2,1)S(1)}, u32[]{:S(2)}, u32[]{:S(2)}) collective-permute-start(bf16[40,640]{1,0:T(8,128)(2,1)S(1)} %add_convert_fusion), channel_id=1, source_target_pairs={{0,32},{32,0},{64,96},{96,64},{128,160},{160,128},{192,224},{224,1... | collective-permute-start | bytes 153608 | tf_op jit(solution)/shard_map/ppermute | solution.py:419
  139.5 2.1 %collective-permute-done.6 = bf16[40,640]{1,0:T(8,128)(2,1)S(1)} collective-permute-done((bf16[40,640]{1,0:T(8,128)(2,1)S(1)}, bf16[40,640]{1,0:T(8,128)(2,1)S(1)}, u32[]{:S(2)}, u32[]{:S(2)}) %collective-permute-start.6) | collective-permute-done | bytes 51232 | tf_op jit(solution)/shard_map/ppermute | solution.py:419
  141.6 0.7 fusion
  142.3 1.4 %slice_bitcast_fusion = (bf16[1,1,256,1152]{3,2,1,0:T(8,128)(2,1)}, bf16[1,1,256,1152]{3,2,1,0:T(8,128)(2,1)}, bf16[1,1,256,1152]{3,2,1,0:T(8,128)(2,1)}, bf16[1,1,256,1152]{3,2,1,0:T(8,128)(2,1)}) fusion(bf16[256,4608]{1,0:T(8,128)(2,1)S(1)} %bitcast.24), kind=kLoop, calls=%fused_computation | loop fusion | bytes 4718592 | tf_op jit(solution)/shard_map/reshape | solution.py:466
  (11 shorter events, 0.1 us)
Async XLA Ops:
  3.3 9.9 %copy-start = (bf16[1152,36]{0,1:T(8,128)(2,1)S(1)}, bf16[1152,36]{0,1:T(8,128)(2,1)}, u32[]{:S(2)}) copy-start(bf16[1152,36]{0,1:T(8,128)(2,1)} %param.10) | copy-start | bytes 248836
  3.3 11.7 %copy-start.1 = (s32[1,4]{1,0:T(1,128)S(1)}, s32[1,4]{1,0:T(1,128)}, u32[]{:S(2)}) copy-start(s32[1,4]{1,0:T(1,128)} %lens_ref.1) | copy-start | bytes 52
  3.3 38.9 %all-to-all-start = ((bf16[32,8,4608]{2,1,0:T(8,128)(2,1)}), bf16[32,8,4608]{2,1,0:T(8,128)(2,1)S(1)}, u32[]{:S(2)}, u32[]{:S(2)}) async-start(bf16[32,8,4608]{2,1,0:T(8,128)(2,1)} %bitcast.25), calls=%async_computation | async-start | bytes 4718592 | tf_op jit(solution)/shard_map/all_to_all | solution.py:442
  42.2 7.4 %copy-start.2 = (bf16[32,8,4608]{2,1,0:T(8,128)(2,1)}, bf16[32,8,4608]{2,1,0:T(8,128)(2,1)S(1)}, u32[]{:S(2)}) copy-start(bf16[32,8,4608]{2,1,0:T(8,128)(2,1)S(1)} %all-to-all-done) | copy-start | bytes 7077892
  42.2 26.1 %all-to-all-start.2 = ((bf16[32,8,2688]{2,1,0:T(8,128)(2,1)}), bf16[32,8,2688]{2,1,0:T(8,128)(2,1)}, u32[]{:S(2)}, u32[]{:S(2)}) async-start(bf16[32,8,2688]{2,1,0:T(8,128)(2,1)} %bitcast.26), calls=%async_computation.2 | async-start | bytes 2752512 | tf_op jit(solution)/shard_map/all_to_all | solution.py:442
  56.2 4.3 %collective-permute-start = (bf16[8,40,1152]{2,1,0:T(8,128)(2,1)}, bf16[8,40,1152]{2,1,0:T(8,128)(2,1)S(1)}, u32[]{:S(2)}, u32[]{:S(2)}) collective-permute-start(bf16[8,40,1152]{2,1,0:T(8,128)(2,1)} %get-tuple-element.18), channel_id=1, source_target_pairs={{0,1},{1,0},{2,3},{3,2},{4,5},{5,4},{6,7},{7,6},{8,9},{9,8},{10,11... | collective-permute-start | bytes 2211848 | tf_op jit(solution)/shard_map/ppermute | solution.py:445
  58.3 4.3 %collective-permute-start.1 = (bf16[8,40,1152]{2,1,0:T(8,128)(2,1)}, bf16[8,40,1152]{2,1,0:T(8,128)(2,1)S(1)}, u32[]{:S(2)}, u32[]{:S(2)}) collective-permute-start(bf16[8,40,1152]{2,1,0:T(8,128)(2,1)} %get-tuple-element.19), channel_id=1, source_target_pairs={{0,1},{1,0},{2,3},{3,2},{4,5},{5,4},{6,7},{7,6},{8,9},{9,8},{10,11... | collective-permute-start | bytes 2211848 | tf_op jit(solution)/shard_map/ppermute | solution.py:445
  68.3 29.0 %all-to-all-start.1 = ((bf16[32,40,640]{2,1,0:T(8,128)(2,1)}), bf16[32,40,640]{2,1,0:T(8,128)(2,1)}, u32[]{:S(2)}, u32[]{:S(2)}) async-start(bf16[32,40,640]{2,1,0:T(8,128)(2,1)} %bitcast.8), calls=%async_computation.1 | async-start | bytes 3276800 | tf_op jit(solution)/shard_map/all_to_all | solution.py:459
  74.9 5.2 %collective-permute-start.2 = (bf16[256,2688]{1,0:T(8,128)(2,1)}, bf16[256,2688]{1,0:T(8,128)(2,1)S(1)}, u32[]{:S(2)}, u32[]{:S(2)}) collective-permute-start(bf16[256,2688]{1,0:T(8,128)(2,1)} %bitcast.10.own_hbm), channel_id=1, source_target_pairs={{0,1},{1,0},{2,3},{3,2},{4,5},{5,4},{6,7},{7,6},{8,9},{9,8},{10,11... | collective-permute-start | bytes 4128776 | tf_op jit(solution)/shard_map/ppermute | solution.py:445
  98.7 43.6 %all-to-all-start.3 = ((bf16[32,8,4608]{2,1,0:T(8,128)(2,1)}), bf16[32,8,4608]{2,1,0:T(8,128)(2,1)S(1)}, u32[]{:S(2)}, u32[]{:S(2)}) async-start(bf16[32,8,4608]{2,1,0:T(8,128)(2,1)} %bitcast.27), calls=%async_computation.3 | async-start | bytes 4718592 | tf_op jit(solution)/shard_map/all_to_all | solution.py:442
  104.5 7.7 %collective-permute-start.3 = (bf16[40,640]{1,0:T(8,128)(2,1)S(1)}, bf16[40,640]{1,0:T(8,128)(2,1)S(1)}, u32[]{:S(2)}, u32[]{:S(2)}) collective-permute-start(bf16[40,640]{1,0:T(8,128)(2,1)S(1)} %total.1), channel_id=1, source_target_pairs={{0,64},{32,96},{64,0},{96,32},{128,192},{160,224},{192,128},{224,1... | collective-permute-start | bytes 153608 | tf_op jit(solution)/shard_map/ppermute | solution.py:419
  112.3 11.3 %collective-permute-start.4 = (bf16[40,640]{1,0:T(8,128)(2,1)S(1)}, bf16[40,640]{1,0:T(8,128)(2,1)S(1)}, u32[]{:S(2)}, u32[]{:S(2)}) collective-permute-start(bf16[40,640]{1,0:T(8,128)(2,1)S(1)} %add_convert_fusion.2), channel_id=1, source_target_pairs={{0,128},{32,160},{64,192},{96,224},{128,0},{160,32},{192,64},{224,... | collective-permute-start | bytes 153608 | tf_op jit(solution)/shard_map/ppermute | solution.py:419
  123.5 9.9 %collective-permute-start.5 = (bf16[40,640]{1,0:T(8,128)(2,1)S(1)}, bf16[40,640]{1,0:T(8,128)(2,1)S(1)}, u32[]{:S(2)}, u32[]{:S(2)}) collective-permute-start(bf16[40,640]{1,0:T(8,128)(2,1)S(1)} %add_convert_fusion.1), channel_id=1, source_target_pairs={{0,448},{32,480},{64,384},{96,416},{128,320},{160,352},{192,256},{... | collective-permute-start | bytes 153608 | tf_op jit(solution)/shard_map/ppermute | solution.py:419
  133.4 8.1 %collective-permute-start.6 = (bf16[40,640]{1,0:T(8,128)(2,1)S(1)}, bf16[40,640]{1,0:T(8,128)(2,1)S(1)}, u32[]{:S(2)}, u32[]{:S(2)}) collective-permute-start(bf16[40,640]{1,0:T(8,128)(2,1)S(1)} %add_convert_fusion), channel_id=1, source_target_pairs={{0,32},{32,0},{64,96},{96,64},{128,160},{160,128},{192,224},{224,1... | collective-permute-start | bytes 153608 | tf_op jit(solution)/shard_map/ppermute | solution.py:419

commit v5 on v4

--- a/solution.py
+++ b/solution.py
@@ -226,13 +226,33 @@
 
 
 def join_kernel(keep_ref, first_ref, second_ref, out_ref):
-    size = out_ref.shape[3]
+    width = keep_ref.shape[2]
+    size = lane_half(width)
     half = first_ref.shape[0]
     for at, ref in ((0, first_ref), (half, second_ref)):
-        rows = pl.ds(at, half)
-        total = (keep_ref[rows].astype(F32) + ref[...].astype(F32)).astype(BF16)
-        out_ref[0, rows] = total[:, :, :size]
-        out_ref[1, rows] = total[:, :, total.shape[2] - size :]
+        ids = pl.ds(at, half)
+        total = keep_ref[ids].astype(F32) + ref[...].astype(F32)
+        groups = [total[:, i * 8 : i * 8 + 8, :].astype(BF16) for i in range(5)]
+        for d, whole, rest in ((0, (0, 1), groups[2][:, :, :size]), (1, (3, 4), groups[2][:, :, width - size :])):
+            for i, group in enumerate(whole):
+                out_ref[d, ids, :, pl.ds(i * width, width)] = groups[group]
+            out_ref[d, ids, :, pl.ds(2 * width, size)] = rest
+
+
+def finish_kernel(place_ref, mine_ref, far_ref, near_other_ref, far_other_ref, out_ref, held_ref):
+    shard, width = out_ref.shape
+    size = lane_half(width)
+    mine = mine_ref[...].astype(F32) + far_ref[...].astype(F32)
+    other = near_other_ref[...].astype(F32) + far_other_ref[...].astype(F32)
+    low = place_ref[0] == 0
+    lower, upper = jnp.where(low, mine, other), jnp.where(low, other, mine)
+    for half, groups in ((lower, (0, 1)), (upper, (3, 4))):
+        for i, group in enumerate(groups):
+            held_ref[pl.ds(group * 8, 8), :] = half[:, i * width : (i + 1) * width]
+    held_ref[pl.ds(16, 8), pl.ds(0, size)] = lower[:, 2 * width :]
+    held_ref[pl.ds(16, 8), pl.ds(size, width - size)] = upper[:, 2 * width + 2 * size - width :]
+    rows = held_ref.shape[0]
+    out_ref[...] = jnp.where(place_ref[1] == 0, held_ref[pl.ds(0, shard), :], held_ref[pl.ds(rows - shard, shard), :])
 
 
 def backward_kernel(
@@ -391,7 +411,7 @@
 
 def join(keep, first, second):
     chips, pitch, width = keep.shape
-    outs = [((2, chips, pitch, lane_half(width)), BF16)]
+    outs = [((2, chips, 8, 2 * width + lane_half(width)), BF16)]
     return call(join_kernel, "join", outs, (keep, first, second), flops=JOIN_FLOPS)[0]
 
 
@@ -414,22 +434,27 @@
     return (width // LANES + 1) // 2 * LANES
 
 
-def sum_over_pairs(block, n_dp, width):
-    def exchange(block, other):
-        return lax.ppermute(block, "dp", [(i, other(i)) for i in range(n_dp)])
-
-    def mirrored(i):
-        return n_dp - i - (2 if i % 2 == 0 else 0)
-
-    hop = 2
-    while hop < n_dp:
-        theirs = exchange(block, mirrored if hop == n_dp // 2 else lambda i: i ^ hop)
-        block = (block.astype(F32) + theirs.astype(F32)).astype(BF16)
-        hop *= 2
-    theirs = exchange(block, lambda i: i ^ 1)
-    low = jnp.bitwise_and(lax.axis_index("dp"), 1) == 0
-    lower, upper = jnp.where(low, block, theirs), jnp.where(low, theirs, block)
-    return jnp.concatenate([lower, upper[:, 2 * lower.shape[1] - width :]], axis=1).astype(F32)
+def sum_over_pairs(block, place, shard, width, n_dp):
+    half, quarter = n_dp // 2, n_dp // 4
+
+    def exchange(block, source):
+        return lax.ppermute(block, "dp", [(source(i) % n_dp, i) for i in range(n_dp)])
+
+    def added(block, source):
+        return (block.astype(F32) + exchange(block, source).astype(F32)).astype(BF16)
+
+    def second(i):
+        return i ^ quarter if i % 2 == 0 else i + quarter * (1 if i // quarter % 2 else -1)
+
+    def third(i):
+        return n_dp - 2 - i if i % 2 == 0 else half - i
+
+    block = added(added(block, lambda i: i ^ 2), second)
+    far, near_other = exchange(block, third), exchange(block, lambda i: i ^ 1)
+    far_other = exchange(block, lambda i: third(i ^ 1))
+    args = (place, block, far, near_other, far_other)
+    scratch = [pltpu.VMEM((40, width), F32)]
+    return call(finish_kernel, "finish", [((shard, width), F32)], args, smem=1, scratch=scratch)[0]
 
 
 def on_device(n_seq, n_dp, queries, key_vectors, value_vectors, out_grad, out_weight, clip_frames):
@@ -461,8 +486,8 @@
     y = backward(pick, x, own, partner(own), bias, mixed)
     total, y = lax.optimization_barrier((total_of(parts), y))
     back = swap(y).reshape(patches, 4 * width)
-    total = sum_over_pairs(total, n_dp, width)
-    weight_grad = jnp.where(core == 0, total[:shard], total[total.shape[0] - shard :]).T
+    place = jnp.stack([jnp.bitwise_and(lax.axis_index("dp"), 1).astype(jnp.int32), core])
+    weight_grad = sum_over_pairs(total, place, shard, width, n_dp).T
     outs = [back[:, i * width : (i + 1) * width].reshape(queries.shape) for i in range(4)]
     return (*outs, weight_grad)
 

time: 145 us -> 150 us (1.034)
  starting transfers between devices: 59.3 us -> 62.7 us
  waiting for transfers between devices: 50.7 us -> 52.8 us
    ppermute x4 -> x5, waiting for transfers between devices: 13.6 us -> 17 us  [exchange(): lax.ppermute(block, 'dp', [(source(i) % n_dp, i) for i in range(n_dp)])]
    ppermute x4 -> x5, starting transfers between devices: 23.3 us -> 26.3 us  [exchange(): lax.ppermute(block, 'dp', [(source(i) % n_dp, i) for i in range(n_dp)])]
    pallas_call x7 -> x8, Pallas kernels: 30.6 us -> 31.7 us  [call(): pl.pallas_call(kernel, out_shape=[pltpu.HBM(s.shape, s.dtype) if i in hbm...]
  transfers between devices with their start and end apart: 11 -> 12, of which waited for: 9 -> 8; matrix products, arithmetic and copies ran while one was open for 1% -> 0% of each run, Pallas kernels for 18% -> 19%
where the time goes in v5:
time: 150 us
  starting transfers between devices  62.7 us (42%)
  waiting for transfers between devices  52.8 us (35%)
  Pallas kernels  31.7 us (21%)
    pallas_call x8, Pallas kernels, call(): pl.pallas_call(kernel, out_shape=[pltpu.HBM(s.shape, s.dtype) if i in hbm...  31.7 us
    all_to_all x3, waiting for transfers between devices, swap(): lax.all_to_all(block.reshape(n_seq, positions, -1), 'seq', 0, 0, tiled=True)  28.8 us
    ppermute x5, starting transfers between devices, exchange(): lax.ppermute(block, 'dp', [(source(i) % n_dp, i) for i in range(n_dp)])  26.3 us
    all_to_all x3, starting transfers between devices, swap(): lax.all_to_all(block.reshape(n_seq, positions, -1), 'seq', 0, 0, tiled=True)  23.4 us
    ppermute x5, waiting for transfers between devices, exchange(): lax.ppermute(block, 'dp', [(source(i) % n_dp, i) for i in range(n_dp)])  17 us
    all_to_all x1, starting transfers between devices, on_device(): lax.all_to_all(chip, ('dp', 'seq'), 0, 0, tiled=True, axis_index_groups=p...  6.59 us
    ppermute x3, starting transfers between devices, partner(): return lax.ppermute(block, 'seq', [(i, i ^ 1) for i in range(n_seq)])  6.43 us
    ppermute x3, waiting for transfers between devices, partner(): return lax.ppermute(block, 'seq', [(i, i ^ 1) for i in range(n_seq)])  5.16 us
  transfers between devices with their start and end apart: 12, of which 8 were waited for; matrix products, arithmetic and copies ran while one was open for 0% of the time, Pallas kernels for 19%

profile of v5, /device:TPU:6, one launch (start us, length us, event | category | flops | bytes accessed | tf_op | source)
XLA Modules:
  0.0 149.7 jit_solution(3400397269088250480)
XLA Ops:
  0.6 2.6 %pack.1 = bf16[256,4608]{1,0:T(8,128)(2,1)} custom-call(bf16[256,1152]{1,0:T(8,128)(2,1)} %bitcast.28, bf16[256,1152]{1,0:T(8,128)(2,1)} %bitcast.29, bf16[256,1152]{1,0:T(8,128)(2,1)} %bitcast.30, bf16[256,1152]{1,0:T(8,128)(2,1)} %bitcast.31), custom_call_target="tpu_custom_call" | custom-call | bytes 4718592 | tf_op jit(solution)/shard_map/pack/pallas_call | solution.py:363
  3.2 0.0 copy-start
  3.2 0.0 copy-start.1
  3.2 10.6 %all-to-all-start = ((bf16[32,8,4608]{2,1,0:T(8,128)(2,1)}), bf16[32,8,4608]{2,1,0:T(8,128)(2,1)}, u32[]{:S(2)}, u32[]{:S(2)}) async-start(bf16[32,8,4608]{2,1,0:T(8,128)(2,1)} %bitcast.25), calls=%async_computation | async-start | bytes 4718592 | tf_op jit(solution)/shard_map/all_to_all | solution.py:467
  13.8 1.8 %spread.1 = bf16[256,2688]{1,0:T(8,128)(2,1)} custom-call(bf16[36,1152]{1,0:T(8,128)(2,1)S(1)} %bitcast.23), custom_call_target="tpu_custom_call" | custom-call | bytes 1459200 | tf_op jit(solution)/shard_map/spread/pallas_call | solution.py:363
  15.6 2.6 %tables.1 = (bf16[1152,1152]{1,0:T(8,128)(2,1)}, f32[256,256]{1,0:T(8,128)S(1)}) custom-call(s32[1]{0:T(128)} %bitcast.core_ref, s32[1,4]{1,0:T(1,128)S(1)} %copy-done.1), custom_call_target="tpu_custom_call" | custom-call | bytes 2916372 | tf_op jit(solution)/shard_map/tables/pallas_call | solution.py:363
  18.2 24.7 %all-to-all-done = bf16[32,8,4608]{2,1,0:T(8,128)(2,1)} async-done(((bf16[32,8,4608]{2,1,0:T(8,128)(2,1)}), bf16[32,8,4608]{2,1,0:T(8,128)(2,1)}, u32[]{:S(2)}, u32[]{:S(2)}) %all-to-all-start) | async-done | bytes 2359328 | tf_op jit(solution)/shard_map/all_to_all | solution.py:467
  42.9 7.3 %all-to-all-start.2 = ((bf16[32,8,2688]{2,1,0:T(8,128)(2,1)}), bf16[32,8,2688]{2,1,0:T(8,128)(2,1)}, u32[]{:S(2)}, u32[]{:S(2)}) async-start(bf16[32,8,2688]{2,1,0:T(8,128)(2,1)} %bitcast.26), calls=%async_computation.2 | async-start | bytes 2752512 | tf_op jit(solution)/shard_map/all_to_all | solution.py:467
  50.3 6.7 %forward.1 = (bf16[256,1152]{1,0:T(8,128)(2,1)S(1)}, bf16[16,40,1152]{2,1,0:T(8,128)(2,1)S(1)}, bf16[8,40,1152]{2,1,0:T(8,128)(2,1)}, bf16[8,40,1152]{2,1,0:T(8,128)(2,1)}) custom-call(s32[1]{0:T(128)} %bitcast.core_ref, bf16[256,4608]{1,0:T(8,128)(2,1)} %bitcast.7.x_hbm, f32[256,256]{1,0:T(8,128)S(1)} %get-tuple-element.16.bias_ref), custom_call_target="tpu_custom_call" | custom-call | flops 99999997952 | tf_op jit(solution)/shard_map/forward/pallas_call | solution.py:363
  56.9 2.1 %collective-permute-start = (bf16[8,40,1152]{2,1,0:T(8,128)(2,1)}, bf16[8,40,1152]{2,1,0:T(8,128)(2,1)S(1)}, u32[]{:S(2)}, u32[]{:S(2)}) collective-permute-start(bf16[8,40,1152]{2,1,0:T(8,128)(2,1)} %get-tuple-element.18), channel_id=1, source_target_pairs={{0,1},{1,0},{2,3},{3,2},{4,5},{5,4},{6,7},{7,6},{8,9},{9,8},{10,11... | collective-permute-start | bytes 2211848 | tf_op jit(solution)/shard_map/ppermute | solution.py:470
  59.0 2.3 %collective-permute-start.1 = (bf16[8,40,1152]{2,1,0:T(8,128)(2,1)}, bf16[8,40,1152]{2,1,0:T(8,128)(2,1)S(1)}, u32[]{:S(2)}, u32[]{:S(2)}) collective-permute-start(bf16[8,40,1152]{2,1,0:T(8,128)(2,1)} %get-tuple-element.19), channel_id=1, source_target_pairs={{0,1},{1,0},{2,3},{3,2},{4,5},{5,4},{6,7},{7,6},{8,9},{9,8},{10,11... | collective-permute-start | bytes 2211848 | tf_op jit(solution)/shard_map/ppermute | solution.py:470
  61.3 2.0 %collective-permute-done.1.second_ref = bf16[8,40,1152]{2,1,0:T(8,128)(2,1)S(1)} collective-permute-done((bf16[8,40,1152]{2,1,0:T(8,128)(2,1)}, bf16[8,40,1152]{2,1,0:T(8,128)(2,1)S(1)}, u32[]{:S(2)}, u32[]{:S(2)}) %collective-permute-start.1) | collective-permute-done | bytes 737312 | tf_op jit(solution)/shard_map/ppermute | solution.py:470
  63.3 1.6 %join.1 = bf16[2,16,8,2944]{3,2,1,0:T(8,128)(2,1)} custom-call(bf16[16,40,1152]{2,1,0:T(8,128)(2,1)S(1)} %get-tuple-element.17.keep_ref, bf16[8,40,1152]{2,1,0:T(8,128)(2,1)S(1)} %collective-permute-done.first_ref, bf16[8,40,1152]{2,1,0:T(8,128)(2,1)S(1)} %collective-permute-done.1.second_ref), custom_call_target="tpu_custom_call" | custom-call | flops 1000000000 | tf_op jit(solution)/shard_map/join/pallas_call | solution.py:363
  64.9 4.1 %all-to-all-done.2 = bf16[32,8,2688]{2,1,0:T(8,128)(2,1)} async-done(((bf16[32,8,2688]{2,1,0:T(8,128)(2,1)}), bf16[32,8,2688]{2,1,0:T(8,128)(2,1)}, u32[]{:S(2)}, u32[]{:S(2)}) %all-to-all-start.2) | async-done | bytes 1376288 | tf_op jit(solution)/shard_map/all_to_all | solution.py:467
  69.0 6.6 %all-to-all-start.1 = ((bf16[32,8,2944]{2,1,0:T(8,128)(2,1)}), bf16[32,8,2944]{2,1,0:T(8,128)(2,1)}, u32[]{:S(2)}, u32[]{:S(2)}) async-start(bf16[32,8,2944]{2,1,0:T(8,128)(2,1)} %bitcast.8), calls=%async_computation.1 | async-start | bytes 3014656 | tf_op jit(solution)/shard_map/all_to_all | solution.py:484
  75.6 2.1 %collective-permute-start.2 = (bf16[256,2688]{1,0:T(8,128)(2,1)}, bf16[256,2688]{1,0:T(8,128)(2,1)S(1)}, u32[]{:S(2)}, u32[]{:S(2)}) collective-permute-start(bf16[256,2688]{1,0:T(8,128)(2,1)} %bitcast.10.own_hbm), channel_id=1, source_target_pairs={{0,1},{1,0},{2,3},{3,2},{4,5},{5,4},{6,7},{7,6},{8,9},{9,8},{10,11... | collective-permute-start | bytes 4128776 | tf_op jit(solution)/shard_map/ppermute | solution.py:470
  77.7 3.1 %collective-permute-done.2.other_ref = bf16[256,2688]{1,0:T(8,128)(2,1)S(1)} collective-permute-done((bf16[256,2688]{1,0:T(8,128)(2,1)}, bf16[256,2688]{1,0:T(8,128)(2,1)S(1)}, u32[]{:S(2)}, u32[]{:S(2)}) %collective-permute-start.2) | collective-permute-done | bytes 1376288 | tf_op jit(solution)/shard_map/ppermute | solution.py:470
  80.8 13.9 %backward.1 = bf16[256,4608]{1,0:T(8,128)(2,1)} custom-call(bf16[1152,1152]{1,0:T(8,128)(2,1)} %get-tuple-element.20.pick_hbm, bf16[256,4608]{1,0:T(8,128)(2,1)} %bitcast.7.x_hbm, bf16[256,2688]{1,0:T(8,128)(2,1)} %bitcast.10.own_hbm, bf16[256,2688]{1,0:T(8,128)(2,1)S(1)} %collective-permute-done.2.other_ref, f32[256,256]{1,0:T(8,128)S(1)} %get-tuple-element.16.bias_ref, ...), custom_call_target="tpu_custom_call" | custom-call | flops 5939134464 | tf_op jit(solution)/shard_map/backward/pallas_call | solution.py:363
  94.7 1.9 %all-to-all-done.1.parts_hbm = bf16[32,8,2944]{2,1,0:T(8,128)(2,1)} async-done(((bf16[32,8,2944]{2,1,0:T(8,128)(2,1)}), bf16[32,8,2944]{2,1,0:T(8,128)(2,1)}, u32[]{:S(2)}, u32[]{:S(2)}) %all-to-all-start.1) | async-done | bytes 1507360 | tf_op jit(solution)/shard_map/all_to_all | solution.py:484
  96.6 1.4 total.1
  98.0 5.5 %all-to-all-start.3 = ((bf16[32,8,4608]{2,1,0:T(8,128)(2,1)}), bf16[32,8,4608]{2,1,0:T(8,128)(2,1)S(1)}, u32[]{:S(2)}, u32[]{:S(2)}) async-start(bf16[32,8,4608]{2,1,0:T(8,128)(2,1)} %bitcast.27), calls=%async_computation.3 | async-start | bytes 4718592 | tf_op jit(solution)/shard_map/all_to_all | solution.py:467
  103.6 2.9 %collective-permute-start.3 = (bf16[8,2944]{1,0:T(8,128)(2,1)S(1)}, bf16[8,2944]{1,0:T(8,128)(2,1)S(1)}, u32[]{:S(2)}, u32[]{:S(2)}) collective-permute-start(bf16[8,2944]{1,0:T(8,128)(2,1)S(1)} %total.1), channel_id=1, source_target_pairs={{64,0},{96,32},{0,64},{32,96},{192,128},{224,160},{128,192},{160,2... | collective-permute-start | bytes 141320 | tf_op jit(solution)/shard_map/ppermute | solution.py:441
  106.5 4.4 %collective-permute-done.3 = bf16[8,2944]{1,0:T(8,128)(2,1)S(1)} collective-permute-done((bf16[8,2944]{1,0:T(8,128)(2,1)S(1)}, bf16[8,2944]{1,0:T(8,128)(2,1)S(1)}, u32[]{:S(2)}, u32[]{:S(2)}) %collective-permute-start.3) | collective-permute-done | bytes 47136 | tf_op jit(solution)/shard_map/ppermute | solution.py:441
  110.9 6.7 %collective-permute-start.4 = (bf16[8,2944]{1,0:T(8,128)(2,1)S(1)}, bf16[8,2944]{1,0:T(8,128)(2,1)S(1)}, u32[]{:S(2)}, u32[]{:S(2)}) collective-permute-start(bf16[8,2944]{1,0:T(8,128)(2,1)S(1)} %add_convert_fusion.1), channel_id=1, source_target_pairs={{128,0},{416,32},{192,64},{480,96},{0,128},{288,160},{64,192},{352... | collective-permute-start | bytes 141320 | tf_op jit(solution)/shard_map/ppermute | solution.py:441
  117.6 3.5 %collective-permute-done.4 = bf16[8,2944]{1,0:T(8,128)(2,1)S(1)} collective-permute-done((bf16[8,2944]{1,0:T(8,128)(2,1)S(1)}, bf16[8,2944]{1,0:T(8,128)(2,1)S(1)}, u32[]{:S(2)}, u32[]{:S(2)}) %collective-permute-start.4) | collective-permute-done | bytes 47136 | tf_op jit(solution)/shard_map/ppermute | solution.py:441
  121.1 8.3 %collective-permute-start.5 = (bf16[8,2944]{1,0:T(8,128)(2,1)S(1)}, bf16[8,2944]{1,0:T(8,128)(2,1)S(1)}, u32[]{:S(2)}, u32[]{:S(2)}) collective-permute-start(bf16[8,2944]{1,0:T(8,128)(2,1)S(1)} %add_convert_fusion.mine_ref), channel_id=1, source_target_pairs={{448,0},{224,32},{384,64},{160,96},{320,128},{96,160},{256,192},{3... | collective-permute-start | bytes 141320 | tf_op jit(solution)/shard_map/ppermute | solution.py:441
  129.5 5.0 %collective-permute-start.6 = (bf16[8,2944]{1,0:T(8,128)(2,1)S(1)}, bf16[8,2944]{1,0:T(8,128)(2,1)S(1)}, u32[]{:S(2)}, u32[]{:S(2)}) collective-permute-start(bf16[8,2944]{1,0:T(8,128)(2,1)S(1)} %add_convert_fusion.mine_ref), channel_id=1, source_target_pairs={{32,0},{0,32},{96,64},{64,96},{160,128},{128,160},{224,192},{192,2... | collective-permute-start | bytes 141320 | tf_op jit(solution)/shard_map/ppermute | solution.py:441
  134.4 3.4 %collective-permute-start.7 = (bf16[8,2944]{1,0:T(8,128)(2,1)S(1)}, bf16[8,2944]{1,0:T(8,128)(2,1)S(1)}, u32[]{:S(2)}, u32[]{:S(2)}) collective-permute-start(bf16[8,2944]{1,0:T(8,128)(2,1)S(1)} %add_convert_fusion.mine_ref), channel_id=1, source_target_pairs={{224,0},{448,32},{160,64},{384,96},{96,128},{320,160},{32,192},{25... | collective-permute-start | bytes 141320 | tf_op jit(solution)/shard_map/ppermute | solution.py:441
  137.8 0.1 pad_add_fusion.place_ref
  137.9 9.1 %collective-permute-done.7.far_other_ref = bf16[8,2944]{1,0:T(8,128)(2,1)S(1)} collective-permute-done((bf16[8,2944]{1,0:T(8,128)(2,1)S(1)}, bf16[8,2944]{1,0:T(8,128)(2,1)S(1)}, u32[]{:S(2)}, u32[]{:S(2)}) %collective-permute-start.7) | collective-permute-done | bytes 47136 | tf_op jit(solution)/shard_map/ppermute | solution.py:441
  147.0 1.3 finish.1
  148.3 1.4 slice_bitcast_fusion
  (8 shorter events, 0.0 us)
Async XLA Ops:
  3.2 10.6 %copy-start = (bf16[1152,36]{0,1:T(8,128)(2,1)S(1)}, bf16[1152,36]{0,1:T(8,128)(2,1)}, u32[]{:S(2)}) copy-start(bf16[1152,36]{0,1:T(8,128)(2,1)} %param.10) | copy-start | bytes 248836
  3.2 12.4 %copy-start.1 = (s32[1,4]{1,0:T(1,128)S(1)}, s32[1,4]{1,0:T(1,128)}, u32[]{:S(2)}) copy-start(s32[1,4]{1,0:T(1,128)} %lens_ref.1) | copy-start | bytes 52
  3.2 39.7 %all-to-all-start = ((bf16[32,8,4608]{2,1,0:T(8,128)(2,1)}), bf16[32,8,4608]{2,1,0:T(8,128)(2,1)}, u32[]{:S(2)}, u32[]{:S(2)}) async-start(bf16[32,8,4608]{2,1,0:T(8,128)(2,1)} %bitcast.25), calls=%async_computation | async-start | bytes 4718592 | tf_op jit(solution)/shard_map/all_to_all | solution.py:467
  42.9 26.1 %all-to-all-start.2 = ((bf16[32,8,2688]{2,1,0:T(8,128)(2,1)}), bf16[32,8,2688]{2,1,0:T(8,128)(2,1)}, u32[]{:S(2)}, u32[]{:S(2)}) async-start(bf16[32,8,2688]{2,1,0:T(8,128)(2,1)} %bitcast.26), calls=%async_computation.2 | async-start | bytes 2752512 | tf_op jit(solution)/shard_map/all_to_all | solution.py:467
  56.9 4.3 %collective-permute-start = (bf16[8,40,1152]{2,1,0:T(8,128)(2,1)}, bf16[8,40,1152]{2,1,0:T(8,128)(2,1)S(1)}, u32[]{:S(2)}, u32[]{:S(2)}) collective-permute-start(bf16[8,40,1152]{2,1,0:T(8,128)(2,1)} %get-tuple-element.18), channel_id=1, source_target_pairs={{0,1},{1,0},{2,3},{3,2},{4,5},{5,4},{6,7},{7,6},{8,9},{9,8},{10,11... | collective-permute-start | bytes 2211848 | tf_op jit(solution)/shard_map/ppermute | solution.py:470
  59.0 4.3 %collective-permute-start.1 = (bf16[8,40,1152]{2,1,0:T(8,128)(2,1)}, bf16[8,40,1152]{2,1,0:T(8,128)(2,1)S(1)}, u32[]{:S(2)}, u32[]{:S(2)}) collective-permute-start(bf16[8,40,1152]{2,1,0:T(8,128)(2,1)} %get-tuple-element.19), channel_id=1, source_target_pairs={{0,1},{1,0},{2,3},{3,2},{4,5},{5,4},{6,7},{7,6},{8,9},{9,8},{10,11... | collective-permute-start | bytes 2211848 | tf_op jit(solution)/shard_map/ppermute | solution.py:470
  69.0 27.6 %all-to-all-start.1 = ((bf16[32,8,2944]{2,1,0:T(8,128)(2,1)}), bf16[32,8,2944]{2,1,0:T(8,128)(2,1)}, u32[]{:S(2)}, u32[]{:S(2)}) async-start(bf16[32,8,2944]{2,1,0:T(8,128)(2,1)} %bitcast.8), calls=%async_computation.1 | async-start | bytes 3014656 | tf_op jit(solution)/shard_map/all_to_all | solution.py:484
  75.6 5.2 %collective-permute-start.2 = (bf16[256,2688]{1,0:T(8,128)(2,1)}, bf16[256,2688]{1,0:T(8,128)(2,1)S(1)}, u32[]{:S(2)}, u32[]{:S(2)}) collective-permute-start(bf16[256,2688]{1,0:T(8,128)(2,1)} %bitcast.10.own_hbm), channel_id=1, source_target_pairs={{0,1},{1,0},{2,3},{3,2},{4,5},{5,4},{6,7},{7,6},{8,9},{9,8},{10,11... | collective-permute-start | bytes 4128776 | tf_op jit(solution)/shard_map/ppermute | solution.py:470
  98.0 50.3 %all-to-all-start.3 = ((bf16[32,8,4608]{2,1,0:T(8,128)(2,1)}), bf16[32,8,4608]{2,1,0:T(8,128)(2,1)S(1)}, u32[]{:S(2)}, u32[]{:S(2)}) async-start(bf16[32,8,4608]{2,1,0:T(8,128)(2,1)} %bitcast.27), calls=%async_computation.3 | async-start | bytes 4718592 | tf_op jit(solution)/shard_map/all_to_all | solution.py:467
  103.6 7.4 %collective-permute-start.3 = (bf16[8,2944]{1,0:T(8,128)(2,1)S(1)}, bf16[8,2944]{1,0:T(8,128)(2,1)S(1)}, u32[]{:S(2)}, u32[]{:S(2)}) collective-permute-start(bf16[8,2944]{1,0:T(8,128)(2,1)S(1)} %total.1), channel_id=1, source_target_pairs={{64,0},{96,32},{0,64},{32,96},{192,128},{224,160},{128,192},{160,2... | collective-permute-start | bytes 141320 | tf_op jit(solution)/shard_map/ppermute | solution.py:441
  110.9 10.2 %collective-permute-start.4 = (bf16[8,2944]{1,0:T(8,128)(2,1)S(1)}, bf16[8,2944]{1,0:T(8,128)(2,1)S(1)}, u32[]{:S(2)}, u32[]{:S(2)}) collective-permute-start(bf16[8,2944]{1,0:T(8,128)(2,1)S(1)} %add_convert_fusion.1), channel_id=1, source_target_pairs={{128,0},{416,32},{192,64},{480,96},{0,128},{288,160},{64,192},{352... | collective-permute-start | bytes 141320 | tf_op jit(solution)/shard_map/ppermute | solution.py:441
  121.1 16.8 %collective-permute-start.5 = (bf16[8,2944]{1,0:T(8,128)(2,1)S(1)}, bf16[8,2944]{1,0:T(8,128)(2,1)S(1)}, u32[]{:S(2)}, u32[]{:S(2)}) collective-permute-start(bf16[8,2944]{1,0:T(8,128)(2,1)S(1)} %add_convert_fusion.mine_ref), channel_id=1, source_target_pairs={{448,0},{224,32},{384,64},{160,96},{320,128},{96,160},{256,192},{3... | collective-permute-start | bytes 141320 | tf_op jit(solution)/shard_map/ppermute | solution.py:441
  129.5 8.5 %collective-permute-start.6 = (bf16[8,2944]{1,0:T(8,128)(2,1)S(1)}, bf16[8,2944]{1,0:T(8,128)(2,1)S(1)}, u32[]{:S(2)}, u32[]{:S(2)}) collective-permute-start(bf16[8,2944]{1,0:T(8,128)(2,1)S(1)} %add_convert_fusion.mine_ref), channel_id=1, source_target_pairs={{32,0},{0,32},{96,64},{64,96},{160,128},{128,160},{224,192},{192,2... | collective-permute-start | bytes 141320 | tf_op jit(solution)/shard_map/ppermute | solution.py:441
  134.4 12.6 %collective-permute-start.7 = (bf16[8,2944]{1,0:T(8,128)(2,1)S(1)}, bf16[8,2944]{1,0:T(8,128)(2,1)S(1)}, u32[]{:S(2)}, u32[]{:S(2)}) collective-permute-start(bf16[8,2944]{1,0:T(8,128)(2,1)S(1)} %add_convert_fusion.mine_ref), channel_id=1, source_target_pairs={{224,0},{448,32},{160,64},{384,96},{96,128},{320,160},{32,192},{25... | collective-permute-start | bytes 141320 | tf_op jit(solution)/shard_map/ppermute | solution.py:441

commit v6 on v5

--- a/solution.py
+++ b/solution.py
@@ -81,6 +81,7 @@
 
 FWD_FLOPS = 10**11
 JOIN_FLOPS = 10**9
+FINISH_FLOPS = 3 * 10**9
 GROUP = 8
 FULL = 16
 ODD = 2
@@ -239,11 +240,10 @@
             out_ref[d, ids, :, pl.ds(2 * width, size)] = rest
 
 
-def finish_kernel(place_ref, mine_ref, far_ref, near_other_ref, far_other_ref, out_ref, held_ref):
+def finish_kernel(place_ref, mine_ref, other_ref, out_ref, held_ref):
     shard, width = out_ref.shape
     size = lane_half(width)
-    mine = mine_ref[...].astype(F32) + far_ref[...].astype(F32)
-    other = near_other_ref[...].astype(F32) + far_other_ref[...].astype(F32)
+    mine, other = mine_ref[...].astype(F32), other_ref[...].astype(F32)
     low = place_ref[0] == 0
     lower, upper = jnp.where(low, mine, other), jnp.where(low, other, mine)
     for half, groups in ((lower, (0, 1)), (upper, (3, 4))):
@@ -338,20 +338,10 @@
         copy.wait()
 
 
-def total_kernel(parts_hbm, out_ref, parts_ref, sems):
-    count = parts_hbm.shape[0]
-    step = count // 4
-    fetches = [
-        pltpu.make_async_copy(parts_hbm.at[pl.ds(i * step, step)], parts_ref.at[pl.ds(i * step, step)], sems.at[i])
-        for i in range(4)
-    ]
-    for fetch in fetches:
-        fetch.start()
-    total = jnp.zeros(out_ref.shape, F32)
-    for i, fetch in enumerate(fetches):
-        fetch.wait()
-        for j in range(i * step, (i + 1) * step):
-            total = total + parts_ref[j].astype(F32)
+def total_kernel(parts_ref, out_ref):
+    total = parts_ref[0].astype(F32)
+    for j in range(1, parts_ref.shape[0]):
+        total = total + parts_ref[j].astype(F32)
     out_ref[...] = total.astype(BF16)
 
 
@@ -426,8 +416,7 @@
 
 
 def total_of(parts):
-    scratch = [pltpu.VMEM(parts.shape, BF16), dma(4)]
-    return call(total_kernel, "total", [(parts.shape[1:], BF16)], (parts,), hbm_in=1, scratch=scratch)[0]
+    return call(total_kernel, "total", [(parts.shape[1:], BF16)], (parts,))[0]
 
 
 def lane_half(width):
@@ -449,12 +438,10 @@
     def third(i):
         return n_dp - 2 - i if i % 2 == 0 else half - i
 
-    block = added(added(block, lambda i: i ^ 2), second)
-    far, near_other = exchange(block, third), exchange(block, lambda i: i ^ 1)
-    far_other = exchange(block, lambda i: third(i ^ 1))
-    args = (place, block, far, near_other, far_other)
+    block = added(added(added(block, lambda i: i ^ 2), second), third)
+    args = (place, block, exchange(block, lambda i: i ^ 1))
     scratch = [pltpu.VMEM((40, width), F32)]
-    return call(finish_kernel, "finish", [((shard, width), F32)], args, smem=1, scratch=scratch)[0]
+    return call(finish_kernel, "finish", [((shard, width), F32)], args, smem=1, scratch=scratch, flops=FINISH_FLOPS)[0]
 
 
 def on_device(n_seq, n_dp, queries, key_vectors, value_vectors, out_grad, out_weight, clip_frames):

time: 150 us -> 141 us (0.940); the launches traced: 150 us -> 139 us
  waiting for transfers between devices: 52.8 us -> 43.1 us
  starting transfers between devices: 62.7 us -> 61.1 us
  local copies, waits for them, and re-layouts: 1.46 us -> 3.06 us
    ppermute x5 -> x4, waiting for transfers between devices: 17 us -> 7.47 us  [exchange(): lax.ppermute(block, 'dp', [(source(i) % n_dp, i) for i in range(n_dp)])]
    reshape x1, local copies, waits for them, and re-layouts: 1.44 us -> 3.05 us  [on_device(): back[:, i * width:(i + 1) * width].reshape(queries.shape)]
    ppermute x5 -> x4, starting transfers between devices: 26.3 us -> 25.5 us  [exchange(): lax.ppermute(block, 'dp', [(source(i) % n_dp, i) for i in range(n_dp)])]
  transfers between devices with their start and end apart: 12 -> 11, of which waited for: 8 -> 8; matrix products, arithmetic and copies ran while one was open for 0% -> 0% of each run, Pallas kernels for 19% -> 20%
where the time goes in v6:
time: 141 us; the launch traced here: 139 us
  starting transfers between devices  61.1 us (43%)
  waiting for transfers between devices  43.1 us (31%)
  Pallas kernels  30.6 us (22%)
  local copies, waits for them, and re-layouts  3.06 us (2%)
    pallas_call x8, Pallas kernels, call(): pl.pallas_call(kernel, out_shape=[pltpu.HBM(s.shape, s.dtype) if i in hbm...  30.6 us
    all_to_all x3, waiting for transfers between devices, swap(): lax.all_to_all(block.reshape(n_seq, positions, -1), 'seq', 0, 0, tiled=True)  28.7 us
    ppermute x4, starting transfers between devices, exchange(): lax.ppermute(block, 'dp', [(source(i) % n_dp, i) for i in range(n_dp)])  25.5 us
    all_to_all x3, starting transfers between devices, swap(): lax.all_to_all(block.reshape(n_seq, positions, -1), 'seq', 0, 0, tiled=True)  23.2 us
    ppermute x4, waiting for transfers between devices, exchange(): lax.ppermute(block, 'dp', [(source(i) % n_dp, i) for i in range(n_dp)])  7.47 us
    ppermute x3, starting transfers between devices, partner(): return lax.ppermute(block, 'seq', [(i, i ^ 1) for i in range(n_seq)])  6.43 us
    all_to_all x1, starting transfers between devices, on_device(): lax.all_to_all(chip, ('dp', 'seq'), 0, 0, tiled=True, axis_index_groups=p...  5.93 us
    ppermute x3, waiting for transfers between devices, partner(): return lax.ppermute(block, 'seq', [(i, i ^ 1) for i in range(n_seq)])  5.16 us
  transfers between devices with their start and end apart: 11, of which 8 were waited for; matrix products, arithmetic and copies ran while one was open for 0% of the time, Pallas kernels for 20%

profile of v6, /device:TPU:6, one launch (start us, length us, event | category | flops | bytes accessed | tf_op | source)
XLA Modules:
  0.0 138.9 jit_solution(13953311764826322825)
XLA Ops:
  0.6 2.6 %pack.1 = bf16[256,4608]{1,0:T(8,128)(2,1)} custom-call(bf16[256,1152]{1,0:T(8,128)(2,1)} %bitcast.29, bf16[256,1152]{1,0:T(8,128)(2,1)} %bitcast.30, bf16[256,1152]{1,0:T(8,128)(2,1)} %bitcast.31, bf16[256,1152]{1,0:T(8,128)(2,1)} %bitcast.32), custom_call_target="tpu_custom_call" | custom-call | bytes 4718592 | tf_op jit(solution)/shard_map/pack/pallas_call | solution.py:353
  3.3 0.0 copy-start
  3.3 0.0 copy-start.1
  3.3 9.9 %all-to-all-start = ((bf16[32,8,4608]{2,1,0:T(8,128)(2,1)}), bf16[32,8,4608]{2,1,0:T(8,128)(2,1)S(1)}, u32[]{:S(2)}, u32[]{:S(2)}) async-start(bf16[32,8,4608]{2,1,0:T(8,128)(2,1)} %bitcast.24), calls=%async_computation | async-start | bytes 4718592 | tf_op jit(solution)/shard_map/all_to_all | solution.py:454
  13.2 1.8 %spread.1 = bf16[256,2688]{1,0:T(8,128)(2,1)} custom-call(bf16[36,1152]{1,0:T(8,128)(2,1)S(1)} %bitcast.23), custom_call_target="tpu_custom_call" | custom-call | bytes 1459200 | tf_op jit(solution)/shard_map/spread/pallas_call | solution.py:353
  15.0 2.6 %tables.1 = (bf16[1152,1152]{1,0:T(8,128)(2,1)}, f32[256,256]{1,0:T(8,128)S(1)}) custom-call(s32[1]{0:T(128)} %bitcast.core_ref, s32[1,4]{1,0:T(1,128)S(1)} %copy-done.1), custom_call_target="tpu_custom_call" | custom-call | bytes 2916372 | tf_op jit(solution)/shard_map/tables/pallas_call | solution.py:353
  17.6 24.6 %all-to-all-done = bf16[32,8,4608]{2,1,0:T(8,128)(2,1)S(1)} async-done(((bf16[32,8,4608]{2,1,0:T(8,128)(2,1)}), bf16[32,8,4608]{2,1,0:T(8,128)(2,1)S(1)}, u32[]{:S(2)}, u32[]{:S(2)}) %all-to-all-start) | async-done | bytes 2359328 | tf_op jit(solution)/shard_map/all_to_all | solution.py:454
  42.2 7.3 %all-to-all-start.2 = ((bf16[32,8,2688]{2,1,0:T(8,128)(2,1)}), bf16[32,8,2688]{2,1,0:T(8,128)(2,1)}, u32[]{:S(2)}, u32[]{:S(2)}) async-start(bf16[32,8,2688]{2,1,0:T(8,128)(2,1)} %bitcast.25), calls=%async_computation.2 | async-start | bytes 2752512 | tf_op jit(solution)/shard_map/all_to_all | solution.py:454
  49.6 6.6 %forward.1 = (bf16[256,1152]{1,0:T(8,128)(2,1)S(1)}, bf16[16,40,1152]{2,1,0:T(8,128)(2,1)S(1)}, bf16[8,40,1152]{2,1,0:T(8,128)(2,1)}, bf16[8,40,1152]{2,1,0:T(8,128)(2,1)}) custom-call(s32[1]{0:T(128)} %bitcast.core_ref, bf16[256,4608]{1,0:T(8,128)(2,1)} %bitcast.27, f32[256,256]{1,0:T(8,128)S(1)} %get-tuple-element.16.bias_ref), custom_call_target="tpu_custom_call" | custom-call | flops 99999997952 | tf_op jit(solution)/shard_map/forward/pallas_call | solution.py:353
  56.2 2.1 %collective-permute-start = (bf16[8,40,1152]{2,1,0:T(8,128)(2,1)}, bf16[8,40,1152]{2,1,0:T(8,128)(2,1)S(1)}, u32[]{:S(2)}, u32[]{:S(2)}) collective-permute-start(bf16[8,40,1152]{2,1,0:T(8,128)(2,1)} %get-tuple-element.18), channel_id=1, source_target_pairs={{0,1},{1,0},{2,3},{3,2},{4,5},{5,4},{6,7},{7,6},{8,9},{9,8},{10,11... | collective-permute-start | bytes 2211848 | tf_op jit(solution)/shard_map/ppermute | solution.py:457
  58.3 2.3 %collective-permute-start.1 = (bf16[8,40,1152]{2,1,0:T(8,128)(2,1)}, bf16[8,40,1152]{2,1,0:T(8,128)(2,1)S(1)}, u32[]{:S(2)}, u32[]{:S(2)}) collective-permute-start(bf16[8,40,1152]{2,1,0:T(8,128)(2,1)} %get-tuple-element.19), channel_id=1, source_target_pairs={{0,1},{1,0},{2,3},{3,2},{4,5},{5,4},{6,7},{7,6},{8,9},{9,8},{10,11... | collective-permute-start | bytes 2211848 | tf_op jit(solution)/shard_map/ppermute | solution.py:457
  60.6 0.0 collective-permute-done.first_ref
  60.6 2.0 %collective-permute-done.1.second_ref = bf16[8,40,1152]{2,1,0:T(8,128)(2,1)S(1)} collective-permute-done((bf16[8,40,1152]{2,1,0:T(8,128)(2,1)}, bf16[8,40,1152]{2,1,0:T(8,128)(2,1)S(1)}, u32[]{:S(2)}, u32[]{:S(2)}) %collective-permute-start.1) | collective-permute-done | bytes 737312 | tf_op jit(solution)/shard_map/ppermute | solution.py:457
  62.6 1.6 %join.1 = bf16[2,16,8,2944]{3,2,1,0:T(8,128)(2,1)} custom-call(bf16[16,40,1152]{2,1,0:T(8,128)(2,1)S(1)} %get-tuple-element.17.keep_ref, bf16[8,40,1152]{2,1,0:T(8,128)(2,1)S(1)} %collective-permute-done.first_ref, bf16[8,40,1152]{2,1,0:T(8,128)(2,1)S(1)} %collective-permute-done.1.second_ref), custom_call_target="tpu_custom_call" | custom-call | flops 1000000000 | tf_op jit(solution)/shard_map/join/pallas_call | solution.py:353
  64.2 4.1 %all-to-all-done.2 = bf16[32,8,2688]{2,1,0:T(8,128)(2,1)} async-done(((bf16[32,8,2688]{2,1,0:T(8,128)(2,1)}), bf16[32,8,2688]{2,1,0:T(8,128)(2,1)}, u32[]{:S(2)}, u32[]{:S(2)}) %all-to-all-start.2) | async-done | bytes 1376288 | tf_op jit(solution)/shard_map/all_to_all | solution.py:454
  68.3 5.9 %all-to-all-start.1 = ((bf16[32,8,2944]{2,1,0:T(8,128)(2,1)}), bf16[32,8,2944]{2,1,0:T(8,128)(2,1)S(1)}, u32[]{:S(2)}, u32[]{:S(2)}) async-start(bf16[32,8,2944]{2,1,0:T(8,128)(2,1)} %bitcast.8), calls=%async_computation.1 | async-start | bytes 3014656 | tf_op jit(solution)/shard_map/all_to_all | solution.py:471
  74.2 2.1 %collective-permute-start.2 = (bf16[256,2688]{1,0:T(8,128)(2,1)}, bf16[256,2688]{1,0:T(8,128)(2,1)S(1)}, u32[]{:S(2)}, u32[]{:S(2)}) collective-permute-start(bf16[256,2688]{1,0:T(8,128)(2,1)} %bitcast.10.own_hbm), channel_id=1, source_target_pairs={{0,1},{1,0},{2,3},{3,2},{4,5},{5,4},{6,7},{7,6},{8,9},{9,8},{10,11... | collective-permute-start | bytes 4128776 | tf_op jit(solution)/shard_map/ppermute | solution.py:457
  76.3 3.1 %collective-permute-done.2.other_ref = bf16[256,2688]{1,0:T(8,128)(2,1)S(1)} collective-permute-done((bf16[256,2688]{1,0:T(8,128)(2,1)}, bf16[256,2688]{1,0:T(8,128)(2,1)S(1)}, u32[]{:S(2)}, u32[]{:S(2)}) %collective-permute-start.2) | collective-permute-done | bytes 1376288 | tf_op jit(solution)/shard_map/ppermute | solution.py:457
  79.4 13.9 %backward.1 = bf16[256,4608]{1,0:T(8,128)(2,1)} custom-call(bf16[1152,1152]{1,0:T(8,128)(2,1)} %get-tuple-element.20.pick_hbm, bf16[256,4608]{1,0:T(8,128)(2,1)} %bitcast.28, bf16[256,2688]{1,0:T(8,128)(2,1)} %bitcast.10.own_hbm, bf16[256,2688]{1,0:T(8,128)(2,1)S(1)} %collective-permute-done.2.other_ref, f32[256,256]{1,0:T(8,128)S(1)} %get-tuple-element.16.bias_ref, ...), custom_call_target="tpu_custom_call" | custom-call | flops 5939134464 | tf_op jit(solution)/shard_map/backward/pallas_call | solution.py:353
  93.3 1.8 %all-to-all-done.1.parts_ref = bf16[32,8,2944]{2,1,0:T(8,128)(2,1)S(1)} async-done(((bf16[32,8,2944]{2,1,0:T(8,128)(2,1)}), bf16[32,8,2944]{2,1,0:T(8,128)(2,1)S(1)}, u32[]{:S(2)}, u32[]{:S(2)}) %all-to-all-start.1) | async-done | bytes 1507360 | tf_op jit(solution)/shard_map/all_to_all | solution.py:471
  95.2 0.2 total.1
  95.4 3.8 %collective-permute-start.3 = (bf16[8,2944]{1,0:T(8,128)(2,1)S(1)}, bf16[8,2944]{1,0:T(8,128)(2,1)S(1)}, u32[]{:S(2)}, u32[]{:S(2)}) collective-permute-start(bf16[8,2944]{1,0:T(8,128)(2,1)S(1)} %total.1), channel_id=1, source_target_pairs={{64,0},{96,32},{0,64},{32,96},{192,128},{224,160},{128,192},{160,2... | collective-permute-start | bytes 141320 | tf_op jit(solution)/shard_map/ppermute | solution.py:430
  99.2 6.0 %all-to-all-start.3 = ((bf16[32,8,4608]{2,1,0:T(8,128)(2,1)}), bf16[32,8,4608]{2,1,0:T(8,128)(2,1)}, u32[]{:S(2)}, u32[]{:S(2)}) async-start(bf16[32,8,4608]{2,1,0:T(8,128)(2,1)} %bitcast.26), calls=%async_computation.3 | async-start | bytes 4718592 | tf_op jit(solution)/shard_map/all_to_all | solution.py:454
  105.2 9.1 %collective-permute-start.4 = (bf16[8,2944]{1,0:T(8,128)(2,1)S(1)}, bf16[8,2944]{1,0:T(8,128)(2,1)S(1)}, u32[]{:S(2)}, u32[]{:S(2)}) collective-permute-start(bf16[8,2944]{1,0:T(8,128)(2,1)S(1)} %add_convert_fusion.2), channel_id=1, source_target_pairs={{128,0},{416,32},{192,64},{480,96},{0,128},{288,160},{64,192},{352... | collective-permute-start | bytes 141320 | tf_op jit(solution)/shard_map/ppermute | solution.py:430
  114.3 3.1 %collective-permute-done.4 = bf16[8,2944]{1,0:T(8,128)(2,1)S(1)} collective-permute-done((bf16[8,2944]{1,0:T(8,128)(2,1)S(1)}, bf16[8,2944]{1,0:T(8,128)(2,1)S(1)}, u32[]{:S(2)}, u32[]{:S(2)}) %collective-permute-start.4) | collective-permute-done | bytes 47136 | tf_op jit(solution)/shard_map/ppermute | solution.py:430
  117.4 7.8 %collective-permute-start.5 = (bf16[8,2944]{1,0:T(8,128)(2,1)S(1)}, bf16[8,2944]{1,0:T(8,128)(2,1)S(1)}, u32[]{:S(2)}, u32[]{:S(2)}) collective-permute-start(bf16[8,2944]{1,0:T(8,128)(2,1)S(1)} %add_convert_fusion.1), channel_id=1, source_target_pairs={{448,0},{224,32},{384,64},{160,96},{320,128},{96,160},{256,192},{3... | collective-permute-start | bytes 141320 | tf_op jit(solution)/shard_map/ppermute | solution.py:430
  125.3 2.4 %collective-permute-done.5 = bf16[8,2944]{1,0:T(8,128)(2,1)S(1)} collective-permute-done((bf16[8,2944]{1,0:T(8,128)(2,1)S(1)}, bf16[8,2944]{1,0:T(8,128)(2,1)S(1)}, u32[]{:S(2)}, u32[]{:S(2)}) %collective-permute-start.5) | collective-permute-done | bytes 47136 | tf_op jit(solution)/shard_map/ppermute | solution.py:430
  127.7 4.8 %collective-permute-start.6 = (bf16[8,2944]{1,0:T(8,128)(2,1)S(1)}, bf16[8,2944]{1,0:T(8,128)(2,1)S(1)}, u32[]{:S(2)}, u32[]{:S(2)}) collective-permute-start(bf16[8,2944]{1,0:T(8,128)(2,1)S(1)} %add_convert_fusion.mine_ref), channel_id=1, source_target_pairs={{32,0},{0,32},{96,64},{64,96},{160,128},{128,160},{224,192},{192,2... | collective-permute-start | bytes 141320 | tf_op jit(solution)/shard_map/ppermute | solution.py:430
  132.6 0.1 pad_add_fusion.place_ref
  132.7 2.0 %collective-permute-done.6.other_ref = bf16[8,2944]{1,0:T(8,128)(2,1)S(1)} collective-permute-done((bf16[8,2944]{1,0:T(8,128)(2,1)S(1)}, bf16[8,2944]{1,0:T(8,128)(2,1)S(1)}, u32[]{:S(2)}, u32[]{:S(2)}) %collective-permute-start.6) | collective-permute-done | bytes 47136 | tf_op jit(solution)/shard_map/ppermute | solution.py:430
  134.6 1.3 finish.1
  135.9 3.0 %slice_bitcast_fusion = (bf16[1,1,256,1152]{3,2,1,0:T(8,128)(2,1)}, bf16[1,1,256,1152]{3,2,1,0:T(8,128)(2,1)}, bf16[1,1,256,1152]{3,2,1,0:T(8,128)(2,1)}, bf16[1,1,256,1152]{3,2,1,0:T(8,128)(2,1)}) fusion(bf16[256,4608]{1,0:T(8,128)(2,1)} %bitcast.12), kind=kLoop, calls=%fused_computation | loop fusion | bytes 4718592 | tf_op jit(solution)/shard_map/reshape | solution.py:478
  (9 shorter events, 0.1 us)
Async XLA Ops:
  3.3 9.9 %copy-start = (bf16[1152,36]{0,1:T(8,128)(2,1)S(1)}, bf16[1152,36]{0,1:T(8,128)(2,1)}, u32[]{:S(2)}) copy-start(bf16[1152,36]{0,1:T(8,128)(2,1)} %param.10) | copy-start | bytes 248836
  3.3 11.7 %copy-start.1 = (s32[1,4]{1,0:T(1,128)S(1)}, s32[1,4]{1,0:T(1,128)}, u32[]{:S(2)}) copy-start(s32[1,4]{1,0:T(1,128)} %lens_ref.1) | copy-start | bytes 52
  3.3 38.9 %all-to-all-start = ((bf16[32,8,4608]{2,1,0:T(8,128)(2,1)}), bf16[32,8,4608]{2,1,0:T(8,128)(2,1)S(1)}, u32[]{:S(2)}, u32[]{:S(2)}) async-start(bf16[32,8,4608]{2,1,0:T(8,128)(2,1)} %bitcast.24), calls=%async_computation | async-start | bytes 4718592 | tf_op jit(solution)/shard_map/all_to_all | solution.py:454
  42.2 7.4 %copy-start.2 = (bf16[32,8,4608]{2,1,0:T(8,128)(2,1)}, bf16[32,8,4608]{2,1,0:T(8,128)(2,1)S(1)}, u32[]{:S(2)}) copy-start(bf16[32,8,4608]{2,1,0:T(8,128)(2,1)S(1)} %all-to-all-done) | copy-start | bytes 7077892
  42.2 26.1 %all-to-all-start.2 = ((bf16[32,8,2688]{2,1,0:T(8,128)(2,1)}), bf16[32,8,2688]{2,1,0:T(8,128)(2,1)}, u32[]{:S(2)}, u32[]{:S(2)}) async-start(bf16[32,8,2688]{2,1,0:T(8,128)(2,1)} %bitcast.25), calls=%async_computation.2 | async-start | bytes 2752512 | tf_op jit(solution)/shard_map/all_to_all | solution.py:454
  56.2 4.3 %collective-permute-start = (bf16[8,40,1152]{2,1,0:T(8,128)(2,1)}, bf16[8,40,1152]{2,1,0:T(8,128)(2,1)S(1)}, u32[]{:S(2)}, u32[]{:S(2)}) collective-permute-start(bf16[8,40,1152]{2,1,0:T(8,128)(2,1)} %get-tuple-element.18), channel_id=1, source_target_pairs={{0,1},{1,0},{2,3},{3,2},{4,5},{5,4},{6,7},{7,6},{8,9},{9,8},{10,11... | collective-permute-start | bytes 2211848 | tf_op jit(solution)/shard_map/ppermute | solution.py:457
  58.3 4.3 %collective-permute-start.1 = (bf16[8,40,1152]{2,1,0:T(8,128)(2,1)}, bf16[8,40,1152]{2,1,0:T(8,128)(2,1)S(1)}, u32[]{:S(2)}, u32[]{:S(2)}) collective-permute-start(bf16[8,40,1152]{2,1,0:T(8,128)(2,1)} %get-tuple-element.19), channel_id=1, source_target_pairs={{0,1},{1,0},{2,3},{3,2},{4,5},{5,4},{6,7},{7,6},{8,9},{9,8},{10,11... | collective-permute-start | bytes 2211848 | tf_op jit(solution)/shard_map/ppermute | solution.py:457
  68.3 26.9 %all-to-all-start.1 = ((bf16[32,8,2944]{2,1,0:T(8,128)(2,1)}), bf16[32,8,2944]{2,1,0:T(8,128)(2,1)S(1)}, u32[]{:S(2)}, u32[]{:S(2)}) async-start(bf16[32,8,2944]{2,1,0:T(8,128)(2,1)} %bitcast.8), calls=%async_computation.1 | async-start | bytes 3014656 | tf_op jit(solution)/shard_map/all_to_all | solution.py:471
  74.2 5.2 %collective-permute-start.2 = (bf16[256,2688]{1,0:T(8,128)(2,1)}, bf16[256,2688]{1,0:T(8,128)(2,1)S(1)}, u32[]{:S(2)}, u32[]{:S(2)}) collective-permute-start(bf16[256,2688]{1,0:T(8,128)(2,1)} %bitcast.10.own_hbm), channel_id=1, source_target_pairs={{0,1},{1,0},{2,3},{3,2},{4,5},{5,4},{6,7},{7,6},{8,9},{9,8},{10,11... | collective-permute-start | bytes 4128776 | tf_op jit(solution)/shard_map/ppermute | solution.py:457
  95.4 9.8 %collective-permute-start.3 = (bf16[8,2944]{1,0:T(8,128)(2,1)S(1)}, bf16[8,2944]{1,0:T(8,128)(2,1)S(1)}, u32[]{:S(2)}, u32[]{:S(2)}) collective-permute-start(bf16[8,2944]{1,0:T(8,128)(2,1)S(1)} %total.1), channel_id=1, source_target_pairs={{64,0},{96,32},{0,64},{32,96},{192,128},{224,160},{128,192},{160,2... | collective-permute-start | bytes 141320 | tf_op jit(solution)/shard_map/ppermute | solution.py:430
  99.2 36.7 %all-to-all-start.3 = ((bf16[32,8,4608]{2,1,0:T(8,128)(2,1)}), bf16[32,8,4608]{2,1,0:T(8,128)(2,1)}, u32[]{:S(2)}, u32[]{:S(2)}) async-start(bf16[32,8,4608]{2,1,0:T(8,128)(2,1)} %bitcast.26), calls=%async_computation.3 | async-start | bytes 4718592 | tf_op jit(solution)/shard_map/all_to_all | solution.py:454
  105.2 12.2 %collective-permute-start.4 = (bf16[8,2944]{1,0:T(8,128)(2,1)S(1)}, bf16[8,2944]{1,0:T(8,128)(2,1)S(1)}, u32[]{:S(2)}, u32[]{:S(2)}) collective-permute-start(bf16[8,2944]{1,0:T(8,128)(2,1)S(1)} %add_convert_fusion.2), channel_id=1, source_target_pairs={{128,0},{416,32},{192,64},{480,96},{0,128},{288,160},{64,192},{352... | collective-permute-start | bytes 141320 | tf_op jit(solution)/shard_map/ppermute | solution.py:430
  117.4 10.3 %collective-permute-start.5 = (bf16[8,2944]{1,0:T(8,128)(2,1)S(1)}, bf16[8,2944]{1,0:T(8,128)(2,1)S(1)}, u32[]{:S(2)}, u32[]{:S(2)}) collective-permute-start(bf16[8,2944]{1,0:T(8,128)(2,1)S(1)} %add_convert_fusion.1), channel_id=1, source_target_pairs={{448,0},{224,32},{384,64},{160,96},{320,128},{96,160},{256,192},{3... | collective-permute-start | bytes 141320 | tf_op jit(solution)/shard_map/ppermute | solution.py:430
  127.7 6.9 %collective-permute-start.6 = (bf16[8,2944]{1,0:T(8,128)(2,1)S(1)}, bf16[8,2944]{1,0:T(8,128)(2,1)S(1)}, u32[]{:S(2)}, u32[]{:S(2)}) collective-permute-start(bf16[8,2944]{1,0:T(8,128)(2,1)S(1)} %add_convert_fusion.mine_ref), channel_id=1, source_target_pairs={{32,0},{0,32},{96,64},{64,96},{160,128},{128,160},{224,192},{192,2... | collective-permute-start | bytes 141320 | tf_op jit(solution)/shard_map/ppermute | solution.py:430

commit v7 on v6

--- a/solution.py
+++ b/solution.py
@@ -114,6 +114,18 @@
         fetch.start()
     for fetch, copy in zip(fetches, copies):
         fetch.wait()
+        copy.start()
+    for copy in copies:
+        copy.wait()
+
+
+def unpack_kernel(x_ref, *refs):
+    *outs, sems = refs
+    width = outs[0].shape[1]
+    copies = [
+        pltpu.make_async_copy(x_ref.at[:, pl.ds(i * width, width)], out, sems.at[i]) for i, out in enumerate(outs)
+    ]
+    for copy in copies:
         copy.start()
     for copy in copies:
         copy.wait()
@@ -257,15 +269,16 @@
 
 def backward_kernel(
     pick_hbm, x_hbm, own_hbm, other_ref, bias_ref, mixed_ref, y_ref,
-    pick_ref, x_ref, own_ref, odd_ref, back_ref, out_ref, held_ref, sems
+    pick_ref, x_ref, own_ref, odd_ref, back_ref, out_ref, held_ref, attention_ref, sems
 ):
     rows, width = mixed_ref.shape
-    three, fourth = pl.ds(0, 3 * width), pl.ds(3 * width, width)
+    pairs, third, fourth = pl.ds(0, 2 * width), pl.ds(2 * width, width), pl.ds(3 * width, width)
     fetches = [
-        pltpu.make_async_copy(own_hbm, own_ref, sems.at[7]),
-        pltpu.make_async_copy(pick_hbm, pick_ref, sems.at[8]),
+        pltpu.make_async_copy(x_hbm.at[:, pairs], x_ref.at[:, pairs], sems.at[7]),
+        pltpu.make_async_copy(own_hbm, own_ref, sems.at[8]),
         pltpu.make_async_copy(x_hbm.at[:, fourth], x_ref.at[:, fourth], sems.at[9]),
-        pltpu.make_async_copy(x_hbm.at[:, three], x_ref.at[:, three], sems.at[10]),
+        pltpu.make_async_copy(pick_hbm, pick_ref, sems.at[10]),
+        pltpu.make_async_copy(x_hbm.at[:, third], x_ref.at[:, third], sems.at[11]),
     ]
     for fetch in fetches:
         fetch.start()
@@ -276,8 +289,16 @@
         copies.append(pltpu.make_async_copy(held_ref.at[:, lanes], y_ref.at[:, lanes], sems.at[len(copies)]))
         copies[-1].start()
 
+    fetches[0].wait()
+    bias = bias_ref[...]
+    for head in range(HEADS):
+        start, size = window(head)
+        query_win = jnp.where(head_lanes(head, rows), x_ref[:, pl.ds(start, size)], 0)
+        scores = dot_nt(x_ref[:, pl.ds(width + start, size)], query_win) * SCALE + bias
+        raised = jnp.exp(scores - jnp.max(scores, axis=0, keepdims=True))
+        attention_ref[head] = raised * (1.0 / jnp.sum(raised, axis=0, keepdims=True))
     blocks = FULL // GROUP
-    fetches[0].wait()
+    fetches[1].wait()
     weight = []
     for ref in (own_ref, other_ref):
         weight += [ref[:, pl.ds(b * width, width)] for b in range(blocks)]
@@ -295,8 +316,8 @@
                 lanes = pl.ds((CHUNK * u + q) * LANES, LANES)
                 odd_ref[pl.ds(i * odd_rows, odd_rows), lanes] = got[:, u * LANES : (u + 1) * LANES]
     weight.append(odd_ref[...])
-    fetches[1].wait()
     fetches[2].wait()
+    fetches[3].wait()
     grad = dot_nt(x_ref[:, fourth], pick_ref[...]).astype(BF16)
     mixed = mixed_ref[...]
     back = jnp.zeros((rows, width), F32)
@@ -310,8 +331,7 @@
     held_ref[:, pl.ds(0, width)] = dot(out_ref[...], pick_ref[...]).astype(BF16)
     send(0, width)
     query_tiles, key_tiles, value_tiles = [Tiles(held_ref, i * width) for i in (1, 2, 3)]
-    bias = bias_ref[...]
-    fetches[3].wait()
+    fetches[4].wait()
     sent = 0
     for head in range(HEADS):
         start, size = window(head)
@@ -320,9 +340,7 @@
         key_win = jnp.where(lanes, x_ref[:, pl.ds(width + start, size)], 0)
         value_win = x_ref[:, pl.ds(2 * width + start, size)]
         back_win = jnp.where(lanes, back_ref[:, pl.ds(start, size)], 0)
-        scores = dot_nt(key_win, query_win) * SCALE + bias
-        raised = jnp.exp(scores - jnp.max(scores, axis=0, keepdims=True))
-        attention = raised * (1.0 / jnp.sum(raised, axis=0, keepdims=True))
+        attention = attention_ref[head]
         value_tiles.add(head, dot(attention.astype(BF16), back_win))
         drawn = attention * dot_nt(value_win, back_win)
         inner = jnp.sum(drawn, axis=0, keepdims=True)
@@ -374,6 +392,13 @@
     return call(pack_kernel, "pack", outs, arrays, hbm_in=count, hbm_out=(0,), scratch=scratch)[0]
 
 
+def unpack(x, count):
+    rows, wide = x.shape
+    width = wide // count
+    outs = [((rows, width), BF16)] * count
+    return call(unpack_kernel, "unpack", outs, (x,), hbm_out=range(count), scratch=[dma(count)])
+
+
 def spread(weight_t, rows):
     shape = (rows, FULL // GROUP * weight_t.shape[1] + ODD_LANES)
     scratch = [pltpu.VMEM(shape, BF16), dma(1)]
@@ -410,7 +435,8 @@
     flops = 8 * width * rows * width + 12 * HEADS * rows * rows * 256
     one, wide = (rows, width), (rows, 4 * width)
     shapes = ((width, width), wide, own.shape, (width - 4 * rows, width), one, one, wide)
-    scratch = [pltpu.VMEM(shape, BF16) for shape in shapes] + [dma(11)]
+    scratch = [pltpu.VMEM(shape, BF16) for shape in shapes]
+    scratch += [pltpu.VMEM((HEADS, rows, rows), F32), dma(12)]
     args = (pick, x, own, other, bias, mixed)
     return call(backward_kernel, "backward", [(wide, BF16)], args, hbm_in=3, hbm_out=(0,), scratch=scratch, flops=flops)[0]
 
@@ -475,7 +501,7 @@
     back = swap(y).reshape(patches, 4 * width)
     place = jnp.stack([jnp.bitwise_and(lax.axis_index("dp"), 1).astype(jnp.int32), core])
     weight_grad = sum_over_pairs(total, place, shard, width, n_dp).T
-    outs = [back[:, i * width : (i + 1) * width].reshape(queries.shape) for i in range(4)]
+    outs = [out.reshape(queries.shape) for out in unpack(back, 4)]
     return (*outs, weight_grad)
 
 

time: 141 us -> 139 us (0.986)
  local copies, waits for them, and re-layouts: 3.06 us -> 0.02 us
    reshape x1 -> x0, local copies, waits for them, and re-layouts: 3.05 us -> none  [on_device(): back[:, i * width:(i + 1) * width].reshape(queries.shape)]
    pallas_call x8 -> x9, Pallas kernels: 30.6 us -> 31.6 us  [call(): pl.pallas_call(kernel, out_shape=[pltpu.HBM(s.shape, s.dtype) if i in hbm...]
where the time goes in v7:
time: 139 us; the launch traced here: 137 us
  starting transfers between devices  60.6 us (44%)
  waiting for transfers between devices  43.6 us (31%)
  Pallas kernels  31.6 us (23%)
    pallas_call x9, Pallas kernels, call(): pl.pallas_call(kernel, out_shape=[pltpu.HBM(s.shape, s.dtype) if i in hbm...  31.6 us
    all_to_all x3, waiting for transfers between devices, swap(): lax.all_to_all(block.reshape(n_seq, positions, -1), 'seq', 0, 0, tiled=True)  28.7 us
    ppermute x4, starting transfers between devices, exchange(): lax.ppermute(block, 'dp', [(source(i) % n_dp, i) for i in range(n_dp)])  25.5 us
    all_to_all x3, starting transfers between devices, swap(): lax.all_to_all(block.reshape(n_seq, positions, -1), 'seq', 0, 0, tiled=True)  22.7 us
    ppermute x4, waiting for transfers between devices, exchange(): lax.ppermute(block, 'dp', [(source(i) % n_dp, i) for i in range(n_dp)])  7.47 us
    ppermute x3, starting transfers between devices, partner(): return lax.ppermute(block, 'seq', [(i, i ^ 1) for i in range(n_seq)])  6.43 us
    all_to_all x1, starting transfers between devices, on_device(): lax.all_to_all(chip, ('dp', 'seq'), 0, 0, tiled=True, axis_index_groups=p...  5.93 us
    ppermute x3, waiting for transfers between devices, partner(): return lax.ppermute(block, 'seq', [(i, i ^ 1) for i in range(n_seq)])  5.16 us
  transfers between devices with their start and end apart: 11, of which 8 were waited for; matrix products, arithmetic and copies ran while one was open for 0% of the time, Pallas kernels for 20%

profile of v7, /device:TPU:6, one launch (start us, length us, event | category | flops | bytes accessed | tf_op | source)
XLA Modules:
  0.0 136.9 jit_solution(753344708165838414)
XLA Ops:
  0.6 2.6 %pack.1 = bf16[256,4608]{1,0:T(8,128)(2,1)} custom-call(bf16[256,1152]{1,0:T(8,128)(2,1)} %bitcast.26, bf16[256,1152]{1,0:T(8,128)(2,1)} %bitcast.27, bf16[256,1152]{1,0:T(8,128)(2,1)} %bitcast.28, bf16[256,1152]{1,0:T(8,128)(2,1)} %bitcast.29), custom_call_target="tpu_custom_call" | custom-call | bytes 4718592 | tf_op jit(solution)/shard_map/pack/pallas_call | solution.py:371
  3.3 0.0 copy-start
  3.3 0.0 copy-start.1
  3.3 9.9 %all-to-all-start = ((bf16[32,8,4608]{2,1,0:T(8,128)(2,1)}), bf16[32,8,4608]{2,1,0:T(8,128)(2,1)S(1)}, u32[]{:S(2)}, u32[]{:S(2)}) async-start(bf16[32,8,4608]{2,1,0:T(8,128)(2,1)} %bitcast.21), calls=%async_computation | async-start | bytes 4718592 | tf_op jit(solution)/shard_map/all_to_all | solution.py:480
  13.2 1.8 %spread.1 = bf16[256,2688]{1,0:T(8,128)(2,1)} custom-call(bf16[36,1152]{1,0:T(8,128)(2,1)S(1)} %bitcast.20), custom_call_target="tpu_custom_call" | custom-call | bytes 1459200 | tf_op jit(solution)/shard_map/spread/pallas_call | solution.py:371
  15.0 2.6 %tables.1 = (bf16[1152,1152]{1,0:T(8,128)(2,1)}, f32[256,256]{1,0:T(8,128)S(1)}) custom-call(s32[1]{0:T(128)} %bitcast.core_ref, s32[1,4]{1,0:T(1,128)S(1)} %copy-done.1), custom_call_target="tpu_custom_call" | custom-call | bytes 2916372 | tf_op jit(solution)/shard_map/tables/pallas_call | solution.py:371
  17.6 24.6 %all-to-all-done = bf16[32,8,4608]{2,1,0:T(8,128)(2,1)S(1)} async-done(((bf16[32,8,4608]{2,1,0:T(8,128)(2,1)}), bf16[32,8,4608]{2,1,0:T(8,128)(2,1)S(1)}, u32[]{:S(2)}, u32[]{:S(2)}) %all-to-all-start) | async-done | bytes 2359328 | tf_op jit(solution)/shard_map/all_to_all | solution.py:480
  42.2 7.3 %all-to-all-start.2 = ((bf16[32,8,2688]{2,1,0:T(8,128)(2,1)}), bf16[32,8,2688]{2,1,0:T(8,128)(2,1)}, u32[]{:S(2)}, u32[]{:S(2)}) async-start(bf16[32,8,2688]{2,1,0:T(8,128)(2,1)} %bitcast.22), calls=%async_computation.2 | async-start | bytes 2752512 | tf_op jit(solution)/shard_map/all_to_all | solution.py:480
  49.6 6.6 %forward.1 = (bf16[256,1152]{1,0:T(8,128)(2,1)S(1)}, bf16[16,40,1152]{2,1,0:T(8,128)(2,1)S(1)}, bf16[8,40,1152]{2,1,0:T(8,128)(2,1)}, bf16[8,40,1152]{2,1,0:T(8,128)(2,1)}) custom-call(s32[1]{0:T(128)} %bitcast.core_ref, bf16[256,4608]{1,0:T(8,128)(2,1)} %bitcast.24, f32[256,256]{1,0:T(8,128)S(1)} %get-tuple-element.20.bias_ref), custom_call_target="tpu_custom_call" | custom-call | flops 99999997952 | tf_op jit(solution)/shard_map/forward/pallas_call | solution.py:371
  56.2 2.1 %collective-permute-start = (bf16[8,40,1152]{2,1,0:T(8,128)(2,1)}, bf16[8,40,1152]{2,1,0:T(8,128)(2,1)S(1)}, u32[]{:S(2)}, u32[]{:S(2)}) collective-permute-start(bf16[8,40,1152]{2,1,0:T(8,128)(2,1)} %get-tuple-element.22), channel_id=1, source_target_pairs={{0,1},{1,0},{2,3},{3,2},{4,5},{5,4},{6,7},{7,6},{8,9},{9,8},{10,11... | collective-permute-start | bytes 2211848 | tf_op jit(solution)/shard_map/ppermute | solution.py:483
  58.3 2.3 %collective-permute-start.1 = (bf16[8,40,1152]{2,1,0:T(8,128)(2,1)}, bf16[8,40,1152]{2,1,0:T(8,128)(2,1)S(1)}, u32[]{:S(2)}, u32[]{:S(2)}) collective-permute-start(bf16[8,40,1152]{2,1,0:T(8,128)(2,1)} %get-tuple-element.23), channel_id=1, source_target_pairs={{0,1},{1,0},{2,3},{3,2},{4,5},{5,4},{6,7},{7,6},{8,9},{9,8},{10,11... | collective-permute-start | bytes 2211848 | tf_op jit(solution)/shard_map/ppermute | solution.py:483
  60.6 0.0 collective-permute-done.first_ref
  60.6 2.0 %collective-permute-done.1.second_ref = bf16[8,40,1152]{2,1,0:T(8,128)(2,1)S(1)} collective-permute-done((bf16[8,40,1152]{2,1,0:T(8,128)(2,1)}, bf16[8,40,1152]{2,1,0:T(8,128)(2,1)S(1)}, u32[]{:S(2)}, u32[]{:S(2)}) %collective-permute-start.1) | collective-permute-done | bytes 737312 | tf_op jit(solution)/shard_map/ppermute | solution.py:483
  62.6 1.6 %join.1 = bf16[2,16,8,2944]{3,2,1,0:T(8,128)(2,1)} custom-call(bf16[16,40,1152]{2,1,0:T(8,128)(2,1)S(1)} %get-tuple-element.21.keep_ref, bf16[8,40,1152]{2,1,0:T(8,128)(2,1)S(1)} %collective-permute-done.first_ref, bf16[8,40,1152]{2,1,0:T(8,128)(2,1)S(1)} %collective-permute-done.1.second_ref), custom_call_target="tpu_custom_call" | custom-call | flops 1000000000 | tf_op jit(solution)/shard_map/join/pallas_call | solution.py:371
  64.2 4.1 %all-to-all-done.2 = bf16[32,8,2688]{2,1,0:T(8,128)(2,1)} async-done(((bf16[32,8,2688]{2,1,0:T(8,128)(2,1)}), bf16[32,8,2688]{2,1,0:T(8,128)(2,1)}, u32[]{:S(2)}, u32[]{:S(2)}) %all-to-all-start.2) | async-done | bytes 1376288 | tf_op jit(solution)/shard_map/all_to_all | solution.py:480
  68.3 5.9 %all-to-all-start.1 = ((bf16[32,8,2944]{2,1,0:T(8,128)(2,1)}), bf16[32,8,2944]{2,1,0:T(8,128)(2,1)S(1)}, u32[]{:S(2)}, u32[]{:S(2)}) async-start(bf16[32,8,2944]{2,1,0:T(8,128)(2,1)} %bitcast.8), calls=%async_computation.1 | async-start | bytes 3014656 | tf_op jit(solution)/shard_map/all_to_all | solution.py:497
  74.2 2.1 %collective-permute-start.2 = (bf16[256,2688]{1,0:T(8,128)(2,1)}, bf16[256,2688]{1,0:T(8,128)(2,1)S(1)}, u32[]{:S(2)}, u32[]{:S(2)}) collective-permute-start(bf16[256,2688]{1,0:T(8,128)(2,1)} %bitcast.10.own_hbm), channel_id=1, source_target_pairs={{0,1},{1,0},{2,3},{3,2},{4,5},{5,4},{6,7},{7,6},{8,9},{9,8},{10,11... | collective-permute-start | bytes 4128776 | tf_op jit(solution)/shard_map/ppermute | solution.py:483
  76.3 3.1 %collective-permute-done.2.other_ref = bf16[256,2688]{1,0:T(8,128)(2,1)S(1)} collective-permute-done((bf16[256,2688]{1,0:T(8,128)(2,1)}, bf16[256,2688]{1,0:T(8,128)(2,1)S(1)}, u32[]{:S(2)}, u32[]{:S(2)}) %collective-permute-start.2) | collective-permute-done | bytes 1376288 | tf_op jit(solution)/shard_map/ppermute | solution.py:483
  79.4 13.4 %backward.1 = bf16[256,4608]{1,0:T(8,128)(2,1)} custom-call(bf16[1152,1152]{1,0:T(8,128)(2,1)} %get-tuple-element.24.pick_hbm, bf16[256,4608]{1,0:T(8,128)(2,1)} %bitcast.25, bf16[256,2688]{1,0:T(8,128)(2,1)} %bitcast.10.own_hbm, bf16[256,2688]{1,0:T(8,128)(2,1)S(1)} %collective-permute-done.2.other_ref, f32[256,256]{1,0:T(8,128)S(1)} %get-tuple-element.20.bias_ref, ...), custom_call_target="tpu_custom_call" | custom-call | flops 5939134464 | tf_op jit(solution)/shard_map/backward/pallas_call | solution.py:371
  92.9 2.3 %all-to-all-done.1.parts_ref = bf16[32,8,2944]{2,1,0:T(8,128)(2,1)S(1)} async-done(((bf16[32,8,2944]{2,1,0:T(8,128)(2,1)}), bf16[32,8,2944]{2,1,0:T(8,128)(2,1)S(1)}, u32[]{:S(2)}, u32[]{:S(2)}) %all-to-all-start.1) | async-done | bytes 1507360 | tf_op jit(solution)/shard_map/all_to_all | solution.py:497
  95.2 0.2 total.1
  95.4 3.8 %collective-permute-start.3 = (bf16[8,2944]{1,0:T(8,128)(2,1)S(1)}, bf16[8,2944]{1,0:T(8,128)(2,1)S(1)}, u32[]{:S(2)}, u32[]{:S(2)}) collective-permute-start(bf16[8,2944]{1,0:T(8,128)(2,1)S(1)} %total.1), channel_id=1, source_target_pairs={{64,0},{96,32},{0,64},{32,96},{192,128},{224,160},{128,192},{160,2... | collective-permute-start | bytes 141320 | tf_op jit(solution)/shard_map/ppermute | solution.py:456
  99.2 5.5 %all-to-all-start.3 = ((bf16[32,8,4608]{2,1,0:T(8,128)(2,1)}), bf16[32,8,4608]{2,1,0:T(8,128)(2,1)S(1)}, u32[]{:S(2)}, u32[]{:S(2)}) async-start(bf16[32,8,4608]{2,1,0:T(8,128)(2,1)} %bitcast.23), calls=%async_computation.3 | async-start | bytes 4718592 | tf_op jit(solution)/shard_map/all_to_all | solution.py:480
  104.7 9.1 %collective-permute-start.4 = (bf16[8,2944]{1,0:T(8,128)(2,1)S(1)}, bf16[8,2944]{1,0:T(8,128)(2,1)S(1)}, u32[]{:S(2)}, u32[]{:S(2)}) collective-permute-start(bf16[8,2944]{1,0:T(8,128)(2,1)S(1)} %add_convert_fusion.2), channel_id=1, source_target_pairs={{128,0},{416,32},{192,64},{480,96},{0,128},{288,160},{64,192},{352... | collective-permute-start | bytes 141320 | tf_op jit(solution)/shard_map/ppermute | solution.py:456
  113.8 3.1 %collective-permute-done.4 = bf16[8,2944]{1,0:T(8,128)(2,1)S(1)} collective-permute-done((bf16[8,2944]{1,0:T(8,128)(2,1)S(1)}, bf16[8,2944]{1,0:T(8,128)(2,1)S(1)}, u32[]{:S(2)}, u32[]{:S(2)}) %collective-permute-start.4) | collective-permute-done | bytes 47136 | tf_op jit(solution)/shard_map/ppermute | solution.py:456
  116.9 7.8 %collective-permute-start.5 = (bf16[8,2944]{1,0:T(8,128)(2,1)S(1)}, bf16[8,2944]{1,0:T(8,128)(2,1)S(1)}, u32[]{:S(2)}, u32[]{:S(2)}) collective-permute-start(bf16[8,2944]{1,0:T(8,128)(2,1)S(1)} %add_convert_fusion.1), channel_id=1, source_target_pairs={{448,0},{224,32},{384,64},{160,96},{320,128},{96,160},{256,192},{3... | collective-permute-start | bytes 141320 | tf_op jit(solution)/shard_map/ppermute | solution.py:456
  124.8 2.4 %collective-permute-done.5 = bf16[8,2944]{1,0:T(8,128)(2,1)S(1)} collective-permute-done((bf16[8,2944]{1,0:T(8,128)(2,1)S(1)}, bf16[8,2944]{1,0:T(8,128)(2,1)S(1)}, u32[]{:S(2)}, u32[]{:S(2)}) %collective-permute-start.5) | collective-permute-done | bytes 47136 | tf_op jit(solution)/shard_map/ppermute | solution.py:456
  127.2 4.8 %collective-permute-start.6 = (bf16[8,2944]{1,0:T(8,128)(2,1)S(1)}, bf16[8,2944]{1,0:T(8,128)(2,1)S(1)}, u32[]{:S(2)}, u32[]{:S(2)}) collective-permute-start(bf16[8,2944]{1,0:T(8,128)(2,1)S(1)} %add_convert_fusion.mine_ref), channel_id=1, source_target_pairs={{32,0},{0,32},{96,64},{64,96},{160,128},{128,160},{224,192},{192,2... | collective-permute-start | bytes 141320 | tf_op jit(solution)/shard_map/ppermute | solution.py:456
  132.1 0.1 pad_add_fusion.place_ref
  132.1 2.0 %collective-permute-done.6.other_ref = bf16[8,2944]{1,0:T(8,128)(2,1)S(1)} collective-permute-done((bf16[8,2944]{1,0:T(8,128)(2,1)S(1)}, bf16[8,2944]{1,0:T(8,128)(2,1)S(1)}, u32[]{:S(2)}, u32[]{:S(2)}) %collective-permute-start.6) | collective-permute-done | bytes 47136 | tf_op jit(solution)/shard_map/ppermute | solution.py:456
  134.1 1.3 finish.1
  135.4 1.4 %unpack.1 = (bf16[256,1152]{1,0:T(8,128)(2,1)}, bf16[256,1152]{1,0:T(8,128)(2,1)}, bf16[256,1152]{1,0:T(8,128)(2,1)}, bf16[256,1152]{1,0:T(8,128)(2,1)}) custom-call(bf16[256,4608]{1,0:T(8,128)(2,1)S(1)} %bitcast.19), custom_call_target="tpu_custom_call" | custom-call | bytes 4718592 | tf_op jit(solution)/shard_map/unpack/pallas_call | solution.py:371
  (9 shorter events, 0.1 us)
Async XLA Ops:
  3.3 9.9 %copy-start = (bf16[1152,36]{0,1:T(8,128)(2,1)S(1)}, bf16[1152,36]{0,1:T(8,128)(2,1)}, u32[]{:S(2)}) copy-start(bf16[1152,36]{0,1:T(8,128)(2,1)} %param.10) | copy-start | bytes 248836
  3.3 11.7 %copy-start.1 = (s32[1,4]{1,0:T(1,128)S(1)}, s32[1,4]{1,0:T(1,128)}, u32[]{:S(2)}) copy-start(s32[1,4]{1,0:T(1,128)} %lens_ref.1) | copy-start | bytes 52
  3.3 38.9 %all-to-all-start = ((bf16[32,8,4608]{2,1,0:T(8,128)(2,1)}), bf16[32,8,4608]{2,1,0:T(8,128)(2,1)S(1)}, u32[]{:S(2)}, u32[]{:S(2)}) async-start(bf16[32,8,4608]{2,1,0:T(8,128)(2,1)} %bitcast.21), calls=%async_computation | async-start | bytes 4718592 | tf_op jit(solution)/shard_map/all_to_all | solution.py:480
  42.2 7.4 %copy-start.2 = (bf16[32,8,4608]{2,1,0:T(8,128)(2,1)}, bf16[32,8,4608]{2,1,0:T(8,128)(2,1)S(1)}, u32[]{:S(2)}) copy-start(bf16[32,8,4608]{2,1,0:T(8,128)(2,1)S(1)} %all-to-all-done) | copy-start | bytes 7077892
  42.2 26.1 %all-to-all-start.2 = ((bf16[32,8,2688]{2,1,0:T(8,128)(2,1)}), bf16[32,8,2688]{2,1,0:T(8,128)(2,1)}, u32[]{:S(2)}, u32[]{:S(2)}) async-start(bf16[32,8,2688]{2,1,0:T(8,128)(2,1)} %bitcast.22), calls=%async_computation.2 | async-start | bytes 2752512 | tf_op jit(solution)/shard_map/all_to_all | solution.py:480
  56.2 4.3 %collective-permute-start = (bf16[8,40,1152]{2,1,0:T(8,128)(2,1)}, bf16[8,40,1152]{2,1,0:T(8,128)(2,1)S(1)}, u32[]{:S(2)}, u32[]{:S(2)}) collective-permute-start(bf16[8,40,1152]{2,1,0:T(8,128)(2,1)} %get-tuple-element.22), channel_id=1, source_target_pairs={{0,1},{1,0},{2,3},{3,2},{4,5},{5,4},{6,7},{7,6},{8,9},{9,8},{10,11... | collective-permute-start | bytes 2211848 | tf_op jit(solution)/shard_map/ppermute | solution.py:483
  58.3 4.3 %collective-permute-start.1 = (bf16[8,40,1152]{2,1,0:T(8,128)(2,1)}, bf16[8,40,1152]{2,1,0:T(8,128)(2,1)S(1)}, u32[]{:S(2)}, u32[]{:S(2)}) collective-permute-start(bf16[8,40,1152]{2,1,0:T(8,128)(2,1)} %get-tuple-element.23), channel_id=1, source_target_pairs={{0,1},{1,0},{2,3},{3,2},{4,5},{5,4},{6,7},{7,6},{8,9},{9,8},{10,11... | collective-permute-start | bytes 2211848 | tf_op jit(solution)/shard_map/ppermute | solution.py:483
  68.3 26.9 %all-to-all-start.1 = ((bf16[32,8,2944]{2,1,0:T(8,128)(2,1)}), bf16[32,8,2944]{2,1,0:T(8,128)(2,1)S(1)}, u32[]{:S(2)}, u32[]{:S(2)}) async-start(bf16[32,8,2944]{2,1,0:T(8,128)(2,1)} %bitcast.8), calls=%async_computation.1 | async-start | bytes 3014656 | tf_op jit(solution)/shard_map/all_to_all | solution.py:497
  74.2 5.2 %collective-permute-start.2 = (bf16[256,2688]{1,0:T(8,128)(2,1)}, bf16[256,2688]{1,0:T(8,128)(2,1)S(1)}, u32[]{:S(2)}, u32[]{:S(2)}) collective-permute-start(bf16[256,2688]{1,0:T(8,128)(2,1)} %bitcast.10.own_hbm), channel_id=1, source_target_pairs={{0,1},{1,0},{2,3},{3,2},{4,5},{5,4},{6,7},{7,6},{8,9},{9,8},{10,11... | collective-permute-start | bytes 4128776 | tf_op jit(solution)/shard_map/ppermute | solution.py:483
  95.4 9.3 %collective-permute-start.3 = (bf16[8,2944]{1,0:T(8,128)(2,1)S(1)}, bf16[8,2944]{1,0:T(8,128)(2,1)S(1)}, u32[]{:S(2)}, u32[]{:S(2)}) collective-permute-start(bf16[8,2944]{1,0:T(8,128)(2,1)S(1)} %total.1), channel_id=1, source_target_pairs={{64,0},{96,32},{0,64},{32,96},{192,128},{224,160},{128,192},{160,2... | collective-permute-start | bytes 141320 | tf_op jit(solution)/shard_map/ppermute | solution.py:456
  99.2 36.2 %all-to-all-start.3 = ((bf16[32,8,4608]{2,1,0:T(8,128)(2,1)}), bf16[32,8,4608]{2,1,0:T(8,128)(2,1)S(1)}, u32[]{:S(2)}, u32[]{:S(2)}) async-start(bf16[32,8,4608]{2,1,0:T(8,128)(2,1)} %bitcast.23), calls=%async_computation.3 | async-start | bytes 4718592 | tf_op jit(solution)/shard_map/all_to_all | solution.py:480
  104.7 12.2 %collective-permute-start.4 = (bf16[8,2944]{1,0:T(8,128)(2,1)S(1)}, bf16[8,2944]{1,0:T(8,128)(2,1)S(1)}, u32[]{:S(2)}, u32[]{:S(2)}) collective-permute-start(bf16[8,2944]{1,0:T(8,128)(2,1)S(1)} %add_convert_fusion.2), channel_id=1, source_target_pairs={{128,0},{416,32},{192,64},{480,96},{0,128},{288,160},{64,192},{352... | collective-permute-start | bytes 141320 | tf_op jit(solution)/shard_map/ppermute | solution.py:456
  116.9 10.3 %collective-permute-start.5 = (bf16[8,2944]{1,0:T(8,128)(2,1)S(1)}, bf16[8,2944]{1,0:T(8,128)(2,1)S(1)}, u32[]{:S(2)}, u32[]{:S(2)}) collective-permute-start(bf16[8,2944]{1,0:T(8,128)(2,1)S(1)} %add_convert_fusion.1), channel_id=1, source_target_pairs={{448,0},{224,32},{384,64},{160,96},{320,128},{96,160},{256,192},{3... | collective-permute-start | bytes 141320 | tf_op jit(solution)/shard_map/ppermute | solution.py:456
  127.2 6.9 %collective-permute-start.6 = (bf16[8,2944]{1,0:T(8,128)(2,1)S(1)}, bf16[8,2944]{1,0:T(8,128)(2,1)S(1)}, u32[]{:S(2)}, u32[]{:S(2)}) collective-permute-start(bf16[8,2944]{1,0:T(8,128)(2,1)S(1)} %add_convert_fusion.mine_ref), channel_id=1, source_target_pairs={{32,0},{0,32},{96,64},{64,96},{160,128},{128,160},{224,192},{192,2... | collective-permute-start | bytes 141320 | tf_op jit(solution)/shard_map/ppermute | solution.py:456

commit v8 on v7

--- a/solution.py
+++ b/solution.py
@@ -83,6 +83,7 @@
 JOIN_FLOPS = 10**9
 FINISH_FLOPS = 3 * 10**9
 GROUP = 8
+CUT = 384
 FULL = 16
 ODD = 2
 CHUNK = 3
@@ -188,7 +189,7 @@
 
 
 def forward_kernel(
-    core_ref, x_hbm, bias_ref, mixed_ref, keep_ref, first_ref, second_ref, x_ref, part_ref, held_ref, sems
+    core_ref, x_hbm, bias_ref, mixed_ref, keep_ref, first_ref, second_ref, x_ref, part_ref, held_ref, turn_ref, sems
 ):
     rows, width = mixed_ref.shape
     middle = lane_half(width)
@@ -214,57 +215,73 @@
         raised, recip = softmax(query_win, key_win, bias)
         mixed_tiles.add(head, dot((raised * recip).astype(BF16), value_win))
     copies = []
+    turn_ref[...] = jnp.zeros_like(turn_ref)
     fetches[6].wait()
     mixed = mixed_ref[...]
     block = 3 * LANES
     for at in range(0, width, block):
         part_ref[pl.ds(at, block), :] = dot_tn(x_ref[:, pl.ds(3 * width + at, block)], mixed)
-    chips, pitch, _ = held_ref.shape
-    own = core_ref[0] * (width // chips - pitch)
-    other = (width // chips - pitch) - own
+    chips = held_ref.shape[0]
+    shard = width // chips // 2
+
+    def fold(ids, out_ref, other):
+        for core in range(2):
+
+            @pl.when(core_ref[0] == core)
+            def _():
+                for j in ids:
+                    fold_rows(part_ref, (2 * j + (core ^ other)) * shard, shard, out_ref, j, turn_ref)
+
     for step in range(4):
         some = chips // 4
-        for j in range(step * some, (step + 1) * some):
-            at = pl.multiple_of(j * (width // chips) + other, 8)
-            held_ref[j] = part_ref[pl.ds(at, pitch), :].astype(BF16)
+        fold(range(step * some, (step + 1) * some), held_ref, 1)
         source, place = pl.ds(step * some, some), pl.ds(step % 2 * some, some)
         send_ref = first_ref if step < 2 else second_ref
         copies.append(pltpu.make_async_copy(held_ref.at[source], send_ref.at[place], sems.at[step]))
         copies[-1].start()
-    for j in range(chips):
-        at = pl.multiple_of(j * (width // chips) + own, 8)
-        keep_ref[j] = part_ref[pl.ds(at, pitch), :].astype(BF16)
+    fold(range(chips), keep_ref, 0)
     for copy in copies:
         copy.wait()
 
 
+def fold_rows(part_ref, at, shard, out_ref, j, turn_ref):
+    width = part_ref.shape[1]
+    size = lane_half(width)
+    for group in range(shard // 8):
+        rows = part_ref[pl.ds(at + group * 8, 8), :]
+        out_ref[j, :, pl.ds(group * width, width)] = rows.astype(BF16)
+    last = part_ref[pl.ds(at + shard // 8 * 8, 4), :]
+    turn_ref[pl.ds(0, 4), :] = last[:, :size]
+    turn_ref[pl.ds(4, 4), pl.ds(0, width - size)] = last[:, size:]
+    out_ref[j, :, pl.ds(shard // 8 * width, size)] = turn_ref[...].astype(BF16)
+
+
 def join_kernel(keep_ref, first_ref, second_ref, out_ref):
-    width = keep_ref.shape[2]
-    size = lane_half(width)
+    lanes, total = out_ref.shape[3], keep_ref.shape[2]
+    whole = lanes - CUT
     half = first_ref.shape[0]
     for at, ref in ((0, first_ref), (half, second_ref)):
         ids = pl.ds(at, half)
-        total = keep_ref[ids].astype(F32) + ref[...].astype(F32)
-        groups = [total[:, i * 8 : i * 8 + 8, :].astype(BF16) for i in range(5)]
-        for d, whole, rest in ((0, (0, 1), groups[2][:, :, :size]), (1, (3, 4), groups[2][:, :, width - size :])):
-            for i, group in enumerate(whole):
-                out_ref[d, ids, :, pl.ds(i * width, width)] = groups[group]
-            out_ref[d, ids, :, pl.ds(2 * width, size)] = rest
-
-
-def finish_kernel(place_ref, mine_ref, other_ref, out_ref, held_ref):
-    shard, width = out_ref.shape
+        added = (keep_ref[ids].astype(F32) + ref[...].astype(F32)).astype(BF16)
+        out_ref[0, ids, :, pl.ds(0, whole)] = added[:, :, :whole]
+        out_ref[1, ids, :, pl.ds(0, whole)] = added[:, :, whole : 2 * whole]
+        rest = pl.ds(whole, lanes - whole)
+        out_ref[0, ids, :, rest] = added[:, :, 2 * whole : whole + lanes]
+        out_ref[1, ids, :, rest] = added[:, :, total - (lanes - whole) :]
+
+
+def finish_kernel(place_ref, mine_ref, other_ref, out_ref):
+    width = out_ref.shape[1]
     size = lane_half(width)
     mine, other = mine_ref[...].astype(F32), other_ref[...].astype(F32)
     low = place_ref[0] == 0
     lower, upper = jnp.where(low, mine, other), jnp.where(low, other, mine)
-    for half, groups in ((lower, (0, 1)), (upper, (3, 4))):
-        for i, group in enumerate(groups):
-            held_ref[pl.ds(group * 8, 8), :] = half[:, i * width : (i + 1) * width]
-    held_ref[pl.ds(16, 8), pl.ds(0, size)] = lower[:, 2 * width :]
-    held_ref[pl.ds(16, 8), pl.ds(size, width - size)] = upper[:, 2 * width + 2 * size - width :]
-    rows = held_ref.shape[0]
-    out_ref[...] = jnp.where(place_ref[1] == 0, held_ref[pl.ds(0, shard), :], held_ref[pl.ds(rows - shard, shard), :])
+    for group, half in enumerate((lower, lower, upper, upper)):
+        at = group % 2 * width
+        out_ref[pl.ds(group * 8, 8), :] = half[:, at : at + width]
+    turned = jnp.concatenate([lower[:, 2 * width :], upper[:, 2 * width + 2 * CUT - size :]], axis=1)
+    out_ref[pl.ds(32, 4), pl.ds(0, size)] = turned[:4]
+    out_ref[pl.ds(32, 4), pl.ds(size, width - size)] = turned[4:, : width - size]
 
 
 def backward_kernel(
@@ -414,19 +431,19 @@
 
 def forward(core, x, bias, width, chips):
     rows = x.shape[0]
-    pitch = -(-width // chips // 2 // 8) * 8
-    part, half = (chips, pitch, width), (chips // 2, pitch, width)
+    folded = 4 * width + lane_half(width)
+    part, half = (chips, 8, folded), (chips // 2, 8, folded)
     outs = [((rows, width), BF16), (part, BF16), (half, BF16), (half, BF16)]
-    scratch = [pltpu.VMEM(x.shape, BF16), pltpu.VMEM((width, width), F32), pltpu.VMEM(part, BF16), dma(12)]
+    scratch = [pltpu.VMEM(x.shape, BF16), pltpu.VMEM((width, width), F32), pltpu.VMEM(part, BF16)]
+    scratch += [pltpu.VMEM((8, lane_half(width)), F32), dma(12)]
     args = (core, x, bias)
     return call(
         forward_kernel, "forward", outs, args, smem=1, hbm_in=1, hbm_out=(2, 3), scratch=scratch, flops=FWD_FLOPS
     )
 
 
-def join(keep, first, second):
-    chips, pitch, width = keep.shape
-    outs = [((2, chips, 8, 2 * width + lane_half(width)), BF16)]
+def join(keep, first, second, width):
+    outs = [((2, keep.shape[0], 8, 2 * width + CUT), BF16)]
     return call(join_kernel, "join", outs, (keep, first, second), flops=JOIN_FLOPS)[0]
 
 
@@ -466,8 +483,7 @@
 
     block = added(added(added(block, lambda i: i ^ 2), second), third)
     args = (place, block, exchange(block, lambda i: i ^ 1))
-    scratch = [pltpu.VMEM((40, width), F32)]
-    return call(finish_kernel, "finish", [((shard, width), F32)], args, smem=1, scratch=scratch, flops=FINISH_FLOPS)[0]
+    return call(finish_kernel, "finish", [((shard, width), F32)], args, smem=1, flops=FINISH_FLOPS)[0]
 
 
 def on_device(n_seq, n_dp, queries, key_vectors, value_vectors, out_grad, out_weight, clip_frames):
@@ -489,7 +505,7 @@
     pick, bias = tables(core.reshape(1), clip_frames, patches, width, shard, positions)
     mixed, keep, *send = forward(core.reshape(1), x, bias, width, n_seq // 2)
 
-    chip = join(keep, *[partner(block) for block in send])
+    chip = join(keep, *[partner(block) for block in send], width)
     chip = chip.reshape(n_seq, *chip.shape[2:])
     pairs = [
         [(p + d) * n_seq + i for d in (0, 1) for i in range(c, n_seq, 2)] for p in range(0, n_dp, 2) for c in (0, 1)
@@ -499,7 +515,7 @@
     y = backward(pick, x, own, partner(own), bias, mixed)
     total, y = lax.optimization_barrier((total_of(parts), y))
     back = swap(y).reshape(patches, 4 * width)
-    place = jnp.stack([jnp.bitwise_and(lax.axis_index("dp"), 1).astype(jnp.int32), core])
+    place = jnp.bitwise_and(lax.axis_index("dp"), 1).astype(jnp.int32).reshape(1)
     weight_grad = sum_over_pairs(total, place, shard, width, n_dp).T
     outs = [out.reshape(queries.shape) for out in unpack(back, 4)]
     return (*outs, weight_grad)

time: 139 us -> 141 us (1.014)
  the two profiles are of different devices: /device:TPU:6 before, /device:TPU:1 now
where the time goes in v8:
time: 141 us; the launch traced here: 140 us
  starting transfers between devices  59.3 us (42%)
  waiting for transfers between devices  47.2 us (33%)
  Pallas kernels  30.8 us (22%)
  local copies, waits for them, and re-layouts  1.45 us (1%)
    all_to_all x3, waiting for transfers between devices, swap(): lax.all_to_all(block.reshape(n_seq, positions, -1), 'seq', 0, 0, tiled=True)  35.9 us
    pallas_call x9, Pallas kernels, call(): pl.pallas_call(kernel, out_shape=[pltpu.HBM(s.shape, s.dtype) if i in hbm...  30.8 us
    ppermute x4, starting transfers between devices, exchange(): lax.ppermute(block, 'dp', [(source(i) % n_dp, i) for i in range(n_dp)])  24.8 us
    all_to_all x3, starting transfers between devices, swap(): lax.all_to_all(block.reshape(n_seq, positions, -1), 'seq', 0, 0, tiled=True)  23.7 us
    ppermute x3, starting transfers between devices, partner(): return lax.ppermute(block, 'seq', [(i, i ^ 1) for i in range(n_seq)])  6.87 us
    ppermute x4, waiting for transfers between devices, exchange(): lax.ppermute(block, 'dp', [(source(i) % n_dp, i) for i in range(n_dp)])  6.24 us
    ppermute x3, waiting for transfers between devices, partner(): return lax.ppermute(block, 'seq', [(i, i ^ 1) for i in range(n_seq)])  5.03 us
    all_to_all x1, starting transfers between devices, on_device(): lax.all_to_all(chip, ('dp', 'seq'), 0, 0, tiled=True, axis_index_groups=p...  3.96 us
  transfers between devices with their start and end apart: 11, of which 8 were waited for; matrix products, arithmetic and copies ran while one was open for 0% of the time, Pallas kernels for 19%

profile of v8, /device:TPU:1, one launch (start us, length us, event | category | flops | bytes accessed | tf_op | source)
XLA Modules:
  0.0 139.8 jit_solution(8313787619963167605)
XLA Ops:
  0.6 2.6 %pack.1 = bf16[256,4608]{1,0:T(8,128)(2,1)} custom-call(bf16[256,1152]{1,0:T(8,128)(2,1)} %bitcast.26, bf16[256,1152]{1,0:T(8,128)(2,1)} %bitcast.27, bf16[256,1152]{1,0:T(8,128)(2,1)} %bitcast.28, bf16[256,1152]{1,0:T(8,128)(2,1)} %bitcast.29), custom_call_target="tpu_custom_call" | custom-call | bytes 4718592 | tf_op jit(solution)/shard_map/pack/pallas_call | solution.py:388
  3.3 0.0 copy-start
  3.3 10.7 %all-to-all-start = ((bf16[32,8,4608]{2,1,0:T(8,128)(2,1)}), bf16[32,8,4608]{2,1,0:T(8,128)(2,1)S(1)}, u32[]{:S(2)}, u32[]{:S(2)}) async-start(bf16[32,8,4608]{2,1,0:T(8,128)(2,1)} %bitcast.21), calls=%async_computation | async-start | bytes 4718592 | tf_op jit(solution)/shard_map/all_to_all | solution.py:496
  14.0 0.0 copy-start.1
  14.0 1.8 %spread.1 = bf16[256,2688]{1,0:T(8,128)(2,1)} custom-call(bf16[36,1152]{1,0:T(8,128)(2,1)S(1)} %bitcast.20), custom_call_target="tpu_custom_call" | custom-call | bytes 1459200 | tf_op jit(solution)/shard_map/spread/pallas_call | solution.py:388
  15.9 2.6 %tables.1 = (bf16[1152,1152]{1,0:T(8,128)(2,1)}, f32[256,256]{1,0:T(8,128)S(1)}) custom-call(s32[1]{0:T(128)} %bitcast.core_ref, s32[1,4]{1,0:T(1,128)S(1)} %copy-done.1), custom_call_target="tpu_custom_call" | custom-call | bytes 2916372 | tf_op jit(solution)/shard_map/tables/pallas_call | solution.py:388
  18.5 26.7 %all-to-all-done = bf16[32,8,4608]{2,1,0:T(8,128)(2,1)S(1)} async-done(((bf16[32,8,4608]{2,1,0:T(8,128)(2,1)}), bf16[32,8,4608]{2,1,0:T(8,128)(2,1)S(1)}, u32[]{:S(2)}, u32[]{:S(2)}) %all-to-all-start) | async-done | bytes 2359328 | tf_op jit(solution)/shard_map/all_to_all | solution.py:496
  45.2 1.4 %copy-done.2 = bf16[32,8,4608]{2,1,0:T(8,128)(2,1)} copy-done((bf16[32,8,4608]{2,1,0:T(8,128)(2,1)}, bf16[32,8,4608]{2,1,0:T(8,128)(2,1)S(1)}, u32[]{:S(2)}) %copy-start.2) | copy-done | bytes 2359320
  46.6 5.2 %all-to-all-start.2 = ((bf16[32,8,2688]{2,1,0:T(8,128)(2,1)}), bf16[32,8,2688]{2,1,0:T(8,128)(2,1)}, u32[]{:S(2)}, u32[]{:S(2)}) async-start(bf16[32,8,2688]{2,1,0:T(8,128)(2,1)} %bitcast.22), calls=%async_computation.2 | async-start | bytes 2752512 | tf_op jit(solution)/shard_map/all_to_all | solution.py:496
  51.8 6.6 %forward.1 = (bf16[256,1152]{1,0:T(8,128)(2,1)S(1)}, bf16[16,8,5248]{2,1,0:T(8,128)(2,1)S(1)}, bf16[8,8,5248]{2,1,0:T(8,128)(2,1)}, bf16[8,8,5248]{2,1,0:T(8,128)(2,1)}) custom-call(s32[1]{0:T(128)} %bitcast.core_ref, bf16[256,4608]{1,0:T(8,128)(2,1)} %bitcast.23, f32[256,256]{1,0:T(8,128)S(1)} %get-tuple-element.20.bias_ref), custom_call_target="tpu_custom_call" | custom-call | flops 99999997952 | tf_op jit(solution)/shard_map/forward/pallas_call | solution.py:388
  58.4 2.4 %collective-permute-start = (bf16[8,8,5248]{2,1,0:T(8,128)(2,1)}, bf16[8,8,5248]{2,1,0:T(8,128)(2,1)S(1)}, u32[]{:S(2)}, u32[]{:S(2)}) collective-permute-start(bf16[8,8,5248]{2,1,0:T(8,128)(2,1)} %get-tuple-element.22), channel_id=1, source_target_pairs={{0,1},{1,0},{2,3},{3,2},{4,5},{5,4},{6,7},{7,6},{8,9},{9,8},{10,11... | collective-permute-start | bytes 2015240 | tf_op jit(solution)/shard_map/ppermute | solution.py:499
  60.8 1.9 %collective-permute-start.1 = (bf16[8,8,5248]{2,1,0:T(8,128)(2,1)}, bf16[8,8,5248]{2,1,0:T(8,128)(2,1)S(1)}, u32[]{:S(2)}, u32[]{:S(2)}) collective-permute-start(bf16[8,8,5248]{2,1,0:T(8,128)(2,1)} %get-tuple-element.23), channel_id=1, source_target_pairs={{0,1},{1,0},{2,3},{3,2},{4,5},{5,4},{6,7},{7,6},{8,9},{9,8},{10,11... | collective-permute-start | bytes 2015240 | tf_op jit(solution)/shard_map/ppermute | solution.py:499
  62.8 0.0 collective-permute-done.first_ref
  62.8 2.3 %collective-permute-done.1.second_ref = bf16[8,8,5248]{2,1,0:T(8,128)(2,1)S(1)} collective-permute-done((bf16[8,8,5248]{2,1,0:T(8,128)(2,1)}, bf16[8,8,5248]{2,1,0:T(8,128)(2,1)S(1)}, u32[]{:S(2)}, u32[]{:S(2)}) %collective-permute-start.1) | collective-permute-done | bytes 671776 | tf_op jit(solution)/shard_map/ppermute | solution.py:499
  65.1 1.4 %join.1 = bf16[2,16,8,2688]{3,2,1,0:T(8,128)(2,1)} custom-call(bf16[16,8,5248]{2,1,0:T(8,128)(2,1)S(1)} %get-tuple-element.21.keep_ref, bf16[8,8,5248]{2,1,0:T(8,128)(2,1)S(1)} %collective-permute-done.first_ref, bf16[8,8,5248]{2,1,0:T(8,128)(2,1)S(1)} %collective-permute-done.1.second_ref), custom_call_target="tpu_custom_call" | custom-call | flops 1000000000 | tf_op jit(solution)/shard_map/join/pallas_call | solution.py:388
  66.5 6.0 %all-to-all-done.2 = bf16[32,8,2688]{2,1,0:T(8,128)(2,1)} async-done(((bf16[32,8,2688]{2,1,0:T(8,128)(2,1)}), bf16[32,8,2688]{2,1,0:T(8,128)(2,1)}, u32[]{:S(2)}, u32[]{:S(2)}) %all-to-all-start.2) | async-done | bytes 1376288 | tf_op jit(solution)/shard_map/all_to_all | solution.py:496
  72.5 4.0 %all-to-all-start.1 = ((bf16[32,8,2688]{2,1,0:T(8,128)(2,1)}), bf16[32,8,2688]{2,1,0:T(8,128)(2,1)S(1)}, u32[]{:S(2)}, u32[]{:S(2)}) async-start(bf16[32,8,2688]{2,1,0:T(8,128)(2,1)} %bitcast.8), calls=%async_computation.1 | async-start | bytes 2752512 | tf_op jit(solution)/shard_map/all_to_all | solution.py:513
  76.5 2.5 %collective-permute-start.2 = (bf16[256,2688]{1,0:T(8,128)(2,1)}, bf16[256,2688]{1,0:T(8,128)(2,1)S(1)}, u32[]{:S(2)}, u32[]{:S(2)}) collective-permute-start(bf16[256,2688]{1,0:T(8,128)(2,1)} %bitcast.10.own_hbm), channel_id=1, source_target_pairs={{0,1},{1,0},{2,3},{3,2},{4,5},{5,4},{6,7},{7,6},{8,9},{9,8},{10,11... | collective-permute-start | bytes 4128776 | tf_op jit(solution)/shard_map/ppermute | solution.py:499
  79.0 2.8 %collective-permute-done.2.other_ref = bf16[256,2688]{1,0:T(8,128)(2,1)S(1)} collective-permute-done((bf16[256,2688]{1,0:T(8,128)(2,1)}, bf16[256,2688]{1,0:T(8,128)(2,1)S(1)}, u32[]{:S(2)}, u32[]{:S(2)}) %collective-permute-start.2) | collective-permute-done | bytes 1376288 | tf_op jit(solution)/shard_map/ppermute | solution.py:499
  81.8 13.4 %backward.1 = bf16[256,4608]{1,0:T(8,128)(2,1)} custom-call(bf16[1152,1152]{1,0:T(8,128)(2,1)} %get-tuple-element.24.pick_hbm, bf16[256,4608]{1,0:T(8,128)(2,1)} %bitcast.24, bf16[256,2688]{1,0:T(8,128)(2,1)} %bitcast.10.own_hbm, bf16[256,2688]{1,0:T(8,128)(2,1)S(1)} %collective-permute-done.2.other_ref, f32[256,256]{1,0:T(8,128)S(1)} %get-tuple-element.20.bias_ref, ...), custom_call_target="tpu_custom_call" | custom-call | flops 5939134464 | tf_op jit(solution)/shard_map/backward/pallas_call | solution.py:388
  95.2 0.2 total.1
  95.4 3.8 %collective-permute-start.3 = (bf16[8,2688]{1,0:T(8,128)(2,1)S(1)}, bf16[8,2688]{1,0:T(8,128)(2,1)S(1)}, u32[]{:S(2)}, u32[]{:S(2)}) collective-permute-start(bf16[8,2688]{1,0:T(8,128)(2,1)S(1)} %total.1), channel_id=1, source_target_pairs={{64,0},{96,32},{0,64},{32,96},{192,128},{224,160},{128,192},{160,2... | collective-permute-start | bytes 129032 | tf_op jit(solution)/shard_map/ppermute | solution.py:473
  99.3 7.8 %all-to-all-start.3 = ((bf16[32,8,4608]{2,1,0:T(8,128)(2,1)}), bf16[32,8,4608]{2,1,0:T(8,128)(2,1)S(1)}, u32[]{:S(2)}, u32[]{:S(2)}) async-start(bf16[32,8,4608]{2,1,0:T(8,128)(2,1)} %bitcast.25), calls=%async_computation.3 | async-start | bytes 4718592 | tf_op jit(solution)/shard_map/all_to_all | solution.py:496
  107.1 8.8 %collective-permute-start.4 = (bf16[8,2688]{1,0:T(8,128)(2,1)S(1)}, bf16[8,2688]{1,0:T(8,128)(2,1)S(1)}, u32[]{:S(2)}, u32[]{:S(2)}) collective-permute-start(bf16[8,2688]{1,0:T(8,128)(2,1)S(1)} %add_convert_fusion.2), channel_id=1, source_target_pairs={{128,0},{416,32},{192,64},{480,96},{0,128},{288,160},{64,192},{352... | collective-permute-start | bytes 129032 | tf_op jit(solution)/shard_map/ppermute | solution.py:473
  115.9 2.9 %collective-permute-done.4 = bf16[8,2688]{1,0:T(8,128)(2,1)S(1)} collective-permute-done((bf16[8,2688]{1,0:T(8,128)(2,1)S(1)}, bf16[8,2688]{1,0:T(8,128)(2,1)S(1)}, u32[]{:S(2)}, u32[]{:S(2)}) %collective-permute-start.4) | collective-permute-done | bytes 43040 | tf_op jit(solution)/shard_map/ppermute | solution.py:473
  118.8 5.8 %collective-permute-start.5 = (bf16[8,2688]{1,0:T(8,128)(2,1)S(1)}, bf16[8,2688]{1,0:T(8,128)(2,1)S(1)}, u32[]{:S(2)}, u32[]{:S(2)}) collective-permute-start(bf16[8,2688]{1,0:T(8,128)(2,1)S(1)} %add_convert_fusion.1), channel_id=1, source_target_pairs={{448,0},{224,32},{384,64},{160,96},{320,128},{96,160},{256,192},{3... | collective-permute-start | bytes 129032 | tf_op jit(solution)/shard_map/ppermute | solution.py:473
  124.7 1.7 %collective-permute-done.5 = bf16[8,2688]{1,0:T(8,128)(2,1)S(1)} collective-permute-done((bf16[8,2688]{1,0:T(8,128)(2,1)S(1)}, bf16[8,2688]{1,0:T(8,128)(2,1)S(1)}, u32[]{:S(2)}, u32[]{:S(2)}) %collective-permute-start.5) | collective-permute-done | bytes 43040 | tf_op jit(solution)/shard_map/ppermute | solution.py:473
  126.4 6.3 %collective-permute-start.6 = (bf16[8,2688]{1,0:T(8,128)(2,1)S(1)}, bf16[8,2688]{1,0:T(8,128)(2,1)S(1)}, u32[]{:S(2)}, u32[]{:S(2)}) collective-permute-start(bf16[8,2688]{1,0:T(8,128)(2,1)S(1)} %add_convert_fusion.mine_ref), channel_id=1, source_target_pairs={{32,0},{0,32},{96,64},{64,96},{160,128},{128,160},{224,192},{192,2... | collective-permute-start | bytes 129032 | tf_op jit(solution)/shard_map/ppermute | solution.py:473
  132.6 1.7 %collective-permute-done.6.other_ref = bf16[8,2688]{1,0:T(8,128)(2,1)S(1)} collective-permute-done((bf16[8,2688]{1,0:T(8,128)(2,1)S(1)}, bf16[8,2688]{1,0:T(8,128)(2,1)S(1)}, u32[]{:S(2)}, u32[]{:S(2)}) %collective-permute-start.6) | collective-permute-done | bytes 43040 | tf_op jit(solution)/shard_map/ppermute | solution.py:473
  134.3 0.7 finish.1
  135.0 3.2 %all-to-all-done.3 = bf16[32,8,4608]{2,1,0:T(8,128)(2,1)S(1)} async-done(((bf16[32,8,4608]{2,1,0:T(8,128)(2,1)}), bf16[32,8,4608]{2,1,0:T(8,128)(2,1)S(1)}, u32[]{:S(2)}, u32[]{:S(2)}) %all-to-all-start.3) | async-done | bytes 2359328 | tf_op jit(solution)/shard_map/all_to_all | solution.py:496
  138.2 1.4 %unpack.1 = (bf16[256,1152]{1,0:T(8,128)(2,1)}, bf16[256,1152]{1,0:T(8,128)(2,1)}, bf16[256,1152]{1,0:T(8,128)(2,1)}, bf16[256,1152]{1,0:T(8,128)(2,1)}) custom-call(bf16[256,4608]{1,0:T(8,128)(2,1)S(1)} %bitcast.19), custom_call_target="tpu_custom_call" | custom-call | bytes 4718592 | tf_op jit(solution)/shard_map/unpack/pallas_call | solution.py:388
  (8 shorter events, 0.1 us)
Async XLA Ops:
  3.3 10.8 %copy-start = (bf16[1152,36]{0,1:T(8,128)(2,1)S(1)}, bf16[1152,36]{0,1:T(8,128)(2,1)}, u32[]{:S(2)}) copy-start(bf16[1152,36]{0,1:T(8,128)(2,1)} %param.10) | copy-start | bytes 248836
  3.3 41.9 %all-to-all-start = ((bf16[32,8,4608]{2,1,0:T(8,128)(2,1)}), bf16[32,8,4608]{2,1,0:T(8,128)(2,1)S(1)}, u32[]{:S(2)}, u32[]{:S(2)}) async-start(bf16[32,8,4608]{2,1,0:T(8,128)(2,1)} %bitcast.21), calls=%async_computation | async-start | bytes 4718592 | tf_op jit(solution)/shard_map/all_to_all | solution.py:496
  14.0 1.9 %copy-start.1 = (s32[1,4]{1,0:T(1,128)S(1)}, s32[1,4]{1,0:T(1,128)}, u32[]{:S(2)}) copy-start(s32[1,4]{1,0:T(1,128)} %lens_ref.1) | copy-start | bytes 52
  45.2 1.4 %copy-start.2 = (bf16[32,8,4608]{2,1,0:T(8,128)(2,1)}, bf16[32,8,4608]{2,1,0:T(8,128)(2,1)S(1)}, u32[]{:S(2)}) copy-start(bf16[32,8,4608]{2,1,0:T(8,128)(2,1)S(1)} %all-to-all-done) | copy-start | bytes 7077892
  46.6 25.9 %all-to-all-start.2 = ((bf16[32,8,2688]{2,1,0:T(8,128)(2,1)}), bf16[32,8,2688]{2,1,0:T(8,128)(2,1)}, u32[]{:S(2)}, u32[]{:S(2)}) async-start(bf16[32,8,2688]{2,1,0:T(8,128)(2,1)} %bitcast.22), calls=%async_computation.2 | async-start | bytes 2752512 | tf_op jit(solution)/shard_map/all_to_all | solution.py:496
  58.4 4.3 %collective-permute-start = (bf16[8,8,5248]{2,1,0:T(8,128)(2,1)}, bf16[8,8,5248]{2,1,0:T(8,128)(2,1)S(1)}, u32[]{:S(2)}, u32[]{:S(2)}) collective-permute-start(bf16[8,8,5248]{2,1,0:T(8,128)(2,1)} %get-tuple-element.22), channel_id=1, source_target_pairs={{0,1},{1,0},{2,3},{3,2},{4,5},{5,4},{6,7},{7,6},{8,9},{9,8},{10,11... | collective-permute-start | bytes 2015240 | tf_op jit(solution)/shard_map/ppermute | solution.py:499
  60.8 4.2 %collective-permute-start.1 = (bf16[8,8,5248]{2,1,0:T(8,128)(2,1)}, bf16[8,8,5248]{2,1,0:T(8,128)(2,1)S(1)}, u32[]{:S(2)}, u32[]{:S(2)}) collective-permute-start(bf16[8,8,5248]{2,1,0:T(8,128)(2,1)} %get-tuple-element.23), channel_id=1, source_target_pairs={{0,1},{1,0},{2,3},{3,2},{4,5},{5,4},{6,7},{7,6},{8,9},{9,8},{10,11... | collective-permute-start | bytes 2015240 | tf_op jit(solution)/shard_map/ppermute | solution.py:499
  72.5 22.7 %all-to-all-start.1 = ((bf16[32,8,2688]{2,1,0:T(8,128)(2,1)}), bf16[32,8,2688]{2,1,0:T(8,128)(2,1)S(1)}, u32[]{:S(2)}, u32[]{:S(2)}) async-start(bf16[32,8,2688]{2,1,0:T(8,128)(2,1)} %bitcast.8), calls=%async_computation.1 | async-start | bytes 2752512 | tf_op jit(solution)/shard_map/all_to_all | solution.py:513
  76.5 5.3 %collective-permute-start.2 = (bf16[256,2688]{1,0:T(8,128)(2,1)}, bf16[256,2688]{1,0:T(8,128)(2,1)S(1)}, u32[]{:S(2)}, u32[]{:S(2)}) collective-permute-start(bf16[256,2688]{1,0:T(8,128)(2,1)} %bitcast.10.own_hbm), channel_id=1, source_target_pairs={{0,1},{1,0},{2,3},{3,2},{4,5},{5,4},{6,7},{7,6},{8,9},{9,8},{10,11... | collective-permute-start | bytes 4128776 | tf_op jit(solution)/shard_map/ppermute | solution.py:499
  95.4 11.7 %collective-permute-start.3 = (bf16[8,2688]{1,0:T(8,128)(2,1)S(1)}, bf16[8,2688]{1,0:T(8,128)(2,1)S(1)}, u32[]{:S(2)}, u32[]{:S(2)}) collective-permute-start(bf16[8,2688]{1,0:T(8,128)(2,1)S(1)} %total.1), channel_id=1, source_target_pairs={{64,0},{96,32},{0,64},{32,96},{192,128},{224,160},{128,192},{160,2... | collective-permute-start | bytes 129032 | tf_op jit(solution)/shard_map/ppermute | solution.py:473
  99.3 38.9 %all-to-all-start.3 = ((bf16[32,8,4608]{2,1,0:T(8,128)(2,1)}), bf16[32,8,4608]{2,1,0:T(8,128)(2,1)S(1)}, u32[]{:S(2)}, u32[]{:S(2)}) async-start(bf16[32,8,4608]{2,1,0:T(8,128)(2,1)} %bitcast.25), calls=%async_computation.3 | async-start | bytes 4718592 | tf_op jit(solution)/shard_map/all_to_all | solution.py:496
  107.1 11.7 %collective-permute-start.4 = (bf16[8,2688]{1,0:T(8,128)(2,1)S(1)}, bf16[8,2688]{1,0:T(8,128)(2,1)S(1)}, u32[]{:S(2)}, u32[]{:S(2)}) collective-permute-start(bf16[8,2688]{1,0:T(8,128)(2,1)S(1)} %add_convert_fusion.2), channel_id=1, source_target_pairs={{128,0},{416,32},{192,64},{480,96},{0,128},{288,160},{64,192},{352... | collective-permute-start | bytes 129032 | tf_op jit(solution)/shard_map/ppermute | solution.py:473
  118.8 7.5 %collective-permute-start.5 = (bf16[8,2688]{1,0:T(8,128)(2,1)S(1)}, bf16[8,2688]{1,0:T(8,128)(2,1)S(1)}, u32[]{:S(2)}, u32[]{:S(2)}) collective-permute-start(bf16[8,2688]{1,0:T(8,128)(2,1)S(1)} %add_convert_fusion.1), channel_id=1, source_target_pairs={{448,0},{224,32},{384,64},{160,96},{320,128},{96,160},{256,192},{3... | collective-permute-start | bytes 129032 | tf_op jit(solution)/shard_map/ppermute | solution.py:473
  126.4 8.0 %collective-permute-start.6 = (bf16[8,2688]{1,0:T(8,128)(2,1)S(1)}, bf16[8,2688]{1,0:T(8,128)(2,1)S(1)}, u32[]{:S(2)}, u32[]{:S(2)}) collective-permute-start(bf16[8,2688]{1,0:T(8,128)(2,1)S(1)} %add_convert_fusion.mine_ref), channel_id=1, source_target_pairs={{32,0},{0,32},{96,64},{64,96},{160,128},{128,160},{224,192},{192,2... | collective-permute-start | bytes 129032 | tf_op jit(solution)/shard_map/ppermute | solution.py:473

commit v9 on v8

--- a/solution.py
+++ b/solution.py
@@ -189,24 +189,12 @@
 
 
 def forward_kernel(
-    core_ref, x_hbm, bias_ref, mixed_ref, keep_ref, first_ref, second_ref, x_ref, part_ref, held_ref, turn_ref, sems
+    core_ref, x_ref, bias_ref, mixed_ref, keep_ref, first_ref, second_ref, part_ref, held_ref, turn_ref, sems
 ):
     rows, width = mixed_ref.shape
-    middle = lane_half(width)
-    pieces = [(a * width + b, c) for b, c in ((0, middle), (middle, width - middle)) for a in range(3)]
-    pieces.append((3 * width, width))
-    fetches = [
-        pltpu.make_async_copy(x_hbm.at[:, pl.ds(at, size)], x_ref.at[:, pl.ds(at, size)], sems.at[5 + i])
-        for i, (at, size) in enumerate(pieces)
-    ]
-    for fetch in fetches:
-        fetch.start()
     bias = bias_ref[...]
     mixed_tiles = Tiles(mixed_ref)
     for head in range(HEADS):
-        if head in (0, HEADS // 2):
-            for fetch in fetches[3 * (head > 0) : 3 * (head > 0) + 3]:
-                fetch.wait()
         start, size = window(head)
         lanes = head_lanes(head, rows)
         query_win = jnp.where(lanes, x_ref[:, pl.ds(start, size)], 0)
@@ -216,7 +204,6 @@
         mixed_tiles.add(head, dot((raised * recip).astype(BF16), value_win))
     copies = []
     turn_ref[...] = jnp.zeros_like(turn_ref)
-    fetches[6].wait()
     mixed = mixed_ref[...]
     block = 3 * LANES
     for at in range(0, width, block):
@@ -434,11 +421,10 @@
     folded = 4 * width + lane_half(width)
     part, half = (chips, 8, folded), (chips // 2, 8, folded)
     outs = [((rows, width), BF16), (part, BF16), (half, BF16), (half, BF16)]
-    scratch = [pltpu.VMEM(x.shape, BF16), pltpu.VMEM((width, width), F32), pltpu.VMEM(part, BF16)]
-    scratch += [pltpu.VMEM((8, lane_half(width)), F32), dma(12)]
+    scratch = [pltpu.VMEM((width, width), F32), pltpu.VMEM(part, BF16), pltpu.VMEM((8, lane_half(width)), F32), dma(4)]
     args = (core, x, bias)
     return call(
-        forward_kernel, "forward", outs, args, smem=1, hbm_in=1, hbm_out=(2, 3), scratch=scratch, flops=FWD_FLOPS
+        forward_kernel, "forward", outs, args, smem=1, hbm_out=(2, 3), scratch=scratch, flops=FWD_FLOPS
     )
 
 

time: 141 us -> 139 us (0.986)
  Pallas kernels: 30.8 us -> 28.8 us
  waiting for transfers between devices: 47.2 us -> 49.2 us
  local copies, waits for them, and re-layouts: 1.45 us -> 0.02 us
    pallas_call x9, Pallas kernels: 30.8 us -> 28.8 us  [call(): pl.pallas_call(kernel, out_shape=[pltpu.HBM(s.shape, s.dtype) if i in hbm...]
    all_to_all x3, waiting for transfers between devices: 35.9 us -> 37.9 us  [swap(): lax.all_to_all(block.reshape(n_seq, positions, -1), 'seq', 0, 0, tiled=True)]
    unnamed x6, local copies, waits for them, and re-layouts: 1.45 us -> 0.02 us
  transfers between devices with their start and end apart: 11 -> 11, of which waited for: 8 -> 8; matrix products, arithmetic and copies ran while one was open for 0% -> 0% of each run, Pallas kernels for 19% -> 18%
where the time goes in v9:
time: 139 us; the launch traced here: 138 us
  starting transfers between devices  59.3 us (43%)
  waiting for transfers between devices  49.2 us (35%)
  Pallas kernels  28.8 us (21%)
    all_to_all x3, waiting for transfers between devices, swap(): lax.all_to_all(block.reshape(n_seq, positions, -1), 'seq', 0, 0, tiled=True)  37.9 us
    pallas_call x9, Pallas kernels, call(): pl.pallas_call(kernel, out_shape=[pltpu.HBM(s.shape, s.dtype) if i in hbm...  28.8 us
    ppermute x4, starting transfers between devices, exchange(): lax.ppermute(block, 'dp', [(source(i) % n_dp, i) for i in range(n_dp)])  24.8 us
    all_to_all x3, starting transfers between devices, swap(): lax.all_to_all(block.reshape(n_seq, positions, -1), 'seq', 0, 0, tiled=True)  23.7 us
    ppermute x3, starting transfers between devices, partner(): return lax.ppermute(block, 'seq', [(i, i ^ 1) for i in range(n_seq)])  6.87 us
    ppermute x4, waiting for transfers between devices, exchange(): lax.ppermute(block, 'dp', [(source(i) % n_dp, i) for i in range(n_dp)])  6.25 us
    ppermute x3, waiting for transfers between devices, partner(): return lax.ppermute(block, 'seq', [(i, i ^ 1) for i in range(n_seq)])  5.03 us
    all_to_all x1, starting transfers between devices, on_device(): lax.all_to_all(chip, ('dp', 'seq'), 0, 0, tiled=True, axis_index_groups=p...  3.96 us
  transfers between devices with their start and end apart: 11, of which 8 were waited for; matrix products, arithmetic and copies ran while one was open for 0% of the time, Pallas kernels for 18%

profile of v9, /device:TPU:1, one launch (start us, length us, event | category | flops | bytes accessed | tf_op | source)
XLA Modules:
  0.0 138.4 jit_solution(3433298471308685540)
XLA Ops:
  0.6 2.6 %pack.1 = bf16[256,4608]{1,0:T(8,128)(2,1)} custom-call(bf16[256,1152]{1,0:T(8,128)(2,1)} %bitcast.26, bf16[256,1152]{1,0:T(8,128)(2,1)} %bitcast.27, bf16[256,1152]{1,0:T(8,128)(2,1)} %bitcast.28, bf16[256,1152]{1,0:T(8,128)(2,1)} %bitcast.29), custom_call_target="tpu_custom_call" | custom-call | bytes 4718592 | tf_op jit(solution)/shard_map/pack/pallas_call | solution.py:375
  3.3 0.0 copy-start.1
  3.3 10.7 %all-to-all-start = ((bf16[32,8,4608]{2,1,0:T(8,128)(2,1)}), bf16[32,8,4608]{2,1,0:T(8,128)(2,1)S(1)}, u32[]{:S(2)}, u32[]{:S(2)}) async-start(bf16[32,8,4608]{2,1,0:T(8,128)(2,1)} %bitcast.23), calls=%async_computation | async-start | bytes 4718592 | tf_op jit(solution)/shard_map/all_to_all | solution.py:482
  14.0 0.0 copy-start.2
  14.0 1.8 %spread.1 = bf16[256,2688]{1,0:T(8,128)(2,1)} custom-call(bf16[36,1152]{1,0:T(8,128)(2,1)S(1)} %bitcast.22), custom_call_target="tpu_custom_call" | custom-call | bytes 1459200 | tf_op jit(solution)/shard_map/spread/pallas_call | solution.py:375
  15.9 2.6 %tables.1 = (bf16[1152,1152]{1,0:T(8,128)(2,1)}, f32[256,256]{1,0:T(8,128)S(1)}) custom-call(s32[1]{0:T(128)} %bitcast.core_ref, s32[1,4]{1,0:T(1,128)S(1)} %copy-done.2), custom_call_target="tpu_custom_call" | custom-call | bytes 2916372 | tf_op jit(solution)/shard_map/tables/pallas_call | solution.py:375
  18.5 26.7 %all-to-all-done = bf16[32,8,4608]{2,1,0:T(8,128)(2,1)S(1)} async-done(((bf16[32,8,4608]{2,1,0:T(8,128)(2,1)}), bf16[32,8,4608]{2,1,0:T(8,128)(2,1)S(1)}, u32[]{:S(2)}, u32[]{:S(2)}) %all-to-all-start) | async-done | bytes 2359328 | tf_op jit(solution)/shard_map/all_to_all | solution.py:482
  45.2 5.2 %all-to-all-start.2 = ((bf16[32,8,2688]{2,1,0:T(8,128)(2,1)}), bf16[32,8,2688]{2,1,0:T(8,128)(2,1)}, u32[]{:S(2)}, u32[]{:S(2)}) async-start(bf16[32,8,2688]{2,1,0:T(8,128)(2,1)} %bitcast.24), calls=%async_computation.2 | async-start | bytes 2752512 | tf_op jit(solution)/shard_map/all_to_all | solution.py:482
  50.4 4.6 %forward.1 = (bf16[256,1152]{1,0:T(8,128)(2,1)S(1)}, bf16[16,8,5248]{2,1,0:T(8,128)(2,1)S(1)}, bf16[8,8,5248]{2,1,0:T(8,128)(2,1)}, bf16[8,8,5248]{2,1,0:T(8,128)(2,1)}) custom-call(s32[1]{0:T(128)} %bitcast.core_ref, bf16[256,4608]{1,0:T(8,128)(2,1)S(1)} %bitcast.20, f32[256,256]{1,0:T(8,128)S(1)} %get-tuple-element.20.bias_ref), custom_call_target="tpu_custom_call" | custom-call | flops 99999997952 | tf_op jit(solution)/shard_map/forward/pallas_call | solution.py:375
  55.0 2.4 %collective-permute-start = (bf16[8,8,5248]{2,1,0:T(8,128)(2,1)}, bf16[8,8,5248]{2,1,0:T(8,128)(2,1)S(1)}, u32[]{:S(2)}, u32[]{:S(2)}) collective-permute-start(bf16[8,8,5248]{2,1,0:T(8,128)(2,1)} %get-tuple-element.22), channel_id=1, source_target_pairs={{0,1},{1,0},{2,3},{3,2},{4,5},{5,4},{6,7},{7,6},{8,9},{9,8},{10,11... | collective-permute-start | bytes 2015240 | tf_op jit(solution)/shard_map/ppermute | solution.py:485
  57.4 1.9 %collective-permute-start.1 = (bf16[8,8,5248]{2,1,0:T(8,128)(2,1)}, bf16[8,8,5248]{2,1,0:T(8,128)(2,1)S(1)}, u32[]{:S(2)}, u32[]{:S(2)}) collective-permute-start(bf16[8,8,5248]{2,1,0:T(8,128)(2,1)} %get-tuple-element.23), channel_id=1, source_target_pairs={{0,1},{1,0},{2,3},{3,2},{4,5},{5,4},{6,7},{7,6},{8,9},{9,8},{10,11... | collective-permute-start | bytes 2015240 | tf_op jit(solution)/shard_map/ppermute | solution.py:485
  59.4 0.0 collective-permute-done.first_ref
  59.4 2.3 %collective-permute-done.1.second_ref = bf16[8,8,5248]{2,1,0:T(8,128)(2,1)S(1)} collective-permute-done((bf16[8,8,5248]{2,1,0:T(8,128)(2,1)}, bf16[8,8,5248]{2,1,0:T(8,128)(2,1)S(1)}, u32[]{:S(2)}, u32[]{:S(2)}) %collective-permute-start.1) | collective-permute-done | bytes 671776 | tf_op jit(solution)/shard_map/ppermute | solution.py:485
  61.7 1.4 %join.1 = bf16[2,16,8,2688]{3,2,1,0:T(8,128)(2,1)} custom-call(bf16[16,8,5248]{2,1,0:T(8,128)(2,1)S(1)} %get-tuple-element.21.keep_ref, bf16[8,8,5248]{2,1,0:T(8,128)(2,1)S(1)} %collective-permute-done.first_ref, bf16[8,8,5248]{2,1,0:T(8,128)(2,1)S(1)} %collective-permute-done.1.second_ref), custom_call_target="tpu_custom_call" | custom-call | flops 1000000000 | tf_op jit(solution)/shard_map/join/pallas_call | solution.py:375
  63.1 8.0 %all-to-all-done.2 = bf16[32,8,2688]{2,1,0:T(8,128)(2,1)} async-done(((bf16[32,8,2688]{2,1,0:T(8,128)(2,1)}), bf16[32,8,2688]{2,1,0:T(8,128)(2,1)}, u32[]{:S(2)}, u32[]{:S(2)}) %all-to-all-start.2) | async-done | bytes 1376288 | tf_op jit(solution)/shard_map/all_to_all | solution.py:482
  71.1 4.0 %all-to-all-start.1 = ((bf16[32,8,2688]{2,1,0:T(8,128)(2,1)}), bf16[32,8,2688]{2,1,0:T(8,128)(2,1)S(1)}, u32[]{:S(2)}, u32[]{:S(2)}) async-start(bf16[32,8,2688]{2,1,0:T(8,128)(2,1)} %bitcast.8), calls=%async_computation.1 | async-start | bytes 2752512 | tf_op jit(solution)/shard_map/all_to_all | solution.py:499
  75.0 2.5 %collective-permute-start.2 = (bf16[256,2688]{1,0:T(8,128)(2,1)}, bf16[256,2688]{1,0:T(8,128)(2,1)S(1)}, u32[]{:S(2)}, u32[]{:S(2)}) collective-permute-start(bf16[256,2688]{1,0:T(8,128)(2,1)} %bitcast.10.own_hbm), channel_id=1, source_target_pairs={{0,1},{1,0},{2,3},{3,2},{4,5},{5,4},{6,7},{7,6},{8,9},{9,8},{10,11... | collective-permute-start | bytes 4128776 | tf_op jit(solution)/shard_map/ppermute | solution.py:485
  77.6 2.8 %collective-permute-done.2.other_ref = bf16[256,2688]{1,0:T(8,128)(2,1)S(1)} collective-permute-done((bf16[256,2688]{1,0:T(8,128)(2,1)}, bf16[256,2688]{1,0:T(8,128)(2,1)S(1)}, u32[]{:S(2)}, u32[]{:S(2)}) %collective-permute-start.2) | collective-permute-done | bytes 1376288 | tf_op jit(solution)/shard_map/ppermute | solution.py:485
  80.3 13.4 %backward.1 = bf16[256,4608]{1,0:T(8,128)(2,1)} custom-call(bf16[1152,1152]{1,0:T(8,128)(2,1)} %get-tuple-element.24.pick_hbm, bf16[256,4608]{1,0:T(8,128)(2,1)} %bitcast.21, bf16[256,2688]{1,0:T(8,128)(2,1)} %bitcast.10.own_hbm, bf16[256,2688]{1,0:T(8,128)(2,1)S(1)} %collective-permute-done.2.other_ref, f32[256,256]{1,0:T(8,128)S(1)} %get-tuple-element.20.bias_ref, ...), custom_call_target="tpu_custom_call" | custom-call | flops 5939134464 | tf_op jit(solution)/shard_map/backward/pallas_call | solution.py:375
  93.8 0.2 total.1
  94.0 3.8 %collective-permute-start.3 = (bf16[8,2688]{1,0:T(8,128)(2,1)S(1)}, bf16[8,2688]{1,0:T(8,128)(2,1)S(1)}, u32[]{:S(2)}, u32[]{:S(2)}) collective-permute-start(bf16[8,2688]{1,0:T(8,128)(2,1)S(1)} %total.1), channel_id=1, source_target_pairs={{64,0},{96,32},{0,64},{32,96},{192,128},{224,160},{128,192},{160,2... | collective-permute-start | bytes 129032 | tf_op jit(solution)/shard_map/ppermute | solution.py:459
  97.8 7.8 %all-to-all-start.3 = ((bf16[32,8,4608]{2,1,0:T(8,128)(2,1)}), bf16[32,8,4608]{2,1,0:T(8,128)(2,1)S(1)}, u32[]{:S(2)}, u32[]{:S(2)}) async-start(bf16[32,8,4608]{2,1,0:T(8,128)(2,1)} %bitcast.25), calls=%async_computation.3 | async-start | bytes 4718592 | tf_op jit(solution)/shard_map/all_to_all | solution.py:482
  105.6 0.0 collective-permute-done.3
  105.7 8.8 %collective-permute-start.4 = (bf16[8,2688]{1,0:T(8,128)(2,1)S(1)}, bf16[8,2688]{1,0:T(8,128)(2,1)S(1)}, u32[]{:S(2)}, u32[]{:S(2)}) collective-permute-start(bf16[8,2688]{1,0:T(8,128)(2,1)S(1)} %add_convert_fusion.2), channel_id=1, source_target_pairs={{128,0},{416,32},{192,64},{480,96},{0,128},{288,160},{64,192},{352... | collective-permute-start | bytes 129032 | tf_op jit(solution)/shard_map/ppermute | solution.py:459
  114.5 2.9 %collective-permute-done.4 = bf16[8,2688]{1,0:T(8,128)(2,1)S(1)} collective-permute-done((bf16[8,2688]{1,0:T(8,128)(2,1)S(1)}, bf16[8,2688]{1,0:T(8,128)(2,1)S(1)}, u32[]{:S(2)}, u32[]{:S(2)}) %collective-permute-start.4) | collective-permute-done | bytes 43040 | tf_op jit(solution)/shard_map/ppermute | solution.py:459
  117.4 5.8 %collective-permute-start.5 = (bf16[8,2688]{1,0:T(8,128)(2,1)S(1)}, bf16[8,2688]{1,0:T(8,128)(2,1)S(1)}, u32[]{:S(2)}, u32[]{:S(2)}) collective-permute-start(bf16[8,2688]{1,0:T(8,128)(2,1)S(1)} %add_convert_fusion.1), channel_id=1, source_target_pairs={{448,0},{224,32},{384,64},{160,96},{320,128},{96,160},{256,192},{3... | collective-permute-start | bytes 129032 | tf_op jit(solution)/shard_map/ppermute | solution.py:459
  123.2 1.7 %collective-permute-done.5 = bf16[8,2688]{1,0:T(8,128)(2,1)S(1)} collective-permute-done((bf16[8,2688]{1,0:T(8,128)(2,1)S(1)}, bf16[8,2688]{1,0:T(8,128)(2,1)S(1)}, u32[]{:S(2)}, u32[]{:S(2)}) %collective-permute-start.5) | collective-permute-done | bytes 43040 | tf_op jit(solution)/shard_map/ppermute | solution.py:459
  124.9 6.3 %collective-permute-start.6 = (bf16[8,2688]{1,0:T(8,128)(2,1)S(1)}, bf16[8,2688]{1,0:T(8,128)(2,1)S(1)}, u32[]{:S(2)}, u32[]{:S(2)}) collective-permute-start(bf16[8,2688]{1,0:T(8,128)(2,1)S(1)} %add_convert_fusion.mine_ref), channel_id=1, source_target_pairs={{32,0},{0,32},{96,64},{64,96},{160,128},{128,160},{224,192},{192,2... | collective-permute-start | bytes 129032 | tf_op jit(solution)/shard_map/ppermute | solution.py:459
  131.2 1.7 %collective-permute-done.6.other_ref = bf16[8,2688]{1,0:T(8,128)(2,1)S(1)} collective-permute-done((bf16[8,2688]{1,0:T(8,128)(2,1)S(1)}, bf16[8,2688]{1,0:T(8,128)(2,1)S(1)}, u32[]{:S(2)}, u32[]{:S(2)}) %collective-permute-start.6) | collective-permute-done | bytes 43040 | tf_op jit(solution)/shard_map/ppermute | solution.py:459
  132.9 0.7 finish.1
  133.6 3.2 %all-to-all-done.3 = bf16[32,8,4608]{2,1,0:T(8,128)(2,1)S(1)} async-done(((bf16[32,8,4608]{2,1,0:T(8,128)(2,1)}), bf16[32,8,4608]{2,1,0:T(8,128)(2,1)S(1)}, u32[]{:S(2)}, u32[]{:S(2)}) %all-to-all-start.3) | async-done | bytes 2359328 | tf_op jit(solution)/shard_map/all_to_all | solution.py:482
  136.8 1.4 %unpack.1 = (bf16[256,1152]{1,0:T(8,128)(2,1)}, bf16[256,1152]{1,0:T(8,128)(2,1)}, bf16[256,1152]{1,0:T(8,128)(2,1)}, bf16[256,1152]{1,0:T(8,128)(2,1)}) custom-call(bf16[256,4608]{1,0:T(8,128)(2,1)S(1)} %bitcast.19), custom_call_target="tpu_custom_call" | custom-call | bytes 4718592 | tf_op jit(solution)/shard_map/unpack/pallas_call | solution.py:375
  (8 shorter events, 0.1 us)
Async XLA Ops:
  3.3 10.8 %copy-start.1 = (bf16[1152,36]{0,1:T(8,128)(2,1)S(1)}, bf16[1152,36]{0,1:T(8,128)(2,1)}, u32[]{:S(2)}) copy-start(bf16[1152,36]{0,1:T(8,128)(2,1)} %param.10) | copy-start | bytes 248836
  3.3 41.9 %all-to-all-start = ((bf16[32,8,4608]{2,1,0:T(8,128)(2,1)}), bf16[32,8,4608]{2,1,0:T(8,128)(2,1)S(1)}, u32[]{:S(2)}, u32[]{:S(2)}) async-start(bf16[32,8,4608]{2,1,0:T(8,128)(2,1)} %bitcast.23), calls=%async_computation | async-start | bytes 4718592 | tf_op jit(solution)/shard_map/all_to_all | solution.py:482
  14.0 1.9 %copy-start.2 = (s32[1,4]{1,0:T(1,128)S(1)}, s32[1,4]{1,0:T(1,128)}, u32[]{:S(2)}) copy-start(s32[1,4]{1,0:T(1,128)} %lens_ref.1) | copy-start | bytes 52
  45.2 5.2 %copy-start = (bf16[32,8,4608]{2,1,0:T(8,128)(2,1)}, bf16[32,8,4608]{2,1,0:T(8,128)(2,1)S(1)}, u32[]{:S(2)}) copy-start(bf16[32,8,4608]{2,1,0:T(8,128)(2,1)S(1)} %all-to-all-done) | copy-start | bytes 7077892
  45.2 25.9 %all-to-all-start.2 = ((bf16[32,8,2688]{2,1,0:T(8,128)(2,1)}), bf16[32,8,2688]{2,1,0:T(8,128)(2,1)}, u32[]{:S(2)}, u32[]{:S(2)}) async-start(bf16[32,8,2688]{2,1,0:T(8,128)(2,1)} %bitcast.24), calls=%async_computation.2 | async-start | bytes 2752512 | tf_op jit(solution)/shard_map/all_to_all | solution.py:482
  55.0 4.3 %collective-permute-start = (bf16[8,8,5248]{2,1,0:T(8,128)(2,1)}, bf16[8,8,5248]{2,1,0:T(8,128)(2,1)S(1)}, u32[]{:S(2)}, u32[]{:S(2)}) collective-permute-start(bf16[8,8,5248]{2,1,0:T(8,128)(2,1)} %get-tuple-element.22), channel_id=1, source_target_pairs={{0,1},{1,0},{2,3},{3,2},{4,5},{5,4},{6,7},{7,6},{8,9},{9,8},{10,11... | collective-permute-start | bytes 2015240 | tf_op jit(solution)/shard_map/ppermute | solution.py:485
  57.4 4.2 %collective-permute-start.1 = (bf16[8,8,5248]{2,1,0:T(8,128)(2,1)}, bf16[8,8,5248]{2,1,0:T(8,128)(2,1)S(1)}, u32[]{:S(2)}, u32[]{:S(2)}) collective-permute-start(bf16[8,8,5248]{2,1,0:T(8,128)(2,1)} %get-tuple-element.23), channel_id=1, source_target_pairs={{0,1},{1,0},{2,3},{3,2},{4,5},{5,4},{6,7},{7,6},{8,9},{9,8},{10,11... | collective-permute-start | bytes 2015240 | tf_op jit(solution)/shard_map/ppermute | solution.py:485
  71.1 22.7 %all-to-all-start.1 = ((bf16[32,8,2688]{2,1,0:T(8,128)(2,1)}), bf16[32,8,2688]{2,1,0:T(8,128)(2,1)S(1)}, u32[]{:S(2)}, u32[]{:S(2)}) async-start(bf16[32,8,2688]{2,1,0:T(8,128)(2,1)} %bitcast.8), calls=%async_computation.1 | async-start | bytes 2752512 | tf_op jit(solution)/shard_map/all_to_all | solution.py:499
  75.0 5.3 %collective-permute-start.2 = (bf16[256,2688]{1,0:T(8,128)(2,1)}, bf16[256,2688]{1,0:T(8,128)(2,1)S(1)}, u32[]{:S(2)}, u32[]{:S(2)}) collective-permute-start(bf16[256,2688]{1,0:T(8,128)(2,1)} %bitcast.10.own_hbm), channel_id=1, source_target_pairs={{0,1},{1,0},{2,3},{3,2},{4,5},{5,4},{6,7},{7,6},{8,9},{9,8},{10,11... | collective-permute-start | bytes 4128776 | tf_op jit(solution)/shard_map/ppermute | solution.py:485
  94.0 11.7 %collective-permute-start.3 = (bf16[8,2688]{1,0:T(8,128)(2,1)S(1)}, bf16[8,2688]{1,0:T(8,128)(2,1)S(1)}, u32[]{:S(2)}, u32[]{:S(2)}) collective-permute-start(bf16[8,2688]{1,0:T(8,128)(2,1)S(1)} %total.1), channel_id=1, source_target_pairs={{64,0},{96,32},{0,64},{32,96},{192,128},{224,160},{128,192},{160,2... | collective-permute-start | bytes 129032 | tf_op jit(solution)/shard_map/ppermute | solution.py:459
  97.8 38.9 %all-to-all-start.3 = ((bf16[32,8,4608]{2,1,0:T(8,128)(2,1)}), bf16[32,8,4608]{2,1,0:T(8,128)(2,1)S(1)}, u32[]{:S(2)}, u32[]{:S(2)}) async-start(bf16[32,8,4608]{2,1,0:T(8,128)(2,1)} %bitcast.25), calls=%async_computation.3 | async-start | bytes 4718592 | tf_op jit(solution)/shard_map/all_to_all | solution.py:482
  105.7 11.7 %collective-permute-start.4 = (bf16[8,2688]{1,0:T(8,128)(2,1)S(1)}, bf16[8,2688]{1,0:T(8,128)(2,1)S(1)}, u32[]{:S(2)}, u32[]{:S(2)}) collective-permute-start(bf16[8,2688]{1,0:T(8,128)(2,1)S(1)} %add_convert_fusion.2), channel_id=1, source_target_pairs={{128,0},{416,32},{192,64},{480,96},{0,128},{288,160},{64,192},{352... | collective-permute-start | bytes 129032 | tf_op jit(solution)/shard_map/ppermute | solution.py:459
  117.4 7.5 %collective-permute-start.5 = (bf16[8,2688]{1,0:T(8,128)(2,1)S(1)}, bf16[8,2688]{1,0:T(8,128)(2,1)S(1)}, u32[]{:S(2)}, u32[]{:S(2)}) collective-permute-start(bf16[8,2688]{1,0:T(8,128)(2,1)S(1)} %add_convert_fusion.1), channel_id=1, source_target_pairs={{448,0},{224,32},{384,64},{160,96},{320,128},{96,160},{256,192},{3... | collective-permute-start | bytes 129032 | tf_op jit(solution)/shard_map/ppermute | solution.py:459
  124.9 8.0 %collective-permute-start.6 = (bf16[8,2688]{1,0:T(8,128)(2,1)S(1)}, bf16[8,2688]{1,0:T(8,128)(2,1)S(1)}, u32[]{:S(2)}, u32[]{:S(2)}) collective-permute-start(bf16[8,2688]{1,0:T(8,128)(2,1)S(1)} %add_convert_fusion.mine_ref), channel_id=1, source_target_pairs={{32,0},{0,32},{96,64},{64,96},{160,128},{128,160},{224,192},{192,2... | collective-permute-start | bytes 129032 | tf_op jit(solution)/shard_map/ppermute | solution.py:459

commit v10 on v9

--- a/solution.py
+++ b/solution.py
@@ -271,9 +271,21 @@
     out_ref[pl.ds(32, 4), pl.ds(size, width - size)] = turned[4:, : width - size]
 
 
+def scores_kernel(x_ref, bias_ref, attention_ref):
+    rows = x_ref.shape[0]
+    width = x_ref.shape[1] // 4
+    bias = bias_ref[...]
+    for head in range(HEADS):
+        start, size = window(head)
+        query_win = jnp.where(head_lanes(head, rows), x_ref[:, pl.ds(start, size)], 0)
+        scores = dot_nt(x_ref[:, pl.ds(width + start, size)], query_win) * SCALE + bias
+        raised = jnp.exp(scores - jnp.max(scores, axis=0, keepdims=True))
+        attention_ref[head] = raised * (1.0 / jnp.sum(raised, axis=0, keepdims=True))
+
+
 def backward_kernel(
-    pick_hbm, x_hbm, own_hbm, other_ref, bias_ref, mixed_ref, y_ref,
-    pick_ref, x_ref, own_ref, odd_ref, back_ref, out_ref, held_ref, attention_ref, sems
+    pick_hbm, x_hbm, own_hbm, other_ref, attention_ref, mixed_ref, y_ref,
+    pick_ref, x_ref, own_ref, odd_ref, back_ref, out_ref, held_ref, sems
 ):
     rows, width = mixed_ref.shape
     pairs, third, fourth = pl.ds(0, 2 * width), pl.ds(2 * width, width), pl.ds(3 * width, width)
@@ -293,15 +305,8 @@
         copies.append(pltpu.make_async_copy(held_ref.at[:, lanes], y_ref.at[:, lanes], sems.at[len(copies)]))
         copies[-1].start()
 
+    blocks = FULL // GROUP
     fetches[0].wait()
-    bias = bias_ref[...]
-    for head in range(HEADS):
-        start, size = window(head)
-        query_win = jnp.where(head_lanes(head, rows), x_ref[:, pl.ds(start, size)], 0)
-        scores = dot_nt(x_ref[:, pl.ds(width + start, size)], query_win) * SCALE + bias
-        raised = jnp.exp(scores - jnp.max(scores, axis=0, keepdims=True))
-        attention_ref[head] = raised * (1.0 / jnp.sum(raised, axis=0, keepdims=True))
-    blocks = FULL // GROUP
     fetches[1].wait()
     weight = []
     for ref in (own_ref, other_ref):
@@ -433,14 +438,18 @@
     return call(join_kernel, "join", outs, (keep, first, second), flops=JOIN_FLOPS)[0]
 
 
-def backward(pick, x, own, other, bias, mixed):
+def scores(x, bias):
+    rows = x.shape[0]
+    return call(scores_kernel, "scores", [((HEADS, rows, rows), F32)], (x, bias))[0]
+
+
+def backward(pick, x, own, other, attention, mixed):
     rows, width = mixed.shape
     flops = 8 * width * rows * width + 12 * HEADS * rows * rows * 256
     one, wide = (rows, width), (rows, 4 * width)
     shapes = ((width, width), wide, own.shape, (width - 4 * rows, width), one, one, wide)
-    scratch = [pltpu.VMEM(shape, BF16) for shape in shapes]
-    scratch += [pltpu.VMEM((HEADS, rows, rows), F32), dma(12)]
-    args = (pick, x, own, other, bias, mixed)
+    scratch = [pltpu.VMEM(shape, BF16) for shape in shapes] + [dma(12)]
+    args = (pick, x, own, other, attention, mixed)
     return call(backward_kernel, "backward", [(wide, BF16)], args, hbm_in=3, hbm_out=(0,), scratch=scratch, flops=flops)[0]
 
 
@@ -498,7 +507,7 @@
     ]
     parts = lax.all_to_all(chip, ("dp", "seq"), 0, 0, tiled=True, axis_index_groups=pairs)
 
-    y = backward(pick, x, own, partner(own), bias, mixed)
+    y = backward(pick, x, own, partner(own), scores(x, bias), mixed)
     total, y = lax.optimization_barrier((total_of(parts), y))
     back = swap(y).reshape(patches, 4 * width)
     place = jnp.bitwise_and(lax.axis_index("dp"), 1).astype(jnp.int32).reshape(1)

time: 139 us -> 140 us (level)
  the two profiles are of different devices: /device:TPU:1 before, /device:TPU:6 now
where the time goes in v10:
time: 140 us; the launch traced here: 137 us
  starting transfers between devices  61.5 us (44%)
  waiting for transfers between devices  43.5 us (31%)
  Pallas kernels  29.9 us (21%)
    all_to_all x3, waiting for transfers between devices, swap(): lax.all_to_all(block.reshape(n_seq, positions, -1), 'seq', 0, 0, tiled=True)  30.9 us
    pallas_call x10, Pallas kernels, call(): pl.pallas_call(kernel, out_shape=[pltpu.HBM(s.shape, s.dtype) if i in hbm...  29.9 us
    ppermute x4, starting transfers between devices, exchange(): lax.ppermute(block, 'dp', [(source(i) % n_dp, i) for i in range(n_dp)])  25.2 us
    all_to_all x3, starting transfers between devices, swap(): lax.all_to_all(block.reshape(n_seq, positions, -1), 'seq', 0, 0, tiled=True)  23.2 us
    ppermute x4, waiting for transfers between devices, exchange(): lax.ppermute(block, 'dp', [(source(i) % n_dp, i) for i in range(n_dp)])  7.46 us
    all_to_all x1, starting transfers between devices, on_device(): lax.all_to_all(chip, ('dp', 'seq'), 0, 0, tiled=True, axis_index_groups=p...  6.58 us
    ppermute x3, starting transfers between devices, partner(): return lax.ppermute(block, 'seq', [(i, i ^ 1) for i in range(n_seq)])  6.43 us
    ppermute x3, waiting for transfers between devices, partner(): return lax.ppermute(block, 'seq', [(i, i ^ 1) for i in range(n_seq)])  3.34 us
  transfers between devices with their start and end apart: 11, of which 8 were waited for; matrix products, arithmetic and copies ran while one was open for 0% of the time, Pallas kernels for 18%

profile of v10, /device:TPU:6, one launch (start us, length us, event | category | flops | bytes accessed | tf_op | source)
XLA Modules:
  0.0 137.1 jit_solution(12080401169807497614)
XLA Ops:
  0.6 2.6 %pack.1 = bf16[256,4608]{1,0:T(8,128)(2,1)} custom-call(bf16[256,1152]{1,0:T(8,128)(2,1)} %bitcast.28, bf16[256,1152]{1,0:T(8,128)(2,1)} %bitcast.29, bf16[256,1152]{1,0:T(8,128)(2,1)} %bitcast.30, bf16[256,1152]{1,0:T(8,128)(2,1)} %bitcast.31), custom_call_target="tpu_custom_call" | custom-call | bytes 4718592 | tf_op jit(solution)/shard_map/pack/pallas_call | solution.py:380
  3.2 0.0 copy-start.2
  3.2 0.0 copy-start.3
  3.2 9.9 %all-to-all-start = ((bf16[32,8,4608]{2,1,0:T(8,128)(2,1)}), bf16[32,8,4608]{2,1,0:T(8,128)(2,1)S(1)}, u32[]{:S(2)}, u32[]{:S(2)}) async-start(bf16[32,8,4608]{2,1,0:T(8,128)(2,1)} %bitcast.25), calls=%async_computation | async-start | bytes 4718592 | tf_op jit(solution)/shard_map/all_to_all | solution.py:491
  13.1 1.8 %spread.1 = bf16[256,2688]{1,0:T(8,128)(2,1)} custom-call(bf16[36,1152]{1,0:T(8,128)(2,1)S(1)} %bitcast.24), custom_call_target="tpu_custom_call" | custom-call | bytes 1459200 | tf_op jit(solution)/shard_map/spread/pallas_call | solution.py:380
  15.0 2.6 %tables.1 = (bf16[1152,1152]{1,0:T(8,128)(2,1)}, f32[256,256]{1,0:T(8,128)S(1)}) custom-call(s32[1]{0:T(128)} %bitcast.core_ref, s32[1,4]{1,0:T(1,128)S(1)} %copy-done.3), custom_call_target="tpu_custom_call" | custom-call | bytes 2916372 | tf_op jit(solution)/shard_map/tables/pallas_call | solution.py:380
  17.6 24.6 %all-to-all-done = bf16[32,8,4608]{2,1,0:T(8,128)(2,1)S(1)} async-done(((bf16[32,8,4608]{2,1,0:T(8,128)(2,1)}), bf16[32,8,4608]{2,1,0:T(8,128)(2,1)S(1)}, u32[]{:S(2)}, u32[]{:S(2)}) %all-to-all-start) | async-done | bytes 2359328 | tf_op jit(solution)/shard_map/all_to_all | solution.py:491
  42.1 7.3 %all-to-all-start.2 = ((bf16[32,8,2688]{2,1,0:T(8,128)(2,1)}), bf16[32,8,2688]{2,1,0:T(8,128)(2,1)}, u32[]{:S(2)}, u32[]{:S(2)}) async-start(bf16[32,8,2688]{2,1,0:T(8,128)(2,1)} %bitcast.26), calls=%async_computation.2 | async-start | bytes 2752512 | tf_op jit(solution)/shard_map/all_to_all | solution.py:491
  49.5 4.7 %forward.1 = (bf16[256,1152]{1,0:T(8,128)(2,1)S(1)}, bf16[16,8,5248]{2,1,0:T(8,128)(2,1)S(1)}, bf16[8,8,5248]{2,1,0:T(8,128)(2,1)}, bf16[8,8,5248]{2,1,0:T(8,128)(2,1)}) custom-call(s32[1]{0:T(128)} %bitcast.core_ref, bf16[256,4608]{1,0:T(8,128)(2,1)S(1)} %bitcast.19, f32[256,256]{1,0:T(8,128)S(1)} %get-tuple-element.20.bias_ref), custom_call_target="tpu_custom_call" | custom-call | flops 99999997952 | tf_op jit(solution)/shard_map/forward/pallas_call | solution.py:380
  54.2 2.0 %collective-permute-start = (bf16[8,8,5248]{2,1,0:T(8,128)(2,1)}, bf16[8,8,5248]{2,1,0:T(8,128)(2,1)S(1)}, u32[]{:S(2)}, u32[]{:S(2)}) collective-permute-start(bf16[8,8,5248]{2,1,0:T(8,128)(2,1)} %get-tuple-element.22), channel_id=1, source_target_pairs={{0,1},{1,0},{2,3},{3,2},{4,5},{5,4},{6,7},{7,6},{8,9},{9,8},{10,11... | collective-permute-start | bytes 2015240 | tf_op jit(solution)/shard_map/ppermute | solution.py:494
  56.2 2.3 %collective-permute-start.1 = (bf16[8,8,5248]{2,1,0:T(8,128)(2,1)}, bf16[8,8,5248]{2,1,0:T(8,128)(2,1)S(1)}, u32[]{:S(2)}, u32[]{:S(2)}) collective-permute-start(bf16[8,8,5248]{2,1,0:T(8,128)(2,1)} %get-tuple-element.23), channel_id=1, source_target_pairs={{0,1},{1,0},{2,3},{3,2},{4,5},{5,4},{6,7},{7,6},{8,9},{9,8},{10,11... | collective-permute-start | bytes 2015240 | tf_op jit(solution)/shard_map/ppermute | solution.py:494
  58.5 1.9 %collective-permute-done.1.second_ref = bf16[8,8,5248]{2,1,0:T(8,128)(2,1)S(1)} collective-permute-done((bf16[8,8,5248]{2,1,0:T(8,128)(2,1)}, bf16[8,8,5248]{2,1,0:T(8,128)(2,1)S(1)}, u32[]{:S(2)}, u32[]{:S(2)}) %collective-permute-start.1) | collective-permute-done | bytes 671776 | tf_op jit(solution)/shard_map/ppermute | solution.py:494
  60.5 0.3 join.1
  60.8 1.1 copy-done.1
  61.9 6.3 %all-to-all-done.2 = bf16[32,8,2688]{2,1,0:T(8,128)(2,1)} async-done(((bf16[32,8,2688]{2,1,0:T(8,128)(2,1)}), bf16[32,8,2688]{2,1,0:T(8,128)(2,1)}, u32[]{:S(2)}, u32[]{:S(2)}) %all-to-all-start.2) | async-done | bytes 1376288 | tf_op jit(solution)/shard_map/all_to_all | solution.py:491
  68.2 6.6 %all-to-all-start.1 = ((bf16[32,8,2688]{2,1,0:T(8,128)(2,1)}), bf16[32,8,2688]{2,1,0:T(8,128)(2,1)}, u32[]{:S(2)}, u32[]{:S(2)}) async-start(bf16[32,8,2688]{2,1,0:T(8,128)(2,1)} %bitcast.23), calls=%async_computation.1 | async-start | bytes 2752512 | tf_op jit(solution)/shard_map/all_to_all | solution.py:508
  74.8 2.1 %collective-permute-start.2 = (bf16[256,2688]{1,0:T(8,128)(2,1)}, bf16[256,2688]{1,0:T(8,128)(2,1)S(1)}, u32[]{:S(2)}, u32[]{:S(2)}) collective-permute-start(bf16[256,2688]{1,0:T(8,128)(2,1)} %bitcast.10.own_hbm), channel_id=1, source_target_pairs={{0,1},{1,0},{2,3},{3,2},{4,5},{5,4},{6,7},{7,6},{8,9},{9,8},{10,11... | collective-permute-start | bytes 4128776 | tf_op jit(solution)/shard_map/ppermute | solution.py:494
  76.9 1.7 %scores.1.attention_ref = f32[16,256,256]{2,1,0:T(8,128)S(1)} custom-call(bf16[256,4608]{1,0:T(8,128)(2,1)S(1)} %bitcast.20, f32[256,256]{1,0:T(8,128)S(1)} %get-tuple-element.20.bias_ref), custom_call_target="tpu_custom_call" | custom-call | bytes 6815744 | tf_op jit(solution)/shard_map/scores/pallas_call | solution.py:380
  78.6 1.4 %collective-permute-done.2.other_ref = bf16[256,2688]{1,0:T(8,128)(2,1)S(1)} collective-permute-done((bf16[256,2688]{1,0:T(8,128)(2,1)}, bf16[256,2688]{1,0:T(8,128)(2,1)S(1)}, u32[]{:S(2)}, u32[]{:S(2)}) %collective-permute-start.2) | collective-permute-done | bytes 1376288 | tf_op jit(solution)/shard_map/ppermute | solution.py:494
  80.0 12.5 %backward.1 = bf16[256,4608]{1,0:T(8,128)(2,1)} custom-call(bf16[1152,1152]{1,0:T(8,128)(2,1)} %get-tuple-element.24.pick_hbm, bf16[256,4608]{1,0:T(8,128)(2,1)} %bitcast.21, bf16[256,2688]{1,0:T(8,128)(2,1)} %bitcast.10.own_hbm, bf16[256,2688]{1,0:T(8,128)(2,1)S(1)} %collective-permute-done.2.other_ref, f32[16,256,256]{2,1,0:T(8,128)S(1)} %scores.1.attention_ref, ...), custom_call_target="tpu_custom_call" | custom-call | flops 5939134464 | tf_op jit(solution)/shard_map/backward/pallas_call | solution.py:380
  92.6 1.8 %all-to-all-done.1.parts_ref = bf16[32,8,2688]{2,1,0:T(8,128)(2,1)} async-done(((bf16[32,8,2688]{2,1,0:T(8,128)(2,1)}), bf16[32,8,2688]{2,1,0:T(8,128)(2,1)}, u32[]{:S(2)}, u32[]{:S(2)}) %all-to-all-start.1) | async-done | bytes 1376288 | tf_op jit(solution)/shard_map/all_to_all | solution.py:508
  94.4 1.5 %total.1 = bf16[8,2688]{1,0:T(8,128)(2,1)S(1)} custom-call(bf16[32,8,2688]{2,1,0:T(8,128)(2,1)} %all-to-all-done.1.parts_ref), custom_call_target="tpu_custom_call" | custom-call | bytes 1419264 | tf_op jit(solution)/shard_map/total/pallas_call | solution.py:380
  96.0 3.1 %collective-permute-start.3 = (bf16[8,2688]{1,0:T(8,128)(2,1)S(1)}, bf16[8,2688]{1,0:T(8,128)(2,1)S(1)}, u32[]{:S(2)}, u32[]{:S(2)}) collective-permute-start(bf16[8,2688]{1,0:T(8,128)(2,1)S(1)} %total.1), channel_id=1, source_target_pairs={{64,0},{96,32},{0,64},{32,96},{192,128},{224,160},{128,192},{160,2... | collective-permute-start | bytes 129032 | tf_op jit(solution)/shard_map/ppermute | solution.py:468
  99.1 6.0 %all-to-all-start.3 = ((bf16[32,8,4608]{2,1,0:T(8,128)(2,1)}), bf16[32,8,4608]{2,1,0:T(8,128)(2,1)S(1)}, u32[]{:S(2)}, u32[]{:S(2)}) async-start(bf16[32,8,4608]{2,1,0:T(8,128)(2,1)} %bitcast.27), calls=%async_computation.3 | async-start | bytes 4718592 | tf_op jit(solution)/shard_map/all_to_all | solution.py:491
  105.1 9.1 %collective-permute-start.4 = (bf16[8,2688]{1,0:T(8,128)(2,1)S(1)}, bf16[8,2688]{1,0:T(8,128)(2,1)S(1)}, u32[]{:S(2)}, u32[]{:S(2)}) collective-permute-start(bf16[8,2688]{1,0:T(8,128)(2,1)S(1)} %add_convert_fusion.2), channel_id=1, source_target_pairs={{128,0},{416,32},{192,64},{480,96},{0,128},{288,160},{64,192},{352... | collective-permute-start | bytes 129032 | tf_op jit(solution)/shard_map/ppermute | solution.py:468
  114.2 3.0 %collective-permute-done.4 = bf16[8,2688]{1,0:T(8,128)(2,1)S(1)} collective-permute-done((bf16[8,2688]{1,0:T(8,128)(2,1)S(1)}, bf16[8,2688]{1,0:T(8,128)(2,1)S(1)}, u32[]{:S(2)}, u32[]{:S(2)}) %collective-permute-start.4) | collective-permute-done | bytes 43040 | tf_op jit(solution)/shard_map/ppermute | solution.py:468
  117.3 8.2 %collective-permute-start.5 = (bf16[8,2688]{1,0:T(8,128)(2,1)S(1)}, bf16[8,2688]{1,0:T(8,128)(2,1)S(1)}, u32[]{:S(2)}, u32[]{:S(2)}) collective-permute-start(bf16[8,2688]{1,0:T(8,128)(2,1)S(1)} %add_convert_fusion.1), channel_id=1, source_target_pairs={{448,0},{224,32},{384,64},{160,96},{320,128},{96,160},{256,192},{3... | collective-permute-start | bytes 129032 | tf_op jit(solution)/shard_map/ppermute | solution.py:468
  125.5 2.4 %collective-permute-done.5 = bf16[8,2688]{1,0:T(8,128)(2,1)S(1)} collective-permute-done((bf16[8,2688]{1,0:T(8,128)(2,1)S(1)}, bf16[8,2688]{1,0:T(8,128)(2,1)S(1)}, u32[]{:S(2)}, u32[]{:S(2)}) %collective-permute-start.5) | collective-permute-done | bytes 43040 | tf_op jit(solution)/shard_map/ppermute | solution.py:468
  127.9 4.8 %collective-permute-start.6 = (bf16[8,2688]{1,0:T(8,128)(2,1)S(1)}, bf16[8,2688]{1,0:T(8,128)(2,1)S(1)}, u32[]{:S(2)}, u32[]{:S(2)}) collective-permute-start(bf16[8,2688]{1,0:T(8,128)(2,1)S(1)} %add_convert_fusion.mine_ref), channel_id=1, source_target_pairs={{32,0},{0,32},{96,64},{64,96},{160,128},{128,160},{224,192},{192,2... | collective-permute-start | bytes 129032 | tf_op jit(solution)/shard_map/ppermute | solution.py:468
  132.8 2.0 %collective-permute-done.6.other_ref = bf16[8,2688]{1,0:T(8,128)(2,1)S(1)} collective-permute-done((bf16[8,2688]{1,0:T(8,128)(2,1)S(1)}, bf16[8,2688]{1,0:T(8,128)(2,1)S(1)}, u32[]{:S(2)}, u32[]{:S(2)}) %collective-permute-start.6) | collective-permute-done | bytes 43040 | tf_op jit(solution)/shard_map/ppermute | solution.py:468
  134.8 0.7 finish.1
  135.5 1.4 %unpack.1 = (bf16[256,1152]{1,0:T(8,128)(2,1)}, bf16[256,1152]{1,0:T(8,128)(2,1)}, bf16[256,1152]{1,0:T(8,128)(2,1)}, bf16[256,1152]{1,0:T(8,128)(2,1)}) custom-call(bf16[256,4608]{1,0:T(8,128)(2,1)S(1)} %bitcast.22), custom_call_target="tpu_custom_call" | custom-call | bytes 4718592 | tf_op jit(solution)/shard_map/unpack/pallas_call | solution.py:380
  (11 shorter events, 0.1 us)
Async XLA Ops:
  3.2 9.9 %copy-start.2 = (bf16[1152,36]{0,1:T(8,128)(2,1)S(1)}, bf16[1152,36]{0,1:T(8,128)(2,1)}, u32[]{:S(2)}) copy-start(bf16[1152,36]{0,1:T(8,128)(2,1)} %param.10) | copy-start | bytes 248836
  3.2 11.7 %copy-start.3 = (s32[1,4]{1,0:T(1,128)S(1)}, s32[1,4]{1,0:T(1,128)}, u32[]{:S(2)}) copy-start(s32[1,4]{1,0:T(1,128)} %lens_ref.1) | copy-start | bytes 52
  3.2 38.9 %all-to-all-start = ((bf16[32,8,4608]{2,1,0:T(8,128)(2,1)}), bf16[32,8,4608]{2,1,0:T(8,128)(2,1)S(1)}, u32[]{:S(2)}, u32[]{:S(2)}) async-start(bf16[32,8,4608]{2,1,0:T(8,128)(2,1)} %bitcast.25), calls=%async_computation | async-start | bytes 4718592 | tf_op jit(solution)/shard_map/all_to_all | solution.py:491
  42.1 34.8 %copy-start = (bf16[32,8,4608]{2,1,0:T(8,128)(2,1)}, bf16[32,8,4608]{2,1,0:T(8,128)(2,1)S(1)}, u32[]{:S(2)}) copy-start(bf16[32,8,4608]{2,1,0:T(8,128)(2,1)S(1)} %all-to-all-done) | copy-start | bytes 7077892
  42.1 26.1 %all-to-all-start.2 = ((bf16[32,8,2688]{2,1,0:T(8,128)(2,1)}), bf16[32,8,2688]{2,1,0:T(8,128)(2,1)}, u32[]{:S(2)}, u32[]{:S(2)}) async-start(bf16[32,8,2688]{2,1,0:T(8,128)(2,1)} %bitcast.26), calls=%async_computation.2 | async-start | bytes 2752512 | tf_op jit(solution)/shard_map/all_to_all | solution.py:491
  54.2 4.3 %collective-permute-start = (bf16[8,8,5248]{2,1,0:T(8,128)(2,1)}, bf16[8,8,5248]{2,1,0:T(8,128)(2,1)S(1)}, u32[]{:S(2)}, u32[]{:S(2)}) collective-permute-start(bf16[8,8,5248]{2,1,0:T(8,128)(2,1)} %get-tuple-element.22), channel_id=1, source_target_pairs={{0,1},{1,0},{2,3},{3,2},{4,5},{5,4},{6,7},{7,6},{8,9},{9,8},{10,11... | collective-permute-start | bytes 2015240 | tf_op jit(solution)/shard_map/ppermute | solution.py:494
  56.2 4.3 %collective-permute-start.1 = (bf16[8,8,5248]{2,1,0:T(8,128)(2,1)}, bf16[8,8,5248]{2,1,0:T(8,128)(2,1)S(1)}, u32[]{:S(2)}, u32[]{:S(2)}) collective-permute-start(bf16[8,8,5248]{2,1,0:T(8,128)(2,1)} %get-tuple-element.23), channel_id=1, source_target_pairs={{0,1},{1,0},{2,3},{3,2},{4,5},{5,4},{6,7},{7,6},{8,9},{9,8},{10,11... | collective-permute-start | bytes 2015240 | tf_op jit(solution)/shard_map/ppermute | solution.py:494
  60.8 1.1 copy-start.1
  68.2 26.2 %all-to-all-start.1 = ((bf16[32,8,2688]{2,1,0:T(8,128)(2,1)}), bf16[32,8,2688]{2,1,0:T(8,128)(2,1)}, u32[]{:S(2)}, u32[]{:S(2)}) async-start(bf16[32,8,2688]{2,1,0:T(8,128)(2,1)} %bitcast.23), calls=%async_computation.1 | async-start | bytes 2752512 | tf_op jit(solution)/shard_map/all_to_all | solution.py:508
  74.8 5.2 %collective-permute-start.2 = (bf16[256,2688]{1,0:T(8,128)(2,1)}, bf16[256,2688]{1,0:T(8,128)(2,1)S(1)}, u32[]{:S(2)}, u32[]{:S(2)}) collective-permute-start(bf16[256,2688]{1,0:T(8,128)(2,1)} %bitcast.10.own_hbm), channel_id=1, source_target_pairs={{0,1},{1,0},{2,3},{3,2},{4,5},{5,4},{6,7},{7,6},{8,9},{9,8},{10,11... | collective-permute-start | bytes 4128776 | tf_op jit(solution)/shard_map/ppermute | solution.py:494
  96.0 9.2 %collective-permute-start.3 = (bf16[8,2688]{1,0:T(8,128)(2,1)S(1)}, bf16[8,2688]{1,0:T(8,128)(2,1)S(1)}, u32[]{:S(2)}, u32[]{:S(2)}) collective-permute-start(bf16[8,2688]{1,0:T(8,128)(2,1)S(1)} %total.1), channel_id=1, source_target_pairs={{64,0},{96,32},{0,64},{32,96},{192,128},{224,160},{128,192},{160,2... | collective-permute-start | bytes 129032 | tf_op jit(solution)/shard_map/ppermute | solution.py:468
  99.1 36.4 %all-to-all-start.3 = ((bf16[32,8,4608]{2,1,0:T(8,128)(2,1)}), bf16[32,8,4608]{2,1,0:T(8,128)(2,1)S(1)}, u32[]{:S(2)}, u32[]{:S(2)}) async-start(bf16[32,8,4608]{2,1,0:T(8,128)(2,1)} %bitcast.27), calls=%async_computation.3 | async-start | bytes 4718592 | tf_op jit(solution)/shard_map/all_to_all | solution.py:491
  105.1 12.1 %collective-permute-start.4 = (bf16[8,2688]{1,0:T(8,128)(2,1)S(1)}, bf16[8,2688]{1,0:T(8,128)(2,1)S(1)}, u32[]{:S(2)}, u32[]{:S(2)}) collective-permute-start(bf16[8,2688]{1,0:T(8,128)(2,1)S(1)} %add_convert_fusion.2), channel_id=1, source_target_pairs={{128,0},{416,32},{192,64},{480,96},{0,128},{288,160},{64,192},{352... | collective-permute-start | bytes 129032 | tf_op jit(solution)/shard_map/ppermute | solution.py:468
  117.3 10.6 %collective-permute-start.5 = (bf16[8,2688]{1,0:T(8,128)(2,1)S(1)}, bf16[8,2688]{1,0:T(8,128)(2,1)S(1)}, u32[]{:S(2)}, u32[]{:S(2)}) collective-permute-start(bf16[8,2688]{1,0:T(8,128)(2,1)S(1)} %add_convert_fusion.1), channel_id=1, source_target_pairs={{448,0},{224,32},{384,64},{160,96},{320,128},{96,160},{256,192},{3... | collective-permute-start | bytes 129032 | tf_op jit(solution)/shard_map/ppermute | solution.py:468
  127.9 6.8 %collective-permute-start.6 = (bf16[8,2688]{1,0:T(8,128)(2,1)S(1)}, bf16[8,2688]{1,0:T(8,128)(2,1)S(1)}, u32[]{:S(2)}, u32[]{:S(2)}) collective-permute-start(bf16[8,2688]{1,0:T(8,128)(2,1)S(1)} %add_convert_fusion.mine_ref), channel_id=1, source_target_pairs={{32,0},{0,32},{96,64},{64,96},{160,128},{128,160},{224,192},{192,2... | collective-permute-start | bytes 129032 | tf_op jit(solution)/shard_map/ppermute | solution.py:468
